TPU v7x, 256 devices: a whole 4x4x8 slice. The times are simulated.
256 devices in a mesh: dp: 64 (over z, x, core), tensor: 4 (over y).
Axes of the slice: x: 4, y: 4, z: 8, core: 2. Of those that a mesh axis runs over, the one named last changes fastest.
Arguments:
- acts: bfloat16 [32768, 8192], P(('dp', 'tensor')), may hold values from -6 to 6
- key_grad: bfloat16 [32768, 1024], P('dp', 'tensor'), may hold values from -0.25 to 0.25
- w_key: bfloat16 [8192, 1024], P(None, 'tensor'), may hold values from -6 to 6
- error_fb: float32 [524288, 1024], P('dp', 'tensor'), may hold values from -6 to 6
- q_prev: float32 [1024, 64], P('tensor'), may hold values from -6 to 6
Outputs:
- act_grad: bfloat16 [32768, 8192], P(('dp', 'tensor'))
- update: bfloat16 [8192, 1024], P(None, 'tensor')
- q_new: float32 [1024, 64], P('tensor')
All inputs are finite; a program needn't handle non-finite values.
Results may differ from a plain program's by a relative error of at most 0.015.
Values may be sent and summed in bfloat16 or wider, within the bound.
No kernel may reach another device: no remote copies, remote signals or barrier semaphores. Data moves between devices by JAX's collectives and lax.ppermute only.
A program may use at most 128 MiB of HBM per device.

v0:
```python
import jax
import jax.numpy as jnp
from jax import lax
from jax.sharding import PartitionSpec as P


def local(acts, key_grad, w_key, error_fb, q_prev):
    grad_part = key_grad
    weight_grad = lax.dot_general(
        lax.all_gather(acts, "tensor", axis=0, tiled=True),
        grad_part,
        (((0,), (0,)), ((), ())),
        preferred_element_type=jnp.float32,
    )
    merged = weight_grad + error_fb
    p_local = jnp.einsum("dc,cr->rd", merged, q_prev, precision=lax.Precision.HIGHEST)
    grad_part = key_grad
    act_grad = lax.psum_scatter(
        lax.dot_general(
            grad_part, w_key, (((1,), (1,)), ((), ())), preferred_element_type=jnp.float32
        ).astype(jnp.bfloat16),
        "tensor",
        scatter_dimension=0,
        tiled=True,
    )
    p_total = lax.psum(p_local, ("dp", "tensor"))
    gram_mat = jnp.einsum("rd,sd->rs", p_total, p_total, precision=lax.Precision.HIGHEST)
    factor = jnp.linalg.cholesky(gram_mat)
    p_hat = lax.linalg.triangular_solve(factor, p_total, left_side=True, lower=True)
    q_part = jnp.einsum("dc,rd->cr", merged, p_hat, precision=lax.Precision.HIGHEST)
    q_new = lax.psum(q_part, "dp")
    update = jnp.einsum("rd,cr->dc", p_hat, q_new, precision=lax.Precision.HIGHEST)
    return (act_grad, update.astype(jnp.bfloat16), q_new)


def solution(mesh):
    placed = (
        P(("dp", "tensor"), None),
        P("dp", "tensor"),
        P(None, "tensor"),
        P("dp", "tensor"),
        P("tensor", None),
    )
    return jax.shard_map(
        local,
        mesh=mesh,
        in_specs=placed,
        out_specs=(P(("dp", "tensor"), None), P(None, "tensor"), P("tensor", None)),
        check_vma=False,
    )
```

profile of v0, /device:TPU:1, one launch (start us, length us, event | category | flops | bytes accessed | tf_op | source)
XLA Modules:
  0.0 667.8 jit_solution(12124320551584500389)
XLA Ops:
  7.2 0.0 copy-start
  7.2 0.0 all-gather.2.cloned.1.call-start
  7.2 0.7 all-gather.2.cloned.1.call-update
  7.9 0.0 copy-start.3
  7.9 0.0 all-reduce.3.cloned.1.call-start
  8.0 91.4 %all-gather.2.cloned.1.call-done = bf16[512,8192]{1,0:T(8,128)(2,1)} async-done(((bf16[128,8192]{1,0:T(8,128)(2,1)}), bf16[512,8192]{1,0:T(8,128)(2,1)}) %all-gather.2.cloned.1.call-update) | async-done | bytes 8388624 | tf_op jit(solution)/shard_map/all_gather | solution.py:10
  99.3 0.0 copy-done
  99.3 8.1 %convolution_add_fusion = f32[8192,256]{1,0:T(8,128)S(1)} fusion(f32[8192,256]{1,0:T(8,128)} %param.8, bf16[512,8192]{1,0:T(8,128)(2,1)} %all-gather.2.cloned.1.call-done, bf16[512,256]{1,0:T(8,128)(2,1)S(1)} %copy-done), kind=kOutput, calls=%fused_computation.2 | convolution fusion | flops 2149580800 | bytes 25427968 | tf_op jit(solution)/shard_map/dot_general | solution.py:9
  107.5 0.0 copy-start.1
  107.5 3.2 copy-done.1
  110.7 0.0 copy-done.3
  110.7 9.6 %convolution_bitcast_fusion = f32[64,8192]{1,0:T(8,128)} fusion(f32[8192,256]{1,0:T(8,128)S(1)} %convolution_add_fusion, f32[256,64]{0,1:T(8,128)S(1)} %copy-done.3), kind=kOutput, calls=%fused_computation.3 | convolution fusion | flops 1610612736 | bytes 10551296 | tf_op jit(solution)/shard_map/dc,cr->rd/dot_general | solution.py:16
  120.3 0.0 all-reduce.3.cloned.1.call-update
  120.3 0.2 all-reduce.5.cloned.1.call-start
  120.5 260.6 %all-reduce.3.cloned.1.call-done = f32[64,8192]{1,0:T(8,128)} async-done(((f32[64,8192]{1,0:T(8,128)}), f32[64,8192]{1,0:T(8,128)}) %all-reduce.3.cloned.1.call-update) | async-done | bytes 2097168 | tf_op jit(solution)/shard_map/psum | solution.py:26
  381.2 4.0 fusion.4
  385.2 0.1 copy.8
  385.3 5.8 cholesky.16
  391.2 0.6 compare_reduce_fusion
  391.8 0.7 fusion
  392.5 4.9 custom-call.6
  397.4 3.5 fusion.1
  400.9 8.0 %fusion.5 = f32[256,64]{0,1:T(8,128)} fusion(f32[8192,256]{1,0:T(8,128)} %copy-done.1, f32[64,8192]{1,0:T(8,128)S(1)} %fusion.1), kind=kOutput, calls=%fused_computation.15 | convolution fusion | flops 1610612736 | bytes 10551296 | tf_op jit(solution)/shard_map/dc,rd->cr/dot_general | solution.py:30
  408.8 0.0 all-reduce.5.cloned.1.call-update
  408.9 0.3 reduce-scatter.2.cloned.1.call-start
  409.1 7.8 %convolution_convert_fusion = bf16[512,8192]{1,0:T(8,128)(2,1)} fusion(bf16[512,256]{1,0:T(8,128)(2,1)S(1)} %copy-done, bf16[8192,256]{1,0:T(8,128)(2,1)} %param.7), kind=kOutput, calls=%fused_computation | convolution fusion | flops 2151677952 | bytes 12845056 | tf_op jit(solution)/shard_map/dot_general | solution.py:19
  416.9 0.0 reduce-scatter.2.cloned.1.call-update
  416.9 160.6 %all-reduce.5.cloned.1.call-done = f32[256,64]{0,1:T(8,128)} async-done(((f32[256,64]{0,1:T(8,128)}), f32[256,64]{0,1:T(8,128)}) %all-reduce.5.cloned.1.call-update) | async-done | bytes 65552 | tf_op jit(solution)/shard_map/psum | solution.py:31
  577.5 0.0 copy-start.2
  577.5 9.2 %convolution_convert_fusion.1 = bf16[8192,256]{1,0:T(8,128)(2,1)} fusion(f32[64,8192]{1,0:T(8,128)S(1)} %fusion.1, f32[256,64]{0,1:T(8,128)} %all-reduce.5.cloned.1.call-done), kind=kOutput, calls=%fused_computation.1 | convolution fusion | flops 1612709888 | bytes 6356992 | tf_op jit(solution)/shard_map/rd,cr->dc/dot_general | solution.py:32
  586.7 73.9 %reduce-scatter.2.cloned.1.call-done = bf16[128,8192]{1,0:T(8,128)(2,1)} async-done(((bf16[512,8192]{1,0:T(8,128)(2,1)}), bf16[128,8192]{1,0:T(8,128)(2,1)}) %reduce-scatter.2.cloned.1.call-update) | async-done | bytes 2097168 | tf_op jit(solution)/shard_map/reduce_scatter | solution.py:18
  660.6 0.0 copy-done.2
  660.6 0.6 copy.11
  (2 shorter events, 0.0 us)
Async XLA Ops:
  7.2 92.2 %copy-start = (bf16[512,256]{1,0:T(8,128)(2,1)S(1)}, bf16[512,256]{1,0:T(8,128)(2,1)}, u32[]{:S(2)}) copy-start(bf16[512,256]{1,0:T(8,128)(2,1)} %param.6) | copy-start | bytes 786436
  7.2 92.2 %all-gather.2.cloned.1.call-start = ((), (), s32[]{:S(2)}) async-start(), calls=%async_computation.2 | async-start | bytes 10485760 | tf_op jit(solution)/shard_map/all_gather | solution.py:10
  7.9 102.8 %copy-start.3 = (f32[256,64]{0,1:T(8,128)S(1)}, f32[256,64]{0,1:T(8,128)}, u32[]{:S(2)}) copy-start(f32[256,64]{0,1:T(8,128)} %param.9) | copy-start | bytes 196612
  7.9 373.2 %all-reduce.3.cloned.1.call-start = ((), (), s32[]{:S(2)}) async-start(), calls=%async_computation.3 | async-start | bytes 4194304 | tf_op jit(solution)/shard_map/psum | solution.py:26
  107.5 3.2 copy-start.1
  120.3 457.2 %all-reduce.5.cloned.1.call-start = ((), (), s32[]{:S(2)}) async-start(), calls=%async_computation.4 | async-start | bytes 131072 | tf_op jit(solution)/shard_map/psum | solution.py:31
  408.9 251.7 %reduce-scatter.2.cloned.1.call-start = ((), (), s32[]{:S(2)}) async-start(), calls=%async_computation.1 | async-start | bytes 10485760 | tf_op jit(solution)/shard_map/reduce_scatter | solution.py:18
  577.5 83.1 %copy-start.2 = (f32[256,64]{0,1:T(8,128)S(1)}, f32[256,64]{0,1:T(8,128)}, u32[]{:S(2)}) copy-start(f32[256,64]{0,1:T(8,128)} %all-reduce.5.cloned.1.call-done) | copy-start | bytes 196612
Sparse Core Ops, SparseCore 0:
  9.8 89.4 all-gather.1
  120.4 260.7 all-reduce.2
  409.0 168.4 all-reduce.4
  580.5 80.0 reduce-scatter.1
where the time goes:
time: 668 us
  waiting for transfers between devices  587 us (88%)
  matrix products  50.1 us (8%)
  between operations  13.8 us (2%)
  other arithmetic  12.1 us (2%)
    psum x1, waiting for transfers between devices, local(): p_total = lax.psum(p_local, ('dp', 'tensor'))  261 us
    psum x1, waiting for transfers between devices, local(): q_new = lax.psum(q_part, 'dp')  161 us
    all_gather x1, waiting for transfers between devices, local(): lax.all_gather(acts, 'tensor', axis=0, tiled=True)  91.4 us
    reduce_scatter x1, waiting for transfers between devices, local(): lax.psum_scatter(lax.dot_general(grad_part, w_key, (((1,), (1,)), ((), ()...  73.9 us
  transfers between devices with their start and end apart: 4, of which 4 were waited for; matrix products, arithmetic and copies ran while one was open for 3% of the time, Pallas kernels for 0%

commit v1 on v0

v1 whole, which is shorter than its diff:
```python
import jax
import jax.numpy as jnp
from jax import lax
from jax.sharding import Mesh, PartitionSpec as P

F32 = jnp.float32
BF = jnp.bfloat16
N_Z, N_X, N_C, N_Y = 8, 4, 2, 4


def dot(a, b, ca, cb):
    return lax.dot_general(a, b, (((ca,), (cb,)), ((), ())), preferred_element_type=F32)


def shift(v, axis, n, k):
    return lax.ppermute(v, axis, [(i, (i + k) % n) for i in range(n)])


def pick(v, i):
    return lax.dynamic_index_in_dim(v, i, 0, keepdims=False)


def y_scatter_sum(blocks, me):
    total = pick(blocks, me).astype(F32)
    for k in range(1, N_Y):
        sent = shift(pick(blocks, (me + k) % N_Y).astype(BF), "y", N_Y, k)
        total = total + sent.astype(F32)
    return total


def sum_all(p):
    me = lax.axis_index("c")
    half = p.reshape(2, 128, 16, 128)
    got = shift(pick(half, 1 - me).astype(BF), "c", 2, 1)
    own = (pick(half, me) + got.astype(F32)).astype(BF)
    got = lax.all_to_all(own, ("x", "y"), 0, 0, tiled=True)
    own = got.reshape(16, 8, 16, 128).astype(F32).sum(0).astype(BF)
    got = lax.all_to_all(jnp.broadcast_to(own[None], (8, 8, 16, 128)), "z", 0, 0, tiled=True)
    own = got.astype(F32).sum(0).astype(BF)
    got = lax.all_to_all(jnp.broadcast_to(own[None], (16, 8, 16, 128)), ("x", "y"), 0, 0, tiled=True)
    own = got.reshape(128, 16, 128)
    other = shift(own, "c", 2, 1)
    first = jnp.where(me == 0, own, other)
    second = jnp.where(me == 0, other, own)
    return jnp.concatenate([first, second], 0)


def sum_dp(q):
    b = q.astype(BF)
    b = (b.astype(F32) + shift(b, "c", 2, 1).astype(F32)).astype(BF)
    v = [b.astype(F32)] + [shift(b, "x", N_X, k).astype(F32) for k in range(1, N_X)]
    b = ((v[0] + v[2]) + (v[1] + v[3])).astype(BF)
    b = jnp.broadcast_to(b[None], (8, 64, 256))
    return lax.all_to_all(b, "z", 0, 0, tiled=True).astype(F32).sum(0)


def local(acts, key_grad, w_key, error_fb, q_prev):
    y = lax.axis_index("y")
    q_bf = q_prev.astype(BF)
    kgq = dot(q_bf, key_grad, 0, 1)
    kgq = y_scatter_sum(kgq.reshape(64, 4, 128).transpose(1, 0, 2), y)
    act_grad = lax.psum_scatter(
        dot(key_grad, w_key, 1, 1).astype(BF), "y", scatter_dimension=0, tiled=True
    )
    err = error_fb.astype(BF)
    p = dot(q_bf, err, 0, 1) + dot(kgq.astype(BF), acts, 1, 0)
    p = p.reshape(4, 16, 64, 128).transpose(2, 0, 1, 3).reshape(256, 16, 128)
    p = sum_all(p)
    p = p.reshape(64, 4, 16, 128).transpose(1, 2, 0, 3).reshape(64, 8192)
    ap = dot(p, acts, 1, 1).astype(BF)
    ap = [ap] + [shift(ap, "y", N_Y, k) for k in range(1, N_Y)]
    q_err = dot(p, err, 1, 0)
    kg = key_grad.reshape(4, 128, 256)
    q = q_err
    for k in range(N_Y):
        q = q + dot(ap[k], pick(kg, (y - k) % N_Y), 1, 0)
    gram = dot(p, p, 1, 1)
    factor = jnp.linalg.cholesky(gram)
    inv = lax.linalg.triangular_solve(factor, jnp.eye(64, dtype=F32), left_side=True, lower=True)
    q = sum_dp(q)
    q_new = jnp.dot(inv, q, precision=lax.Precision.HIGHEST)
    mix = lax.dot_general(inv, q_new, (((0,), (0,)), ((), ())), precision=lax.Precision.HIGHEST)
    update = dot(p, mix.astype(BF), 0, 0).astype(BF)
    return act_grad, update, q_new.T


def solution(mesh):
    fine = Mesh(mesh.devices.reshape(N_Z, N_X, N_C, N_Y), ("z", "x", "c", "y"))
    dp = ("z", "x", "c")
    rows = P(dp + ("y",), None)
    placed = (rows, P(dp, "y"), P(None, "y"), P(dp, "y"), P("y", None))
    return jax.shard_map(
        local,
        mesh=fine,
        in_specs=placed,
        out_specs=(rows, P(None, "y"), P("y", None)),
        check_vma=False,
    )
```

time: 668 us -> 146 us (0.22)
  waiting for transfers between devices: 587 us -> 9.04 us
  blocking collectives: 0 us -> 48.9 us
  matrix products: 50.1 us -> 28.2 us
  starting transfers between devices: 0.56 us -> 20.7 us
    psum x2 -> x0, waiting for transfers between devices: 421 us -> none  [the longest x1 261 us: local(): p_total = lax.psum(p_local, ('dp', 'tensor'))]
    all_gather x1 -> x0, waiting for transfers between devices: 91.4 us -> none  [local(): lax.all_gather(acts, 'tensor', axis=0, tiled=True)]
    reduce_scatter x1, waiting for transfers between devices: 73.9 us -> 0.01 us  [local(): lax.psum_scatter(dot(key_grad, w_key, 1, 1).astype(BF), 'y', scatter_dime...]
    all_to_all x0 -> x3, blocking collectives: none -> 48.9 us  [the longest x1 17.6 us: sum_all(): lax.all_to_all(jnp.broadcast_to(own[None], (8, 8, 16, 128)), 'z', 0, 0, t...]
    dot_general x6 -> x14, matrix products: 46.7 us -> 28 us  [the longest x12 27.5 us: dot(): lax.dot_general(a, b, (((ca,), (cb,)), ((), ())), preferred_element_type=...]
    ppermute x0 -> x12, starting transfers between devices: none -> 17.2 us  [shift(): return lax.ppermute(v, axis, [(i, (i + k) % n) for i in range(n)])]
  transfers between devices with their start and end apart: 4 -> 14, of which waited for: 4 -> 5; matrix products, arithmetic and copies ran while one was open for 3% -> 28% of each run, Pallas kernels for 0% -> 0%
where the time goes in v1:
time: 146 us; the launch traced here: 143 us
  blocking collectives  48.9 us (33%)
  matrix products  28.2 us (19%)
  starting transfers between devices  20.7 us (14%)
  other arithmetic  15.6 us (11%)
  between operations  14.3 us (10%)
  waiting for transfers between devices  9.04 us (6%)
  local copies, waits for them, and re-layouts  6.28 us (4%)
    dot_general x12, matrix products, dot(): lax.dot_general(a, b, (((ca,), (cb,)), ((), ())), preferred_element_type=...  27.5 us
    all_to_all x1, blocking collectives, sum_all(): lax.all_to_all(jnp.broadcast_to(own[None], (8, 8, 16, 128)), 'z', 0, 0, t...  17.6 us
    ppermute x12, starting transfers between devices, shift(): return lax.ppermute(v, axis, [(i, (i + k) % n) for i in range(n)])  17.2 us
    all_to_all x1, blocking collectives, sum_all(): got = lax.all_to_all(own, ('x', 'y'), 0, 0, tiled=True)  16 us
    all_to_all x1, blocking collectives, sum_all(): lax.all_to_all(jnp.broadcast_to(own[None], (16, 8, 16, 128)), ('x', 'y'),...  15.2 us
    another operation x3, other arithmetic, local(): factor = jnp.linalg.cholesky(gram)  6.51 us
    ppermute x12, waiting for transfers between devices, shift(): return lax.ppermute(v, axis, [(i, (i + k) % n) for i in range(n)])  5.85 us
    another operation x2, other arithmetic, local(): lax.linalg.triangular_solve(factor, jnp.eye(64, dtype=F32), left_side=Tru...  5.55 us
  transfers between devices with their start and end apart: 14, of which 5 were waited for; matrix products, arithmetic and copies ran while one was open for 28% of the time, Pallas kernels for 0%

profile of v1, /device:TPU:1, one launch (start us, length us, event | category | flops | bytes accessed | tf_op | source)
XLA Modules:
  0.0 143.0 jit_solution(17939899529244144905)
XLA Ops:
  7.2 0.0 copy-start
  7.2 0.0 reduce-scatter.2.cloned.1.call-start
  7.2 8.0 %convolution_convert_fusion = bf16[512,8192]{1,0:T(8,128)(2,1)} fusion(bf16[512,256]{1,0:T(8,128)(2,1)} %param.6, bf16[8192,256]{1,0:T(8,128)(2,1)} %param.7), kind=kOutput, calls=%fused_computation | convolution fusion | flops 2151677952 | bytes 12845056 | tf_op jit(solution)/shard_map/dot_general | solution.py:12
  15.2 0.0 reduce-scatter.2.cloned.1.call-update
  15.3 0.9 copy-done.2
  16.2 0.2 fusion.37
  16.4 0.1 reshape.51
  16.5 0.1 constant_dynamic-slice_fusion.2
  16.6 3.6 %collective-permute-start.2 = (bf16[64,128]{1,0:T(8,128)(2,1)S(1)}, bf16[64,128]{1,0:T(8,128)(2,1)S(1)}, u32[]{:S(2)}, u32[]{:S(2)}) collective-permute-start(bf16[64,128]{1,0:T(8,128)(2,1)S(1)} %convert_bitcast_fusion), channel_id=1, source_target_pairs={{0,3},{1,0},{2,1},{3,2},{4,7},{5,4},{6,5},{7,6},{8,11},{9,8},{10,9... | collective-permute-start | bytes 49160 | tf_op jit(solution)/shard_map/ppermute | solution.py:16
  20.3 0.3 collective-permute-start.1
  20.6 0.7 collective-permute-start
  21.3 6.1 %fusion.2 = f32[64,8192]{1,0:T(8,128)} fusion(f32[8192,256]{1,0:T(8,128)} %param.8, f32[256,64]{0,1:T(8,128)S(1)} %copy-done.3), kind=kOutput, calls=%fused_computation.5 | convolution fusion | flops 270548992 | bytes 10551296 | tf_op jit(solution)/shard_map/dot_general | solution.py:12
  27.4 0.0 collective-permute-done.2
  27.4 0.0 collective-permute-done.1
  27.4 2.0 %fusion.4 = f32[8,8,64,128]{3,1,2,0:T(8,128)S(1)} fusion(f32[64,8192]{1,0:T(8,128)} %fusion.2, bf16[128,8192]{1,0:T(8,128)(2,1)S(1)} %copy-done, bf16[64,128]{1,0:T(8,128)(2,1)S(1)} %collective-permute-done.2, bf16[64,128]{1,0:T(8,128)(2,1)S(1)} %collective-permute-done.1, f32[64,128]{1,0:T(8,128)S(1)} %bitcast.93, bf16[64,128]{1,0:T(8,128)(2,1)S(1)} %collective-permute-done), kind=kOutput, calls=%fused_computation.7 | convolution fusion | flops 134799360 | bytes 6373376 | tf_op jit(solution)/shard_map/dot_general | solution.py:12
  29.4 0.4 copy.31
  29.8 1.2 copy.25
  31.0 0.0 copy-start.1
  31.1 1.3 copy-done.1
  32.4 0.1 fusion.21
  32.4 1.6 %collective-permute-start.3 = (bf16[128,16,128]{2,1,0:T(8,128)(2,1)S(1)}, bf16[128,16,128]{2,1,0:T(8,128)(2,1)S(1)}, u32[]{:S(2)}, u32[]{:S(2)}) collective-permute-start(bf16[128,16,128]{2,1,0:T(8,128)(2,1)S(1)} %fusion.21), channel_id=1, source_target_pairs={{0,4},{4,0},{1,5},{5,1},{2,6},{6,2},{3,7},{7,3},{8,12},{12,8},{9,1... | collective-permute-start | bytes 1572872 | tf_op jit(solution)/shard_map/ppermute | solution.py:16
  34.0 1.5 %collective-permute-done.3 = bf16[128,16,128]{2,1,0:T(8,128)(2,1)S(1)} collective-permute-done((bf16[128,16,128]{2,1,0:T(8,128)(2,1)S(1)}, bf16[128,16,128]{2,1,0:T(8,128)(2,1)S(1)}, u32[]{:S(2)}, u32[]{:S(2)}) %collective-permute-start.3) | collective-permute-done | bytes 524320 | tf_op jit(solution)/shard_map/ppermute | solution.py:16
  35.6 1.3 fusion.16
  36.9 16.0 %all_to_all.20 = bf16[128,16,128]{2,1,0:T(8,128)(2,1)S(1)} all-to-all(bf16[128,16,128]{2,1,0:T(8,128)(2,1)S(1)} %fusion.16), channel_id=1, replica_groups=mesh['z'=8,'x'=4,'c'=2,'y'=4] {'x','y'}, dimensions={0} | all-to-all | bytes 1048576 | tf_op jit(solution)/shard_map/all_to_all | solution.py:36
  52.9 0.1 reduce_sum.33
  53.1 17.6 %all_to_all.21 = bf16[8,8,16,128]{3,2,1,0:T(8,128)(2,1)S(1)} all-to-all(bf16[8,8,16,128]{3,2,1,0:T(8,128)(2,1)S(1)} %broadcast_in_dim.7), channel_id=1, replica_groups=mesh['z'=8,'x'=4,'c'=2,'y'=4] {'z'}, dimensions={0} | all-to-all | bytes 524288 | tf_op jit(solution)/shard_map/all_to_all | solution.py:38
  70.7 0.1 broadcast_in_dim.8
  70.8 15.2 %all_to_all.22 = bf16[16,8,16,128]{3,2,1,0:T(8,128)(2,1)S(1)} all-to-all(bf16[16,8,16,128]{3,2,1,0:T(8,128)(2,1)S(1)} %broadcast_in_dim.8), channel_id=1, replica_groups=mesh['z'=8,'x'=4,'c'=2,'y'=4] {'x','y'}, dimensions={0} | all-to-all | bytes 1048576 | tf_op jit(solution)/shard_map/all_to_all | solution.py:40
  86.1 4.1 %collective-permute-start.4 = (bf16[128,16,128]{2,1,0:T(8,128)(2,1)S(1)}, bf16[128,16,128]{2,1,0:T(8,128)(2,1)}, u32[]{:S(2)}, u32[]{:S(2)}) collective-permute-start(bf16[128,16,128]{2,1,0:T(8,128)(2,1)S(1)} %bitcast.90), channel_id=1, source_target_pairs={{0,4},{4,0},{1,5},{5,1},{2,6},{6,2},{3,7},{7,3},{8,12},{12,8},{9,1... | collective-permute-start | bytes 1572872 | tf_op jit(solution)/shard_map/ppermute | solution.py:16
  90.2 1.7 %collective-permute-done.4 = bf16[128,16,128]{2,1,0:T(8,128)(2,1)} collective-permute-done((bf16[128,16,128]{2,1,0:T(8,128)(2,1)S(1)}, bf16[128,16,128]{2,1,0:T(8,128)(2,1)}, u32[]{:S(2)}, u32[]{:S(2)}) %collective-permute-start.4) | collective-permute-done | bytes 524320 | tf_op jit(solution)/shard_map/ppermute | solution.py:16
  91.9 1.1 broadcast_select_fusion.1
  93.0 0.1 pad_maximum_fusion
  93.1 0.7 copy.26
  93.8 0.9 convolution_convert_fusion.3
  94.7 1.1 collective-permute-start.7
  95.8 1.2 collective-permute-start.6
  96.9 0.1 collective-permute-start.5
  97.1 0.1 fusion.27
  97.2 4.5 %fusion.5 = f32[64,256]{1,0:T(8,128)S(1)} fusion(f32[64,256]{1,0:T(8,128)S(1)} %fusion.27, f32[8192,256]{1,0:T(8,128)} %param.8, bf16[8,8,64,128]{3,2,1,0:T(8,128)(2,1)S(1)} %bitcast.79), kind=kOutput, calls=%fused_computation.8 | convolution fusion | flops 270548992 | bytes 9568256 | tf_op jit(solution)/shard_map/dot_general | solution.py:12
  101.7 1.2 fusion.14
  102.9 0.7 copy.27
  103.6 0.8 fusion.22
  104.4 0.1 fusion.24
  104.6 0.2 fusion.10
  104.8 1.3 collective-permute-start.8
  106.1 0.8 fusion.36
  106.8 5.8 %cholesky.17 = f32[64,64]{1,0:T(8,128)S(1)} custom-call(f32[64,64]{1,0:T(8,128)S(1)} %fusion.36), custom_call_target="Cholesky" | custom-call | tf_op jit(solution)/shard_map/jit(cholesky)/cholesky | solution.py:78
  112.7 0.0 collective-permute-done.8
  112.7 1.4 collective-permute-start.11
  114.1 0.2 collective-permute-start.10
  114.3 1.6 %collective-permute-start.9 = (bf16[64,256]{1,0:T(8,128)(2,1)S(1)}, bf16[64,256]{1,0:T(8,128)(2,1)S(1)}, u32[]{:S(2)}, u32[]{:S(2)}) collective-permute-start(bf16[64,256]{1,0:T(8,128)(2,1)S(1)} %add_convert_fusion.1), channel_id=1, source_target_pairs={{0,16},{8,24},{16,0},{24,8},{1,17},{9,25},{17,1},{25,9},{2,18},{10... | collective-permute-start | bytes 98312 | tf_op jit(solution)/shard_map/ppermute | solution.py:16
  115.9 2.1 %collective-permute-done.10 = bf16[64,256]{1,0:T(8,128)(2,1)S(1)} collective-permute-done((bf16[64,256]{1,0:T(8,128)(2,1)S(1)}, bf16[64,256]{1,0:T(8,128)(2,1)S(1)}, u32[]{:S(2)}, u32[]{:S(2)}) %collective-permute-start.10) | collective-permute-done | bytes 32800 | tf_op jit(solution)/shard_map/ppermute | solution.py:16
  118.0 0.5 collective-permute-done.9
  118.6 0.7 broadcast_in_dim.10
  119.3 3.4 %all-to-all-start.3 = ((bf16[8,64,256]{2,1,0:T(8,128)(2,1)}), bf16[8,64,256]{2,1,0:T(8,128)(2,1)S(1)}, u32[]{:S(2)}, u32[]{:S(2)}) async-start(bf16[8,64,256]{2,1,0:T(8,128)(2,1)} %broadcast_in_dim.10), calls=%async_computation.4 | async-start | bytes 524288 | tf_op jit(solution)/shard_map/all_to_all | solution.py:54
  122.7 0.6 compare_reduce_fusion
  123.3 0.7 fusion.33
  124.0 4.9 %custom-call.6 = f32[1,64,64]{1,2,0:T(8,128)S(1)} custom-call(f32[1,64,64]{2,1,0:T(8,128)S(1)} %fusion.33), custom_call_target="InvertDiagBlocksLowerTriangular" | custom-call | tf_op jit(solution)/shard_map/triangular_solve | solution.py:79
  128.9 0.2 fusion.34
  129.1 3.2 %all-to-all-done.3 = bf16[8,64,256]{2,1,0:T(8,128)(2,1)S(1)} async-done(((bf16[8,64,256]{2,1,0:T(8,128)(2,1)}), bf16[8,64,256]{2,1,0:T(8,128)(2,1)S(1)}, u32[]{:S(2)}, u32[]{:S(2)}) %all-to-all-start.3) | async-done | bytes 262176 | tf_op jit(solution)/shard_map/all_to_all | solution.py:54
  132.3 0.2 fusion.44
  132.5 0.0 copy-start.4
  132.6 0.3 convolution_convert_fusion.2
  132.8 3.3 %convolution_convert_fusion.1 = bf16[8192,256]{1,0:T(8,128)(2,1)} fusion(bf16[64,256]{1,0:T(8,128)(2,1)S(1)} %convolution_convert_fusion.2, bf16[8,8,64,128]{3,2,1,0:T(8,128)(2,1)S(1)} %bitcast.81), kind=kOutput, calls=%fused_computation.1 | convolution fusion | flops 270532608 | bytes 5275648 | tf_op jit(solution)/shard_map/dot_general | solution.py:12
  (20 shorter events, 0.2 us)
Async XLA Ops:
  7.2 20.2 %copy-start = (bf16[128,8192]{1,0:T(8,128)(2,1)S(1)}, bf16[128,8192]{1,0:T(8,128)(2,1)}, u32[]{:S(2)}) copy-start(bf16[128,8192]{1,0:T(8,128)(2,1)} %param.5) | copy-start | bytes 6291460
  7.2 129.0 %reduce-scatter.2.cloned.1.call-start = ((), (), s32[]{:S(2)}) async-start(), calls=%async_computation.5 | async-start | bytes 10485760 | tf_op jit(solution)/shard_map/reduce_scatter | solution.py:62
  15.2 0.9 copy-start.2
  15.2 1.0 copy-start.3
  16.6 10.8 %collective-permute-start.2 = (bf16[64,128]{1,0:T(8,128)(2,1)S(1)}, bf16[64,128]{1,0:T(8,128)(2,1)S(1)}, u32[]{:S(2)}, u32[]{:S(2)}) collective-permute-start(bf16[64,128]{1,0:T(8,128)(2,1)S(1)} %convert_bitcast_fusion), channel_id=1, source_target_pairs={{0,3},{1,0},{2,1},{3,2},{4,7},{5,4},{6,5},{7,6},{8,11},{9,8},{10,9... | collective-permute-start | bytes 49160 | tf_op jit(solution)/shard_map/ppermute | solution.py:16
  20.3 7.1 %collective-permute-start.1 = (bf16[64,128]{1,0:T(8,128)(2,1)S(1)}, bf16[64,128]{1,0:T(8,128)(2,1)S(1)}, u32[]{:S(2)}, u32[]{:S(2)}) collective-permute-start(bf16[64,128]{1,0:T(8,128)(2,1)S(1)} %convert_bitcast_fusion.1), channel_id=1, source_target_pairs={{0,2},{1,3},{2,0},{3,1},{4,6},{5,7},{6,4},{7,5},{8,10},{9,11},{10,... | collective-permute-start | bytes 49160 | tf_op jit(solution)/shard_map/ppermute | solution.py:16
  20.6 6.8 %collective-permute-start = (bf16[64,128]{1,0:T(8,128)(2,1)S(1)}, bf16[64,128]{1,0:T(8,128)(2,1)S(1)}, u32[]{:S(2)}, u32[]{:S(2)}) collective-permute-start(bf16[64,128]{1,0:T(8,128)(2,1)S(1)} %convert_bitcast_fusion.2), channel_id=1, source_target_pairs={{0,1},{1,2},{2,3},{3,0},{4,5},{5,6},{6,7},{7,4},{8,9},{9,10},{10,1... | collective-permute-start | bytes 49160 | tf_op jit(solution)/shard_map/ppermute | solution.py:16
  31.0 1.3 copy-start.1
  32.4 3.1 %collective-permute-start.3 = (bf16[128,16,128]{2,1,0:T(8,128)(2,1)S(1)}, bf16[128,16,128]{2,1,0:T(8,128)(2,1)S(1)}, u32[]{:S(2)}, u32[]{:S(2)}) collective-permute-start(bf16[128,16,128]{2,1,0:T(8,128)(2,1)S(1)} %fusion.21), channel_id=1, source_target_pairs={{0,4},{4,0},{1,5},{5,1},{2,6},{6,2},{3,7},{7,3},{8,12},{12,8},{9,1... | collective-permute-start | bytes 1572872 | tf_op jit(solution)/shard_map/ppermute | solution.py:16
  86.1 5.8 %collective-permute-start.4 = (bf16[128,16,128]{2,1,0:T(8,128)(2,1)S(1)}, bf16[128,16,128]{2,1,0:T(8,128)(2,1)}, u32[]{:S(2)}, u32[]{:S(2)}) collective-permute-start(bf16[128,16,128]{2,1,0:T(8,128)(2,1)S(1)} %bitcast.90), channel_id=1, source_target_pairs={{0,4},{4,0},{1,5},{5,1},{2,6},{6,2},{3,7},{7,3},{8,12},{12,8},{9,1... | collective-permute-start | bytes 1572872 | tf_op jit(solution)/shard_map/ppermute | solution.py:16
  94.7 8.9 %collective-permute-start.7 = (bf16[64,128]{1,0:T(8,128)(2,1)S(1)}, bf16[64,128]{1,0:T(8,128)(2,1)}, u32[]{:S(2)}, u32[]{:S(2)}) collective-permute-start(bf16[64,128]{1,0:T(8,128)(2,1)S(1)} %convolution_convert_fusion.3), channel_id=1, source_target_pairs={{0,3},{1,0},{2,1},{3,2},{4,7},{5,4},{6,5},{7,6},{8,11},{9,8},{10,9... | collective-permute-start | bytes 49160 | tf_op jit(solution)/shard_map/ppermute | solution.py:16
  95.8 8.7 %collective-permute-start.6 = (bf16[64,128]{1,0:T(8,128)(2,1)S(1)}, bf16[64,128]{1,0:T(8,128)(2,1)S(1)}, u32[]{:S(2)}, u32[]{:S(2)}) collective-permute-start(bf16[64,128]{1,0:T(8,128)(2,1)S(1)} %convolution_convert_fusion.3), channel_id=1, source_target_pairs={{0,2},{1,3},{2,0},{3,1},{4,6},{5,7},{6,4},{7,5},{8,10},{9,11},{10,... | collective-permute-start | bytes 49160 | tf_op jit(solution)/shard_map/ppermute | solution.py:16
  96.9 7.6 %collective-permute-start.5 = (bf16[64,128]{1,0:T(8,128)(2,1)S(1)}, bf16[64,128]{1,0:T(8,128)(2,1)S(1)}, u32[]{:S(2)}, u32[]{:S(2)}) collective-permute-start(bf16[64,128]{1,0:T(8,128)(2,1)S(1)} %convolution_convert_fusion.3), channel_id=1, source_target_pairs={{0,1},{1,2},{2,3},{3,0},{4,5},{5,6},{6,7},{7,4},{8,9},{9,10},{10,1... | collective-permute-start | bytes 49160 | tf_op jit(solution)/shard_map/ppermute | solution.py:16
  104.8 7.9 %collective-permute-start.8 = (bf16[64,256]{1,0:T(8,128)(2,1)S(1)}, bf16[64,256]{1,0:T(8,128)(2,1)S(1)}, u32[]{:S(2)}, u32[]{:S(2)}) collective-permute-start(bf16[64,256]{1,0:T(8,128)(2,1)S(1)} %fusion.10), channel_id=1, source_target_pairs={{0,4},{4,0},{1,5},{5,1},{2,6},{6,2},{3,7},{7,3},{8,12},{12,8},{9,1... | collective-permute-start | bytes 98312 | tf_op jit(solution)/shard_map/ppermute | solution.py:16
  112.7 3.2 %collective-permute-start.11 = (bf16[64,256]{1,0:T(8,128)(2,1)S(1)}, bf16[64,256]{1,0:T(8,128)(2,1)S(1)}, u32[]{:S(2)}, u32[]{:S(2)}) collective-permute-start(bf16[64,256]{1,0:T(8,128)(2,1)S(1)} %add_convert_fusion.1), channel_id=1, source_target_pairs={{0,24},{8,0},{16,8},{24,16},{1,25},{9,1},{17,9},{25,17},{2,26},{10... | collective-permute-start | bytes 98312 | tf_op jit(solution)/shard_map/ppermute | solution.py:16
  114.1 4.0 %collective-permute-start.10 = (bf16[64,256]{1,0:T(8,128)(2,1)S(1)}, bf16[64,256]{1,0:T(8,128)(2,1)S(1)}, u32[]{:S(2)}, u32[]{:S(2)}) collective-permute-start(bf16[64,256]{1,0:T(8,128)(2,1)S(1)} %add_convert_fusion.1), channel_id=1, source_target_pairs={{0,8},{8,16},{16,24},{24,0},{1,9},{9,17},{17,25},{25,1},{2,10},{10... | collective-permute-start | bytes 98312 | tf_op jit(solution)/shard_map/ppermute | solution.py:16
  114.3 4.3 %collective-permute-start.9 = (bf16[64,256]{1,0:T(8,128)(2,1)S(1)}, bf16[64,256]{1,0:T(8,128)(2,1)S(1)}, u32[]{:S(2)}, u32[]{:S(2)}) collective-permute-start(bf16[64,256]{1,0:T(8,128)(2,1)S(1)} %add_convert_fusion.1), channel_id=1, source_target_pairs={{0,16},{8,24},{16,0},{24,8},{1,17},{9,25},{17,1},{25,9},{2,18},{10... | collective-permute-start | bytes 98312 | tf_op jit(solution)/shard_map/ppermute | solution.py:16
  119.3 13.0 %all-to-all-start.3 = ((bf16[8,64,256]{2,1,0:T(8,128)(2,1)}), bf16[8,64,256]{2,1,0:T(8,128)(2,1)S(1)}, u32[]{:S(2)}, u32[]{:S(2)}) async-start(bf16[8,64,256]{2,1,0:T(8,128)(2,1)} %broadcast_in_dim.10), calls=%async_computation.4 | async-start | bytes 524288 | tf_op jit(solution)/shard_map/all_to_all | solution.py:54
  132.5 3.6 %copy-start.4 = (f32[64,256]{1,0:T(8,128)}, f32[64,256]{1,0:T(8,128)S(1)}, u32[]{:S(2)}) copy-start(f32[64,256]{1,0:T(8,128)S(1)} %fusion.44) | copy-start | bytes 196612
Sparse Core Ops, SparseCore 0:
  15.4 98.8 reduce-scatter.1

commit v2 on v1

v2 whole, which is shorter than its diff:
```python
import functools

import jax
import jax.numpy as jnp
from jax import lax
from jax.experimental import pallas as pl
from jax.experimental.pallas import tpu as pltpu
from jax.sharding import Mesh, PartitionSpec as P

F32 = jnp.float32
BF = jnp.bfloat16
N_Z, N_X, N_C, N_Y = 8, 4, 2, 4
D, RANK, COLS, ROWS = 8192, 64, 256, 128
LANES = 128
CHUNKS = D // LANES
HALF = CHUNKS // 2
STEP = 8
SPAN = STEP * LANES
VMEM = 48 * 1024 * 1024


def dot(a, b, ca, cb):
    return lax.dot_general(a, b, (((ca,), (cb,)), ((), ())), preferred_element_type=F32)


def shift(v, axis, n, k):
    return lax.ppermute(v, axis, [(i, (i + k) % n) for i in range(n)])


def pick(v, i):
    return lax.dynamic_index_in_dim(v, i, 0, keepdims=False)


def call(body, name, grid, scalars, in_specs, out_specs, out_shape, scratch, flops, nbytes):
    return pl.pallas_call(
        body,
        name=name,
        grid_spec=pltpu.PrefetchScalarGridSpec(
            num_scalar_prefetch=scalars,
            grid=grid,
            in_specs=in_specs,
            out_specs=out_specs,
            scratch_shapes=scratch,
        ),
        out_shape=out_shape,
        compiler_params=pltpu.CompilerParams(vmem_limit_bytes=VMEM),
        cost_estimate=pl.CostEstimate(flops=flops, bytes_accessed=nbytes, transcendentals=0),
    )


def whole(shape):
    return pl.BlockSpec(shape, lambda i, *s: (0,) * len(shape))


def partial_body(kg, w, out):
    out[...] = dot(kg[...], w[...], 1, 1).astype(BF)


def partial_grad(kg, w):
    n = kg.shape[0]
    return call(
        partial_body, "partial", (D // SPAN,), 0,
        [whole((n, COLS)), pl.BlockSpec((SPAN, COLS), lambda i: (i, 0))],
        pl.BlockSpec((n, SPAN), lambda i: (0, i)),
        jax.ShapeDtypeStruct((n, D), BF), [], 2 * n * COLS * D, 2 * D * (COLS + n),
    )(kg, w)


def left_body(h, q, kgq, err, acts, out):
    p = dot(q[...], err[...].astype(BF), 1, 1) + dot(kgq[...], acts[...], 1, 0)
    for j in range(STEP):
        out[j] = p[:, j * LANES:(j + 1) * LANES].astype(out.dtype)


def left(half, q, kgq, err, acts):
    n = HALF // STEP
    return call(
        left_body, "left", (n,), 1,
        [
            whole((RANK, COLS)),
            whole((RANK, ROWS)),
            pl.BlockSpec((SPAN, COLS), lambda i, h: (h[0] * n + i, 0)),
            pl.BlockSpec((ROWS, SPAN), lambda i, h: (0, h[0] * n + i)),
        ],
        pl.BlockSpec((STEP, RANK, LANES), lambda i, h: (i, 0, 0)),
        jax.ShapeDtypeStruct((HALF, RANK, LANES), BF), [],
        D * RANK * (COLS + ROWS), D // 2 * (COLS * 4 + ROWS * 2 + RANK * 2),
    )(half, q, kgq, err, acts)


def row(p):
    return jnp.concatenate([p[j] for j in range(STEP)], axis=1)


def add_to(out, value):
    @pl.when(pl.program_id(0) == 0)
    def _():
        out[...] = value

    @pl.when(pl.program_id(0) > 0)
    def _():
        out[...] += value


def act_body(h, p, acts, out):
    add_to(out, dot(row(p), acts[...], 1, 1))


def err_body(h, p, err, q, gram):
    v = row(p)
    add_to(q, dot(v, err[...].astype(BF), 1, 0))
    add_to(gram, dot(v, v, 1, 1))


def act_side(half, p, acts):
    n = HALF // STEP
    return call(
        act_body, "acts_p", (n,), 1,
        [
            pl.BlockSpec((STEP, RANK, LANES), lambda i, h: (i, 0, 0)),
            pl.BlockSpec((ROWS, SPAN), lambda i, h: (0, h[0] * n + i)),
        ],
        whole((RANK, ROWS)),
        jax.ShapeDtypeStruct((RANK, ROWS), F32), [],
        D * RANK * ROWS, D * (ROWS + RANK),
    )(half, p, acts)


def err_side(half, p, err):
    n = HALF // STEP
    return call(
        err_body, "err_p", (n,), 1,
        [
            pl.BlockSpec((STEP, RANK, LANES), lambda i, h: (i, 0, 0)),
            pl.BlockSpec((SPAN, COLS), lambda i, h: (h[0] * n + i, 0)),
        ],
        [whole((RANK, COLS)), whole((RANK, RANK))],
        [jax.ShapeDtypeStruct((RANK, COLS), F32), jax.ShapeDtypeStruct((RANK, RANK), F32)], [],
        D * RANK * (COLS + RANK), D * (COLS * 2 + RANK),
    )(half, p, err)


def right_body(y, qa, qb, a0, a1, a2, a3, kg, out):
    q = qa[...] + qb[...]
    for k, a in enumerate((a0, a1, a2, a3)):
        start = pl.multiple_of(lax.rem(y[0] + N_Y - k, N_Y) * ROWS, ROWS)
        q = q + dot(a[...], kg[pl.ds(start, ROWS), :], 1, 0)
    out[...] = q


def right(y, qa, qb, ap, kg):
    return call(
        right_body, "right", (1,), 1,
        [whole((RANK, COLS))] * 2 + [whole((RANK, ROWS))] * 4 + [whole((N_Y * ROWS, COLS))],
        whole((RANK, COLS)),
        jax.ShapeDtypeStruct((RANK, COLS), F32), [],
        2 * RANK * COLS * ROWS * N_Y, 4 * 10**5,
    )(y, qa, qb, *ap, kg)


def update_body(c, own, other, mix, out):
    p = jnp.where(pl.program_id(0) < HALF // STEP, own[...], other[...])
    for j in range(STEP):
        two = jnp.concatenate([p[j], p[j]], axis=0)
        out[j * LANES:(j + 1) * LANES, :] = dot(two, mix[...], 0, 0).astype(BF)


def update_from(c, own, other, mix):
    n = HALF // STEP
    return call(
        update_body, "update", (2 * n,), 1,
        [
            pl.BlockSpec((STEP, RANK, LANES), lambda i, c: (jnp.minimum(i, n - 1), 0, 0)),
            pl.BlockSpec((STEP, RANK, LANES), lambda i, c: (jnp.maximum(i - n, 0), 0, 0)),
            whole((2 * RANK, COLS)),
        ],
        pl.BlockSpec((SPAN, COLS), lambda i, c: (lax.rem(i + c[0] * n, 2 * n), 0)),
        jax.ShapeDtypeStruct((D, COLS), BF), [],
        4 * D * RANK * COLS, 2 * D * (RANK + COLS),
    )(c, own, other, mix)


def pairs(v):
    return (v[0] + v[2]) + (v[1] + v[3])


def ring4(b, axis):
    v = [b.astype(F32)] + [shift(b, axis, 4, k).astype(F32) for k in (1, 2, 3)]
    return pairs(v)


def local(acts, key_grad, w_key, error_fb, q_prev):
    y, c = lax.axis_index("y"), lax.axis_index("c")
    y1, c1 = y.astype(jnp.int32)[None], c.astype(jnp.int32)[None]
    q_t = q_prev.T.astype(BF)
    kgq = dot(q_t, key_grad, 1, 1)
    kgq = kgq.reshape(RANK, N_Y, ROWS).transpose(1, 0, 2)
    kgq, kg = lax.optimization_barrier((kgq, key_grad))
    sent = [shift(pick(kgq, (y + k) % N_Y).astype(BF), "y", N_Y, k) for k in (1, 2, 3)]

    act_grad = lax.psum_scatter(partial_grad(kg, w_key), "y", scatter_dimension=0, tiled=True)

    kgq = pick(kgq, y) + sum(s.astype(F32) for s in sent)
    kgq = kgq.astype(BF)
    give = left(1 - c1, q_t, kgq, error_fb, acts)
    got = shift(give, "c", 2, 1)
    p = left(c1, q_t, kgq, error_fb, acts)
    p = (p.astype(F32) + got.astype(F32)).astype(BF)
    p = lax.all_to_all(p, ("z", "x"), 0, 0, tiled=True).astype(F32).sum(0).astype(BF)
    p = ring4(p, "y").astype(BF)
    p = jnp.broadcast_to(p[None], (HALF, RANK, LANES))
    own = lax.all_to_all(p, ("z", "x"), 0, 0, tiled=True)

    other = shift(own, "c", 2, 1)
    ap_own = act_side(c1, own, acts)
    qa, gram_a = err_side(c1, own, error_fb)
    ap = (ap_own + act_side(1 - c1, other, acts)).astype(BF)
    ap = [ap] + [shift(ap, "y", N_Y, k) for k in (1, 2, 3)]
    qb, gram_b = err_side(1 - c1, other, error_fb)
    gram = gram_a + gram_b
    q = right(y1, qa, qb, ap, key_grad)

    q = q + shift(q, "c", 2, 1)
    q = ring4(q, "x").astype(BF)
    q, gram = lax.optimization_barrier((q, gram))
    q = lax.all_to_all(jnp.broadcast_to(q[None], (N_Z, RANK, COLS)), "z", 0, 0, tiled=True)
    factor = jnp.linalg.cholesky(gram)
    inv = lax.linalg.triangular_solve(factor, jnp.eye(RANK, dtype=F32), left_side=True, lower=True)
    q = q.astype(F32).sum(0)
    q_new = jnp.dot(inv, q, precision=lax.Precision.HIGHEST)
    mix = lax.dot_general(inv, q_new, (((0,), (0,)), ((), ())), precision=lax.Precision.HIGHEST)
    high = mix.astype(BF)
    low = (mix - high.astype(F32)).astype(BF)
    update = update_from(c1, own, other, jnp.concatenate([high, low], 0))
    return act_grad, update, q_new.T


def solution(mesh):
    fine = Mesh(mesh.devices.reshape(N_Z, N_X, N_C, N_Y), ("z", "x", "c", "y"))
    dp = ("z", "x", "c")
    rows = P(dp + ("y",), None)
    return jax.shard_map(
        local,
        mesh=fine,
        in_specs=(rows, P(dp, "y"), P(None, "y"), P(dp, "y"), P("y", None)),
        out_specs=(rows, P(None, "y"), P("y", None)),
        check_vma=False,
    )
```

time: 146 us -> 151 us (1.034)
  Pallas kernels: 0 us -> 28.7 us
  matrix products: 28.2 us -> 1.87 us
  starting transfers between devices: 20.7 us -> 26.8 us
  waiting for transfers between devices: 9.04 us -> 14.4 us
  other arithmetic: 15.6 us -> 12.5 us
  blocking collectives: 48.9 us -> 46.2 us
  local copies, waits for them, and re-layouts: 6.28 us -> 4.24 us
    pallas_call x0 -> x9, Pallas kernels: none -> 28.7 us  [the longest x2 7.84 us: err_side(): call(err_body, 'err_p', (n,), 1, [pl.BlockSpec((STEP, RANK, LANES), lambd...]
    dot_general x12 -> x1, matrix products: 27.5 us -> 1.19 us  [dot(): lax.dot_general(a, b, (((ca,), (cb,)), ((), ())), preferred_element_type=...]
    ppermute x12 -> x15, starting transfers between devices: 17.2 us -> 23.3 us  [shift(): return lax.ppermute(v, axis, [(i, (i + k) % n) for i in range(n)])]
    ppermute x12 -> x15, waiting for transfers between devices: 5.85 us -> 11.7 us  [shift(): return lax.ppermute(v, axis, [(i, (i + k) % n) for i in range(n)])]
    all_to_all x3 -> x2, blocking collectives: 48.9 us -> 46.2 us  [the longest x1 27.7 us: local(): lax.all_to_all(p, ('z', 'x'), 0, 0, tiled=True).astype(F32).sum(0)]
    unnamed x11 -> x12, local copies, waits for them, and re-layouts: 2.59 us -> 3.15 us
  transfers between devices with their start and end apart: 14 -> 17, of which waited for: 5 -> 10; matrix products, arithmetic and copies ran while one was open for 28% -> 10% of each run, Pallas kernels for 0% -> 15%
where the time goes in v2:
time: 151 us; the launch traced here: 149 us
  blocking collectives  46.2 us (31%)
  Pallas kernels  28.7 us (19%)
  starting transfers between devices  26.8 us (18%)
  waiting for transfers between devices  14.4 us (10%)
  between operations  14.4 us (10%)
  other arithmetic  12.5 us (8%)
  local copies, waits for them, and re-layouts  4.24 us (3%)
  matrix products  1.87 us (1%)
    all_to_all x1, blocking collectives, local(): lax.all_to_all(p, ('z', 'x'), 0, 0, tiled=True).astype(F32).sum(0)  27.7 us
    ppermute x15, starting transfers between devices, shift(): return lax.ppermute(v, axis, [(i, (i + k) % n) for i in range(n)])  23.3 us
    all_to_all x1, blocking collectives, local(): own = lax.all_to_all(p, ('z', 'x'), 0, 0, tiled=True)  18.4 us
    ppermute x15, waiting for transfers between devices, shift(): return lax.ppermute(v, axis, [(i, (i + k) % n) for i in range(n)])  11.7 us
    pallas_call x2, Pallas kernels, err_side(): call(err_body, 'err_p', (n,), 1, [pl.BlockSpec((STEP, RANK, LANES), lambd...  7.84 us
    pallas_call x2, Pallas kernels, left(): call(left_body, 'left', (n,), 1, [whole((RANK, COLS)), whole((RANK, ROWS)...  7.37 us
    another operation x3, other arithmetic, local(): factor = jnp.linalg.cholesky(gram)  6.51 us
    pallas_call x1, Pallas kernels, partial_grad(): call(partial_body, 'partial', (D // SPAN,), 0, [whole((n, COLS)), pl.Bloc...  6.42 us
  transfers between devices with their start and end apart: 17, of which 10 were waited for; matrix products, arithmetic and copies ran while one was open for 10% of the time, Pallas kernels for 15%

profile of v2, /device:TPU:1, one launch (start us, length us, event | category | flops | bytes accessed | tf_op | source)
XLA Modules:
  0.0 149.0 jit_solution(9253163566192528402)
XLA Ops:
  7.2 0.0 reduce-scatter.2.cloned.1.call-start
  7.2 1.2 convolution_bitcast_fusion
  8.4 0.0 copy-start.1
  8.4 2.2 %copy-done.1 = bf16[8192,256]{1,0:T(8,128)(2,1)S(1)} copy-done((bf16[8192,256]{1,0:T(8,128)(2,1)S(1)}, bf16[8192,256]{1,0:T(8,128)(2,1)}, u32[]{:S(2)}) %copy-start.1) | copy-done | bytes 4194328
  10.6 0.9 copy-done.2
  11.6 6.4 %partial.1 = bf16[512,8192]{1,0:T(8,128)(2,1)} custom-call(bf16[512,256]{1,0:T(8,128)(2,1)S(1)} %copy-done.2, bf16[8192,256]{1,0:T(8,128)(2,1)S(1)} %copy-done.1), custom_call_target="tpu_custom_call" | custom-call | flops 2147483648 | bytes 12582912 | tf_op jit(solution)/shard_map/partial/pallas_call | solution.py:61
  18.0 0.0 reduce-scatter.2.cloned.1.call-update
  18.1 3.6 %collective-permute-start.2 = (bf16[64,128]{1,0:T(8,128)(2,1)S(1)}, bf16[64,128]{1,0:T(8,128)(2,1)S(1)}, u32[]{:S(2)}, u32[]{:S(2)}) collective-permute-start(bf16[64,128]{1,0:T(8,128)(2,1)S(1)} %get-tuple-element.22), channel_id=1, source_target_pairs={{0,3},{1,0},{2,1},{3,2},{4,7},{5,4},{6,5},{7,6},{8,11},{9,8},{10,9... | collective-permute-start | bytes 49160 | tf_op jit(solution)/shard_map/ppermute | solution.py:27
  21.7 0.3 collective-permute-start.1
  22.1 0.7 collective-permute-start
  22.8 0.0 collective-permute-done.2
  22.8 3.0 %collective-permute-done.1 = bf16[64,128]{1,0:T(8,128)(2,1)S(1)} collective-permute-done((bf16[64,128]{1,0:T(8,128)(2,1)S(1)}, bf16[64,128]{1,0:T(8,128)(2,1)S(1)}, u32[]{:S(2)}, u32[]{:S(2)}) %collective-permute-start.1) | collective-permute-done | bytes 16416 | tf_op jit(solution)/shard_map/ppermute | solution.py:27
  25.8 0.2 collective-permute-done
  26.0 3.6 %left.3 = bf16[32,64,128]{2,1,0:T(8,128)(2,1)S(1)} custom-call(s32[1]{0:T(128)S(6)} %sub.8.h, bf16[64,256]{1,0:T(8,128)(2,1)S(1)} %convert_bitcast_fusion.q, bf16[64,128]{1,0:T(8,128)(2,1)S(1)} %fusion.4.kgq, f32[8192,256]{1,0:T(8,128)} %err.7, bf16[128,8192]{1,0:T(8,128)(2,1)S(1)} %copy-done), custom_call_target="tpu_custom_call" | custom-call | flops 201326592 | bytes 5767168 | tf_op jit(solution)/shard_map/left/pallas_call | solution.py:77
  29.6 2.4 %collective-permute-start.3 = (bf16[32,64,128]{2,1,0:T(8,128)(2,1)S(1)}, bf16[32,64,128]{2,1,0:T(8,128)(2,1)S(1)}, u32[]{:S(2)}, u32[]{:S(2)}) collective-permute-start(bf16[32,64,128]{2,1,0:T(8,128)(2,1)S(1)} %left.3), channel_id=1, source_target_pairs={{0,4},{4,0},{1,5},{5,1},{2,6},{6,2},{3,7},{7,3},{8,12},{12,8},{9,1... | collective-permute-start | bytes 1572872 | tf_op jit(solution)/shard_map/ppermute | solution.py:27
  32.0 3.8 %left.2 = bf16[32,64,128]{2,1,0:T(8,128)(2,1)S(1)} custom-call(s32[1]{0:T(128)} %bitcast.1.h.c, bf16[64,256]{1,0:T(8,128)(2,1)S(1)} %convert_bitcast_fusion.q, bf16[64,128]{1,0:T(8,128)(2,1)S(1)} %fusion.4.kgq, f32[8192,256]{1,0:T(8,128)} %err.7, bf16[128,8192]{1,0:T(8,128)(2,1)S(1)} %copy-done), custom_call_target="tpu_custom_call" | custom-call | flops 201326592 | bytes 5767168 | tf_op jit(solution)/shard_map/left/pallas_call | solution.py:77
  35.8 0.0 collective-permute-done.3
  35.8 0.2 add_convert_fusion
  36.0 27.7 %all_to_all.15 = bf16[32,64,128]{2,1,0:T(8,128)(2,1)S(1)} all-to-all(bf16[32,64,128]{2,1,0:T(8,128)(2,1)S(1)} %add_convert_fusion), channel_id=1, replica_groups=mesh['z'=8,'x'=4,'c'=2,'y'=4] {'z','x'}, dimensions={0} | all-to-all | bytes 1048576 | tf_op jit(solution)/shard_map/all_to_all | solution.py:209
  63.7 0.1 reduce_sum.21
  63.8 0.5 collective-permute-start.6
  64.3 1.0 collective-permute-start.5
  65.3 1.3 collective-permute-start.4
  66.6 0.8 collective-permute-done.6
  67.3 1.7 %collective-permute-done.5 = bf16[64,128]{1,0:T(8,128)(2,1)S(1)} collective-permute-done((bf16[64,128]{1,0:T(8,128)(2,1)S(1)}, bf16[64,128]{1,0:T(8,128)(2,1)S(1)}, u32[]{:S(2)}, u32[]{:S(2)}) %collective-permute-start.5) | collective-permute-done | bytes 16416 | tf_op jit(solution)/shard_map/ppermute | solution.py:27
  69.0 0.9 collective-permute-done.4
  69.9 0.1 broadcast_in_dim.10
  70.0 18.4 %all_to_all.16.p.own = bf16[32,64,128]{2,1,0:T(8,128)(2,1)S(1)} all-to-all(bf16[32,64,128]{2,1,0:T(8,128)(2,1)S(1)} %broadcast_in_dim.10), channel_id=1, replica_groups=mesh['z'=8,'x'=4,'c'=2,'y'=4] {'z','x'}, dimensions={0} | all-to-all | bytes 1048576 | tf_op jit(solution)/shard_map/all_to_all | solution.py:212
  88.5 5.5 %collective-permute-start.7 = (bf16[32,64,128]{2,1,0:T(8,128)(2,1)S(1)}, bf16[32,64,128]{2,1,0:T(8,128)(2,1)S(1)}, u32[]{:S(2)}, u32[]{:S(2)}) collective-permute-start(bf16[32,64,128]{2,1,0:T(8,128)(2,1)S(1)} %all_to_all.16.p.own), channel_id=1, source_target_pairs={{0,4},{4,0},{1,5},{5,1},{2,6},{6,2},{3,7},{7,3},{8,12},{12,8},{9,1... | collective-permute-start | bytes 1572872 | tf_op jit(solution)/shard_map/ppermute | solution.py:27
  94.0 1.0 acts_p.2
  95.0 0.5 collective-permute-done.7.p.other
  95.5 1.0 acts_p.3
  96.5 0.1 collective-permute-start.8
  96.6 2.5 %collective-permute-start.9 = (bf16[64,128]{1,0:T(8,128)(2,1)S(1)}, bf16[64,128]{1,0:T(8,128)(2,1)S(1)}, u32[]{:S(2)}, u32[]{:S(2)}) collective-permute-start(bf16[64,128]{1,0:T(8,128)(2,1)S(1)} %add_convert_fusion.2.a0), channel_id=1, source_target_pairs={{0,2},{1,3},{2,0},{3,1},{4,6},{5,7},{6,4},{7,5},{8,10},{9,11},{10,... | collective-permute-start | bytes 49160 | tf_op jit(solution)/shard_map/ppermute | solution.py:27
  99.2 0.6 collective-permute-start.10
  99.8 3.9 %err_p.2 = (f32[64,256]{1,0:T(8,128)S(1)}, f32[64,64]{1,0:T(8,128)S(1)}) custom-call(s32[1]{0:T(128)} %bitcast.1.h.c, bf16[32,64,128]{2,1,0:T(8,128)(2,1)S(1)} %all_to_all.16.p.own, f32[8192,256]{1,0:T(8,128)} %err.7), custom_call_target="tpu_custom_call" | custom-call | flops 167772160 | bytes 4718592 | tf_op jit(solution)/shard_map/err_p/pallas_call | solution.py:131
  103.7 0.0 copy-start.3
  103.7 4.0 %err_p.3 = (f32[64,256]{1,0:T(8,128)S(1)}, f32[64,64]{1,0:T(8,128)S(1)}) custom-call(s32[1]{0:T(128)S(6)} %sub.8.h, bf16[32,64,128]{2,1,0:T(8,128)(2,1)S(1)} %collective-permute-done.7.p.other, f32[8192,256]{1,0:T(8,128)} %err.7), custom_call_target="tpu_custom_call" | custom-call | flops 167772160 | bytes 4718592 | tf_op jit(solution)/shard_map/err_p/pallas_call | solution.py:131
  107.7 0.0 collective-permute-done.9.a2
  107.7 0.0 collective-permute-done.10.a3
  107.7 0.2 right.1
  107.9 1.2 collective-permute-start.11
  109.2 0.9 collective-permute-done.11
  110.1 0.5 collective-permute-start.13
  110.6 2.3 %collective-permute-start.14 = (f32[64,256]{1,0:T(8,128)S(1)}, f32[64,256]{1,0:T(8,128)S(1)}, u32[]{:S(2)}, u32[]{:S(2)}) collective-permute-start(f32[64,256]{1,0:T(8,128)S(1)} %add.102), channel_id=1, source_target_pairs={{0,24},{8,0},{16,8},{24,16},{1,25},{9,1},{17,9},{25,17},{2,26},{10... | collective-permute-start | bytes 196616 | tf_op jit(solution)/shard_map/ppermute | solution.py:27
  112.8 0.7 collective-permute-start.12
  113.5 0.1 copy.16
  113.6 0.1 copy.17
  113.7 0.8 collective-permute-done.13
  114.5 0.0 collective-permute-done.14
  114.5 3.0 %collective-permute-done.12 = f32[64,256]{1,0:T(8,128)S(1)} collective-permute-done((f32[64,256]{1,0:T(8,128)S(1)}, f32[64,256]{1,0:T(8,128)S(1)}, u32[]{:S(2)}, u32[]{:S(2)}) %collective-permute-start.12) | collective-permute-done | bytes 65568 | tf_op jit(solution)/shard_map/ppermute | solution.py:27
  117.5 0.1 copy.18
  117.6 5.8 %cholesky.17 = f32[64,64]{1,0:T(8,128)S(1)} custom-call(f32[64,64]{1,0:T(8,128)S(1)} %fusion.3), custom_call_target="Cholesky" | custom-call | tf_op jit(solution)/shard_map/jit(cholesky)/cholesky | solution.py:227
  123.4 0.7 broadcast_in_dim.23
  124.2 3.4 %all-to-all-start.2 = ((bf16[8,64,256]{2,1,0:T(8,128)(2,1)}), bf16[8,64,256]{2,1,0:T(8,128)(2,1)S(1)}, u32[]{:S(2)}, u32[]{:S(2)}) async-start(bf16[8,64,256]{2,1,0:T(8,128)(2,1)} %broadcast_in_dim.23), calls=%async_computation.3 | async-start | bytes 524288 | tf_op jit(solution)/shard_map/all_to_all | solution.py:226
  127.6 0.6 compare_reduce_fusion
  128.2 0.7 fusion
  128.9 4.9 %custom-call.6 = f32[1,64,64]{1,2,0:T(8,128)S(1)} custom-call(f32[1,64,64]{2,1,0:T(8,128)S(1)} %fusion), custom_call_target="InvertDiagBlocksLowerTriangular" | custom-call | tf_op jit(solution)/shard_map/triangular_solve | solution.py:228
  133.8 0.2 fusion.1
  134.0 2.6 %all-to-all-done.2 = bf16[8,64,256]{2,1,0:T(8,128)(2,1)S(1)} async-done(((bf16[8,64,256]{2,1,0:T(8,128)(2,1)}), bf16[8,64,256]{2,1,0:T(8,128)(2,1)S(1)}, u32[]{:S(2)}, u32[]{:S(2)}) %all-to-all-start.2) | async-done | bytes 262176 | tf_op jit(solution)/shard_map/all_to_all | solution.py:226
  136.7 0.2 fusion.9
  136.9 0.0 copy-start.5
  136.9 0.3 subtract_convert_fusion
  137.2 4.9 %update.1 = bf16[8192,256]{1,0:T(8,128)(2,1)} custom-call(s32[1]{0:T(128)} %bitcast.1.h.c, bf16[32,64,128]{2,1,0:T(8,128)(2,1)S(1)} %all_to_all.16.p.own, bf16[32,64,128]{2,1,0:T(8,128)(2,1)S(1)} %collective-permute-done.7.p.other, bf16[128,256]{1,0:T(8,128)(2,1)S(1)} %pad_maximum_fusion.mix), custom_call_target="tpu_custom_call" | custom-call | flops 536870912 | bytes 5242880 | tf_op jit(solution)/shard_map/update/pallas_call | solution.py:170
  (22 shorter events, 0.2 us)
Async XLA Ops:
  7.2 134.9 %reduce-scatter.2.cloned.1.call-start = ((), (), s32[]{:S(2)}) async-start(), calls=%async_computation.4 | async-start | bytes 10485760 | tf_op jit(solution)/shard_map/reduce_scatter | solution.py:201
  8.4 2.2 %copy-start.1 = (bf16[8192,256]{1,0:T(8,128)(2,1)S(1)}, bf16[8192,256]{1,0:T(8,128)(2,1)}, u32[]{:S(2)}) copy-start(bf16[8192,256]{1,0:T(8,128)(2,1)} %w.1) | copy-start | bytes 12582916
  10.6 0.9 copy-start.2
  18.0 4.8 %copy-start.4 = (f32[256,64]{0,1:T(8,128)S(1)}, f32[256,64]{0,1:T(8,128)}, u32[]{:S(2)}) copy-start(f32[256,64]{0,1:T(8,128)} %param.9) | copy-start | bytes 196612
  18.0 8.0 %copy-start = (bf16[128,8192]{1,0:T(8,128)(2,1)S(1)}, bf16[128,8192]{1,0:T(8,128)(2,1)}, u32[]{:S(2)}) copy-start(bf16[128,8192]{1,0:T(8,128)(2,1)} %acts.7) | copy-start | bytes 6291460
  18.1 4.7 %collective-permute-start.2 = (bf16[64,128]{1,0:T(8,128)(2,1)S(1)}, bf16[64,128]{1,0:T(8,128)(2,1)S(1)}, u32[]{:S(2)}, u32[]{:S(2)}) collective-permute-start(bf16[64,128]{1,0:T(8,128)(2,1)S(1)} %get-tuple-element.22), channel_id=1, source_target_pairs={{0,3},{1,0},{2,1},{3,2},{4,7},{5,4},{6,5},{7,6},{8,11},{9,8},{10,9... | collective-permute-start | bytes 49160 | tf_op jit(solution)/shard_map/ppermute | solution.py:27
  21.7 4.1 %collective-permute-start.1 = (bf16[64,128]{1,0:T(8,128)(2,1)S(1)}, bf16[64,128]{1,0:T(8,128)(2,1)S(1)}, u32[]{:S(2)}, u32[]{:S(2)}) collective-permute-start(bf16[64,128]{1,0:T(8,128)(2,1)S(1)} %get-tuple-element.23), channel_id=1, source_target_pairs={{0,2},{1,3},{2,0},{3,1},{4,6},{5,7},{6,4},{7,5},{8,10},{9,11},{10,... | collective-permute-start | bytes 49160 | tf_op jit(solution)/shard_map/ppermute | solution.py:27
  22.1 3.9 %collective-permute-start = (bf16[64,128]{1,0:T(8,128)(2,1)S(1)}, bf16[64,128]{1,0:T(8,128)(2,1)S(1)}, u32[]{:S(2)}, u32[]{:S(2)}) collective-permute-start(bf16[64,128]{1,0:T(8,128)(2,1)S(1)} %get-tuple-element.21), channel_id=1, source_target_pairs={{0,1},{1,2},{2,3},{3,0},{4,5},{5,6},{6,7},{7,4},{8,9},{9,10},{10,1... | collective-permute-start | bytes 49160 | tf_op jit(solution)/shard_map/ppermute | solution.py:27
  29.6 6.1 %collective-permute-start.3 = (bf16[32,64,128]{2,1,0:T(8,128)(2,1)S(1)}, bf16[32,64,128]{2,1,0:T(8,128)(2,1)S(1)}, u32[]{:S(2)}, u32[]{:S(2)}) collective-permute-start(bf16[32,64,128]{2,1,0:T(8,128)(2,1)S(1)} %left.3), channel_id=1, source_target_pairs={{0,4},{4,0},{1,5},{5,1},{2,6},{6,2},{3,7},{7,3},{8,12},{12,8},{9,1... | collective-permute-start | bytes 1572872 | tf_op jit(solution)/shard_map/ppermute | solution.py:27
  63.8 3.6 %collective-permute-start.6 = (bf16[64,128]{1,0:T(8,128)(2,1)S(1)}, bf16[64,128]{1,0:T(8,128)(2,1)S(1)}, u32[]{:S(2)}, u32[]{:S(2)}) collective-permute-start(bf16[64,128]{1,0:T(8,128)(2,1)S(1)} %reduce_sum.21), channel_id=1, source_target_pairs={{0,3},{1,0},{2,1},{3,2},{4,7},{5,4},{6,5},{7,6},{8,11},{9,8},{10,9... | collective-permute-start | bytes 49160 | tf_op jit(solution)/shard_map/ppermute | solution.py:27
  64.3 4.7 %collective-permute-start.5 = (bf16[64,128]{1,0:T(8,128)(2,1)S(1)}, bf16[64,128]{1,0:T(8,128)(2,1)S(1)}, u32[]{:S(2)}, u32[]{:S(2)}) collective-permute-start(bf16[64,128]{1,0:T(8,128)(2,1)S(1)} %reduce_sum.21), channel_id=1, source_target_pairs={{0,1},{1,2},{2,3},{3,0},{4,5},{5,6},{6,7},{7,4},{8,9},{9,10},{10,1... | collective-permute-start | bytes 49160 | tf_op jit(solution)/shard_map/ppermute | solution.py:27
  65.3 4.6 %collective-permute-start.4 = (bf16[64,128]{1,0:T(8,128)(2,1)S(1)}, bf16[64,128]{1,0:T(8,128)(2,1)S(1)}, u32[]{:S(2)}, u32[]{:S(2)}) collective-permute-start(bf16[64,128]{1,0:T(8,128)(2,1)S(1)} %reduce_sum.21), channel_id=1, source_target_pairs={{0,2},{1,3},{2,0},{3,1},{4,6},{5,7},{6,4},{7,5},{8,10},{9,11},{10,... | collective-permute-start | bytes 49160 | tf_op jit(solution)/shard_map/ppermute | solution.py:27
  88.5 7.1 %collective-permute-start.7 = (bf16[32,64,128]{2,1,0:T(8,128)(2,1)S(1)}, bf16[32,64,128]{2,1,0:T(8,128)(2,1)S(1)}, u32[]{:S(2)}, u32[]{:S(2)}) collective-permute-start(bf16[32,64,128]{2,1,0:T(8,128)(2,1)S(1)} %all_to_all.16.p.own), channel_id=1, source_target_pairs={{0,4},{4,0},{1,5},{5,1},{2,6},{6,2},{3,7},{7,3},{8,12},{12,8},{9,1... | collective-permute-start | bytes 1572872 | tf_op jit(solution)/shard_map/ppermute | solution.py:27
  96.5 11.2 %collective-permute-start.8 = (bf16[64,128]{1,0:T(8,128)(2,1)S(1)}, bf16[64,128]{1,0:T(8,128)(2,1)S(1)}, u32[]{:S(2)}, u32[]{:S(2)}) collective-permute-start(bf16[64,128]{1,0:T(8,128)(2,1)S(1)} %add_convert_fusion.2.a0), channel_id=1, source_target_pairs={{0,1},{1,2},{2,3},{3,0},{4,5},{5,6},{6,7},{7,4},{8,9},{9,10},{10,1... | collective-permute-start | bytes 49160 | tf_op jit(solution)/shard_map/ppermute | solution.py:27
  96.6 11.1 %collective-permute-start.9 = (bf16[64,128]{1,0:T(8,128)(2,1)S(1)}, bf16[64,128]{1,0:T(8,128)(2,1)S(1)}, u32[]{:S(2)}, u32[]{:S(2)}) collective-permute-start(bf16[64,128]{1,0:T(8,128)(2,1)S(1)} %add_convert_fusion.2.a0), channel_id=1, source_target_pairs={{0,2},{1,3},{2,0},{3,1},{4,6},{5,7},{6,4},{7,5},{8,10},{9,11},{10,... | collective-permute-start | bytes 49160 | tf_op jit(solution)/shard_map/ppermute | solution.py:27
  99.2 8.5 %collective-permute-start.10 = (bf16[64,128]{1,0:T(8,128)(2,1)S(1)}, bf16[64,128]{1,0:T(8,128)(2,1)S(1)}, u32[]{:S(2)}, u32[]{:S(2)}) collective-permute-start(bf16[64,128]{1,0:T(8,128)(2,1)S(1)} %add_convert_fusion.2.a0), channel_id=1, source_target_pairs={{0,3},{1,0},{2,1},{3,2},{4,7},{5,4},{6,5},{7,6},{8,11},{9,8},{10,9... | collective-permute-start | bytes 49160 | tf_op jit(solution)/shard_map/ppermute | solution.py:27
  103.7 4.0 %copy-start.3 = (bf16[512,256]{1,0:T(8,128)(2,1)S(1)}, bf16[512,256]{1,0:T(8,128)(2,1)}, u32[]{:S(2)}) copy-start(bf16[512,256]{1,0:T(8,128)(2,1)} %kg.2) | copy-start | bytes 786436
  107.9 2.1 %collective-permute-start.11 = (f32[64,256]{1,0:T(8,128)S(1)}, f32[64,256]{1,0:T(8,128)S(1)}, u32[]{:S(2)}, u32[]{:S(2)}) collective-permute-start(f32[64,256]{1,0:T(8,128)S(1)} %right.1), channel_id=1, source_target_pairs={{0,4},{4,0},{1,5},{5,1},{2,6},{6,2},{3,7},{7,3},{8,12},{12,8},{9,1... | collective-permute-start | bytes 196616 | tf_op jit(solution)/shard_map/ppermute | solution.py:27
  110.1 4.4 %collective-permute-start.13 = (f32[64,256]{1,0:T(8,128)S(1)}, f32[64,256]{1,0:T(8,128)S(1)}, u32[]{:S(2)}, u32[]{:S(2)}) collective-permute-start(f32[64,256]{1,0:T(8,128)S(1)} %add.102), channel_id=1, source_target_pairs={{0,8},{8,16},{16,24},{24,0},{1,9},{9,17},{17,25},{25,1},{2,10},{10... | collective-permute-start | bytes 196616 | tf_op jit(solution)/shard_map/ppermute | solution.py:27
  110.6 3.9 %collective-permute-start.14 = (f32[64,256]{1,0:T(8,128)S(1)}, f32[64,256]{1,0:T(8,128)S(1)}, u32[]{:S(2)}, u32[]{:S(2)}) collective-permute-start(f32[64,256]{1,0:T(8,128)S(1)} %add.102), channel_id=1, source_target_pairs={{0,24},{8,0},{16,8},{24,16},{1,25},{9,1},{17,9},{25,17},{2,26},{10... | collective-permute-start | bytes 196616 | tf_op jit(solution)/shard_map/ppermute | solution.py:27
  112.8 4.6 %collective-permute-start.12 = (f32[64,256]{1,0:T(8,128)S(1)}, f32[64,256]{1,0:T(8,128)S(1)}, u32[]{:S(2)}, u32[]{:S(2)}) collective-permute-start(f32[64,256]{1,0:T(8,128)S(1)} %add.102), channel_id=1, source_target_pairs={{0,16},{8,24},{16,0},{24,8},{1,17},{9,25},{17,1},{25,9},{2,18},{10... | collective-permute-start | bytes 196616 | tf_op jit(solution)/shard_map/ppermute | solution.py:27
  124.2 12.5 %all-to-all-start.2 = ((bf16[8,64,256]{2,1,0:T(8,128)(2,1)}), bf16[8,64,256]{2,1,0:T(8,128)(2,1)S(1)}, u32[]{:S(2)}, u32[]{:S(2)}) async-start(bf16[8,64,256]{2,1,0:T(8,128)(2,1)} %broadcast_in_dim.23), calls=%async_computation.3 | async-start | bytes 524288 | tf_op jit(solution)/shard_map/all_to_all | solution.py:226
  136.9 5.2 %copy-start.5 = (f32[64,256]{1,0:T(8,128)}, f32[64,256]{1,0:T(8,128)S(1)}, u32[]{:S(2)}) copy-start(f32[64,256]{1,0:T(8,128)S(1)} %fusion.9) | copy-start | bytes 196612
Sparse Core Ops, SparseCore 0:
  18.1 88.3 reduce-scatter.1

commit v3 on v0

v3 whole, which is shorter than its diff:
```python
import jax
import jax.numpy as jnp
from jax import lax
from jax.experimental import pallas as pl
from jax.experimental.pallas import tpu as pltpu
from jax.sharding import Mesh, PartitionSpec as P

F32 = jnp.float32
BF = jnp.bfloat16
N_Z, N_X, N_C, N_Y = 8, 4, 2, 4
D, RANK, COLS, ROWS = 8192, 64, 256, 128
LANES = 128
CHUNKS = D // LANES
HALF = CHUNKS // 2
STEP = 8
SPAN = STEP * LANES
STEPS = HALF // STEP
PARTS = 4
IN_VMEM = pl.BlockSpec(memory_space=pltpu.VMEM)
IN_SMEM = pl.BlockSpec(memory_space=pltpu.SMEM)
IN_HBM = pl.BlockSpec(memory_space=pltpu.HBM)


def dot(a, b, ca, cb):
    return lax.dot_general(a, b, (((ca,), (cb,)), ((), ())), preferred_element_type=F32)


def shift(v, axis, n, k):
    return lax.ppermute(v, axis, [(i, (i + k) % n) for i in range(n)])


def kernel(body, name, ins, outs, out_shape, flops, nbytes, scratch=(), mib=8):
    return pl.pallas_call(
        body,
        name=name,
        in_specs=ins,
        out_specs=outs,
        out_shape=out_shape,
        scratch_shapes=list(scratch),
        compiler_params=pltpu.CompilerParams(vmem_limit_bytes=mib * 1024 * 1024),
        cost_estimate=pl.CostEstimate(flops=flops, bytes_accessed=nbytes, transcendentals=0),
    )


def shape(s, dtype):
    return jax.ShapeDtypeStruct(s, dtype)


def at(half, i):
    return pl.multiple_of(half * (D // 2) + i * SPAN, SPAN)


def tie(first, then):
    return lax.optimization_barrier((first, then))


def small_body(y, q, kg, q_t, own, s1, s2, s3):
    qt = q[...].T.astype(BF)
    q_t[...] = qt
    for k, out in enumerate((own, s1, s2, s3)):
        start = pl.multiple_of(lax.rem(y[0] + k, N_Y) * ROWS, ROWS)
        out[...] = dot(qt, kg[pl.ds(start, ROWS), :], 1, 1).astype(out.dtype)


def small(y, q, kg):
    block = (RANK, ROWS)
    return kernel(
        small_body, "small", [IN_SMEM, IN_VMEM, IN_VMEM], [IN_VMEM] * 5,
        [shape((RANK, COLS), BF), shape(block, F32)] + [shape(block, BF)] * 3,
        2 * RANK * COLS * ROWS * N_Y, 4 * 10**5,
    )(y, q, kg)


def partial_body(kg, w, out, kg_in, w_in, held, sem_kg, sem_w, sem_out):
    n = D // PARTS

    def load(i):
        span = pl.ds(i * n, n)
        return pltpu.make_async_copy(w.at[span], w_in.at[span], sem_w.at[i])

    def store(i):
        cols = pl.ds(i * n, n)
        return pltpu.make_async_copy(held.at[:, cols], out.at[:, cols], sem_out.at[i])

    first = pltpu.make_async_copy(kg, kg_in, sem_kg)
    first.start()
    for i in range(PARTS):
        load(i).start()
    first.wait()
    for i in range(PARTS):
        load(i).wait()
        for j in range(n // SPAN):
            cols = slice(i * n + j * SPAN, i * n + (j + 1) * SPAN)
            held[:, cols] = dot(kg_in[...], w_in[cols, :], 1, 1).astype(BF)
        store(i).start()
    for i in range(PARTS):
        store(i).wait()


def partial_grad(kg, w):
    n = kg.shape[0]
    dma = pltpu.SemaphoreType.DMA
    return kernel(
        partial_body, "partial", [IN_HBM, IN_HBM], IN_HBM, pltpu.HBM((n, D), BF),
        2 * n * COLS * D, 2 * D * (COLS + n),
        [
            pltpu.VMEM((n, COLS), BF), pltpu.VMEM((D, COLS), BF), pltpu.VMEM((n, D), BF),
            dma(()), dma((PARTS,)), dma((PARTS,)),
        ],
        24,
    )(*(pltpu.with_memory_space_constraint(v, pltpu.HBM) for v in (kg, w)))


def error_body(q, err, pe, eb, held, sem):
    def load(i):
        span = pl.ds(i * SPAN, SPAN)
        return pltpu.make_async_copy(err.at[span], held.at[span], sem.at[i])

    for i in range(D // SPAN):
        load(i).start()
    for i in range(D // SPAN):
        load(i).wait()
        span = slice(i * SPAN, (i + 1) * SPAN)
        e = held[span, :].astype(BF)
        eb[span, :] = e
        p = dot(q[...], e, 1, 1)
        for j in range(STEP):
            pe[i * STEP + j] = p[:, j * LANES:(j + 1) * LANES]


def error_side(q, err):
    return kernel(
        error_body, "error", [IN_VMEM, IN_HBM], [IN_VMEM, IN_VMEM],
        [pltpu.VMEM((CHUNKS, RANK, LANES), F32), pltpu.VMEM((D, COLS), BF)],
        2 * D * RANK * COLS, D * (COLS * 6 + RANK * 4),
        [pltpu.VMEM((D, COLS), F32), pltpu.SemaphoreType.DMA((D // SPAN,))], 16,
    )(q, pltpu.with_memory_space_constraint(err, pltpu.HBM))


def left_body(h, k0, k1, k2, k3, pe, acts, out):
    kgq = k0[...]
    for k in (k1, k2, k3):
        kgq = kgq + k[...].astype(F32)
    kgq = kgq.astype(BF)
    for i in range(STEPS):
        p = dot(kgq, acts[:, pl.ds(at(h[0], i), SPAN)], 1, 0)
        for j in range(STEP):
            k = i * STEP + j
            out[k] = (p[:, j * LANES:(j + 1) * LANES] + pe[h[0] * HALF + k]).astype(out.dtype)


def left(half, kgq, pe, acts, dtype):
    return kernel(
        left_body, "left", [IN_SMEM] + [IN_VMEM] * 6, IN_VMEM,
        shape((HALF, RANK, LANES), dtype),
        D * RANK * ROWS, D // 2 * (ROWS * 2 + RANK * 6),
    )(half, *kgq, pe, acts)


def rows(p, i):
    return jnp.concatenate([p[i * STEP + j] for j in range(STEP)], axis=1)


def act_body(h, p, acts, out):
    out[...] = sum(dot(rows(p, i), acts[:, pl.ds(at(h[0], i), SPAN)], 1, 1) for i in range(STEPS))


def act_side(half, p, acts):
    return kernel(
        act_body, "acts_p", [IN_SMEM, IN_VMEM, IN_VMEM], IN_VMEM, shape((RANK, ROWS), F32),
        D * RANK * ROWS, D * (ROWS + RANK),
    )(half, p, acts)


def err_body(h, p, err, out):
    out[...] = sum(
        dot(rows(p, i), err[pl.ds(at(h[0], i), SPAN), :], 1, 0) for i in range(STEPS)
    )


def err_side(half, p, err):
    return kernel(
        err_body, "err_p", [IN_SMEM, IN_VMEM, IN_VMEM], IN_VMEM, shape((RANK, COLS), F32),
        D * RANK * COLS, D * (COLS * 2 + RANK),
    )(half, p, err)


def right_body(y, qa, qb, a0, a1, a2, a3, kg, out):
    q = qa[...] + qb[...]
    for k, a in enumerate((a0, a1, a2, a3)):
        start = pl.multiple_of(lax.rem(y[0] + N_Y - k, N_Y) * ROWS, ROWS)
        q = q + dot(a[...], kg[pl.ds(start, ROWS), :], 1, 0)
    out[...] = q


def right(y, qa, qb, ap, kg):
    return kernel(
        right_body, "right", [IN_SMEM] + [IN_VMEM] * 7, IN_VMEM, shape((RANK, COLS), F32),
        2 * RANK * COLS * ROWS * N_Y, 4 * 10**5,
    )(y, qa, qb, *ap, kg)


def inverse_body(own, other, out):
    gram = jnp.zeros((RANK, RANK), F32)
    for p in (own, other):
        for i in range(STEPS):
            v = rows(p, i)
            gram = gram + dot(v, v, 1, 1)
    r = lax.broadcasted_iota(jnp.int32, (RANK, RANK), 0)
    c = lax.broadcasted_iota(jnp.int32, (RANK, RANK), 1)
    m = jnp.concatenate([gram, jnp.where(r == c, 1.0, 0.0)], axis=1)
    line = lax.broadcasted_iota(jnp.int32, (RANK, 1), 0)
    scale = jnp.zeros((RANK, 1), F32)
    for k in range(RANK):
        pivot = m[k:k + 1, k:k + 1]
        scale = jnp.where(line == k, lax.rsqrt(pivot), scale)
        if k < RANK - 1:
            f = jnp.where(line > k, m[:, k:k + 1] / pivot, 0.0)
            m = m - f * m[k:k + 1, :]
    out[...] = m[:, RANK:] * scale


def inverse(own, other):
    return kernel(
        inverse_body, "inverse", [IN_VMEM, IN_VMEM], IN_VMEM, shape((RANK, RANK), F32),
        2 * D * RANK * RANK, 4 * D * RANK,
    )(own, other)


def update_body(c, own, other, mix, out, held, sem):
    def copy(half):
        span = pl.ds(pl.multiple_of(half * (D // 2), D // 2), D // 2)
        return pltpu.make_async_copy(held.at[span], out.at[span], sem.at[half])

    for half, p in ((c[0], own), (1 - c[0], other)):
        for i in range(STEPS):
            v = rows(p, i)
            v = jnp.concatenate([v, v], axis=0)
            held[pl.ds(at(half, i), SPAN), :] = dot(v, mix[...], 0, 0).astype(BF)
        copy(half).start()
    copy(c[0]).wait()
    copy(1 - c[0]).wait()


def update_from(c, own, other, mix):
    return kernel(
        update_body, "update", [IN_SMEM] + [IN_VMEM] * 3, IN_HBM, shape((D, COLS), BF),
        4 * D * RANK * COLS, 2 * D * (RANK + COLS),
        [pltpu.VMEM((D, COLS), BF), pltpu.SemaphoreType.DMA((2,))], 12,
    )(c, own, other, mix)


def merge_body(v, out):
    total = v[0].astype(F32)
    for i in range(1, v.shape[0]):
        total = total + v[i].astype(F32)
    total = total.astype(BF)
    for i in range(out.shape[0]):
        out[i] = total


def merge(v, copies):
    block = v.shape[1:]
    size = v.size // v.shape[0]
    return kernel(
        merge_body, "merge", [IN_VMEM], IN_VMEM, shape((copies,) + block, BF),
        v.size, 2 * size * (v.shape[0] + copies),
    )(v)


def pairs_body(a, b, c, d, out):
    total = ((a[...] + c[...]) + (b[...] + d[...])).astype(BF)
    for i in range(out.shape[0]):
        out[i] = total


def ring_sum(v, axis, copies):
    v = [v] + [shift(v, axis, 4, k) for k in (1, 2, 3)]
    return kernel(
        pairs_body, "pairs", [IN_VMEM] * 4, IN_VMEM, shape((copies,) + v[0].shape, BF),
        4 * v[0].size, 2 * v[0].size * (8 + copies),
    )(*v)


def exchange(v, axes):
    return lax.all_to_all(v, axes, 0, 0, tiled=True)


def sum_left(p):
    n = HALF // 16
    p = merge(exchange(p, ("x", "y")).reshape(16, n, RANK, LANES), N_Z)
    p = merge(exchange(p, "z"), 16)
    return exchange(p, ("x", "y")).reshape(HALF, RANK, LANES)


def local(acts, key_grad, w_key, error_fb, q_prev):
    y = lax.axis_index("y").astype(jnp.int32)[None]
    c = lax.axis_index("c").astype(jnp.int32)[None]
    part = partial_grad(key_grad, w_key)
    act_grad = lax.psum_scatter(part, "y", scatter_dimension=0, tiled=True)
    q_t, k0, k1, k2, k3 = small(y, q_prev, key_grad)
    k1, q_t = tie(k1, q_t)
    kgq = [k0] + [shift(v, "y", N_Y, k) for k, v in ((1, k1), (2, k2), (3, k3))]
    pe, err = error_side(q_t, error_fb)

    got = shift(left(1 - c, kgq, pe, acts, BF), "c", 2, 1)
    p = left(c, kgq, pe, acts, F32)
    own = sum_left((p + got.astype(F32)).astype(BF))

    other = shift(own, "c", 2, 1)
    ap = act_side(c, own, acts)
    qa = err_side(c, own, err)
    ap = (ap + act_side(1 - c, other, acts)).astype(BF)
    ap = [ap] + [shift(ap, "y", N_Y, k) for k in (1, 2, 3)]
    qb = err_side(1 - c, other, err)
    q = right(y, qa, qb, ap, key_grad)

    q = q + shift(q, "c", 2, 1)
    q = ring_sum(q, "x", N_Z)
    q, other = tie(q, other)
    q = exchange(q, "z")
    inv = inverse(own, other)
    q = q.astype(F32).sum(0)
    q_new = jnp.dot(inv, q, precision=lax.Precision.HIGHEST)
    mix = lax.dot_general(inv, q_new, (((0,), (0,)), ((), ())), precision=lax.Precision.HIGHEST)
    high = mix.astype(BF)
    low = (mix - high.astype(F32)).astype(BF)
    update = update_from(c, own, other, jnp.concatenate([high, low], 0))
    return act_grad, update, q_new.T


def solution(mesh):
    fine = Mesh(mesh.devices.reshape(N_Z, N_X, N_C, N_Y), ("z", "x", "c", "y"))
    dp = ("z", "x", "c")
    rows_of = P(dp + ("y",), None)
    return jax.shard_map(
        local,
        mesh=fine,
        in_specs=(rows_of, P(dp, "y"), P(None, "y"), P(dp, "y"), P("y", None)),
        out_specs=(rows_of, P(None, "y"), P("y", None)),
        check_vma=False,
    )
```

time: 668 us -> 123 us (0.18)
  waiting for transfers between devices: 587 us -> 11.6 us
  matrix products: 50.1 us -> 0.45 us
  blocking collectives: 0 us -> 46.9 us
  starting transfers between devices: 0.56 us -> 24.5 us
  Pallas kernels: 0 us -> 23 us
  other arithmetic: 12.1 us -> 0.21 us
    psum x2 -> x0, waiting for transfers between devices: 421 us -> none  [the longest x1 261 us: local(): p_total = lax.psum(p_local, ('dp', 'tensor'))]
    all_gather x1 -> x0, waiting for transfers between devices: 91.4 us -> none  [local(): lax.all_gather(acts, 'tensor', axis=0, tiled=True)]
    reduce_scatter x1, waiting for transfers between devices: 73.9 us -> 0.02 us  [local(): act_grad = lax.psum_scatter(part, 'y', scatter_dimension=0, tiled=True)]
    all_to_all x0 -> x3, blocking collectives: none -> 46.9 us  [exchange(): return lax.all_to_all(v, axes, 0, 0, tiled=True)]
    dot_general x6 -> x2, matrix products: 46.7 us -> 0.45 us  [the longest x1 0.25 us: local(): lax.dot_general(inv, q_new, (((0,), (0,)), ((), ())), precision=lax.Preci...]
    pallas_call x0 -> x15, Pallas kernels: none -> 23 us  [the longest x1 6.33 us: partial_grad(): kernel(partial_body, 'partial', [IN_HBM, IN_HBM], IN_HBM, pltpu.HBM((n, D...]
    ppermute x0 -> x12, starting transfers between devices: none -> 21.1 us  [shift(): return lax.ppermute(v, axis, [(i, (i + k) % n) for i in range(n)])]
    another operation x5 -> x0, other arithmetic: 12.1 us -> none  [the longest x3 6.52 us: local(): factor = jnp.linalg.cholesky(gram_mat)]
  transfers between devices with their start and end apart: 4 -> 14, of which waited for: 4 -> 10; matrix products, arithmetic and copies ran while one was open for 3% -> 1% of each run, Pallas kernels for 0% -> 14%
where the time goes in v3:
time: 123 us; the launch traced here: 122 us
  blocking collectives  46.9 us (38%)
  starting transfers between devices  24.5 us (20%)
  Pallas kernels  23 us (19%)
  between operations  14.3 us (12%)
  waiting for transfers between devices  11.6 us (9%)
    all_to_all x3, blocking collectives, exchange(): return lax.all_to_all(v, axes, 0, 0, tiled=True)  46.9 us
    ppermute x12, starting transfers between devices, shift(): return lax.ppermute(v, axis, [(i, (i + k) % n) for i in range(n)])  21.1 us
    ppermute x12, waiting for transfers between devices, shift(): return lax.ppermute(v, axis, [(i, (i + k) % n) for i in range(n)])  7.44 us
    pallas_call x1, Pallas kernels, partial_grad(): kernel(partial_body, 'partial', [IN_HBM, IN_HBM], IN_HBM, pltpu.HBM((n, D...  6.33 us
    pallas_call x1, Pallas kernels, inverse(): kernel(inverse_body, 'inverse', [IN_VMEM, IN_VMEM], IN_VMEM, shape((RANK,...  6.05 us
    all_to_all x1, waiting for transfers between devices, exchange(): return lax.all_to_all(v, axes, 0, 0, tiled=True)  4.13 us
    pallas_call x1, Pallas kernels, error_side(): kernel(error_body, 'error', [IN_VMEM, IN_HBM], [IN_VMEM, IN_VMEM], [pltpu...  3.91 us
    all_to_all x1, starting transfers between devices, exchange(): return lax.all_to_all(v, axes, 0, 0, tiled=True)  3.41 us
  transfers between devices with their start and end apart: 14, of which 10 were waited for; matrix products, arithmetic and copies ran while one was open for 1% of the time, Pallas kernels for 14%

profile of v3, /device:TPU:1, one launch (start us, length us, event | category | flops | bytes accessed | tf_op | source)
XLA Modules:
  0.0 122.0 jit_solution(13523977759642493238)
XLA Ops:
  7.2 0.0 reduce-scatter.2.cloned.1.call-start
  7.2 6.3 %partial.1 = bf16[512,8192]{1,0:T(8,128)(2,1)} custom-call(bf16[512,256]{1,0:T(8,128)(2,1)} %kg.5, bf16[8192,256]{1,0:T(8,128)(2,1)} %w.1), custom_call_target="tpu_custom_call" | custom-call | flops 2147483648 | bytes 12582912 | tf_op jit(solution)/shard_map/partial/pallas_call | solution.py:103
  13.6 0.0 copy-start.3
  13.6 0.0 copy-start.1
  13.6 0.0 reduce-scatter.2.cloned.1.call-update
  13.6 0.8 copy-done.3
  14.4 0.1 copy.8.q
  14.5 0.1 copy-done.1
  14.5 0.2 small.1
  14.8 2.2 %collective-permute-start = (bf16[64,128]{1,0:T(8,128)(2,1)S(1)}, bf16[64,128]{1,0:T(8,128)(2,1)S(1)}, u32[]{:S(2)}, u32[]{:S(2)}) collective-permute-start(bf16[64,128]{1,0:T(8,128)(2,1)S(1)} %get-tuple-element.17), channel_id=1, source_target_pairs={{0,1},{1,2},{2,3},{3,0},{4,5},{5,6},{6,7},{7,4},{8,9},{9,10},{10,1... | collective-permute-start | bytes 49160 | tf_op jit(solution)/shard_map/ppermute | solution.py:29
  17.0 2.6 %collective-permute-start.1 = (bf16[64,128]{1,0:T(8,128)(2,1)S(1)}, bf16[64,128]{1,0:T(8,128)(2,1)S(1)}, u32[]{:S(2)}, u32[]{:S(2)}) collective-permute-start(bf16[64,128]{1,0:T(8,128)(2,1)S(1)} %get-tuple-element.18), channel_id=1, source_target_pairs={{0,2},{1,3},{2,0},{3,1},{4,6},{5,7},{6,4},{7,5},{8,10},{9,11},{10,... | collective-permute-start | bytes 49160 | tf_op jit(solution)/shard_map/ppermute | solution.py:29
  19.6 1.1 collective-permute-start.2
  20.7 0.0 copy-start
  20.7 3.9 %error.1 = (f32[64,64,128]{2,1,0:T(8,128)S(1)}, bf16[8192,256]{1,0:T(8,128)(2,1)S(1)}) custom-call(bf16[64,256]{1,0:T(8,128)(2,1)S(1)} %get-tuple-element.20.q, f32[8192,256]{1,0:T(8,128)} %err.1), custom_call_target="tpu_custom_call" | custom-call | flops 268435456 | bytes 14680064 | tf_op jit(solution)/shard_map/error/pallas_call | solution.py:132
  24.6 0.0 collective-permute-done.k1
  24.6 0.0 collective-permute-done.1.k2
  24.6 0.0 collective-permute-done.2.k3
  24.6 0.1 copy-done
  24.7 0.3 left.3
  25.0 1.6 %collective-permute-start.3 = (bf16[32,64,128]{2,1,0:T(8,128)(2,1)S(1)}, bf16[32,64,128]{2,1,0:T(8,128)(2,1)S(1)}, u32[]{:S(2)}, u32[]{:S(2)}) collective-permute-start(bf16[32,64,128]{2,1,0:T(8,128)(2,1)S(1)} %left.3), channel_id=1, source_target_pairs={{0,4},{4,0},{1,5},{5,1},{2,6},{6,2},{3,7},{7,3},{8,12},{12,8},{9,1... | collective-permute-start | bytes 1572872 | tf_op jit(solution)/shard_map/ppermute | solution.py:29
  26.7 0.3 left.2
  27.0 1.2 %collective-permute-done.3 = bf16[32,64,128]{2,1,0:T(8,128)(2,1)S(1)} collective-permute-done((bf16[32,64,128]{2,1,0:T(8,128)(2,1)S(1)}, bf16[32,64,128]{2,1,0:T(8,128)(2,1)S(1)}, u32[]{:S(2)}, u32[]{:S(2)}) %collective-permute-start.3) | collective-permute-done | bytes 524320 | tf_op jit(solution)/shard_map/ppermute | solution.py:29
  28.2 0.1 add_convert_fusion
  28.3 14.6 %all_to_all.20 = bf16[32,64,128]{2,1,0:T(8,128)(2,1)S(1)} all-to-all(bf16[32,64,128]{2,1,0:T(8,128)(2,1)S(1)} %add_convert_fusion), channel_id=1, replica_groups=mesh['z'=8,'x'=4,'c'=2,'y'=4] {'x','y'}, dimensions={0} | all-to-all | bytes 1048576 | tf_op jit(solution)/shard_map/all_to_all | solution.py:286
  43.0 0.1 merge.2
  43.0 17.4 %all_to_all.21.v = bf16[8,2,64,128]{3,2,1,0:T(8,128)(2,1)S(1)} all-to-all(bf16[8,2,64,128]{3,2,1,0:T(8,128)(2,1)S(1)} %merge.2), channel_id=1, replica_groups=mesh['z'=8,'x'=4,'c'=2,'y'=4] {'z'}, dimensions={0} | all-to-all | bytes 524288 | tf_op jit(solution)/shard_map/all_to_all | solution.py:286
  60.5 0.1 merge.3
  60.5 14.9 %all_to_all.22 = bf16[16,2,64,128]{3,2,1,0:T(8,128)(2,1)S(1)} all-to-all(bf16[16,2,64,128]{3,2,1,0:T(8,128)(2,1)S(1)} %merge.3), channel_id=1, replica_groups=mesh['z'=8,'x'=4,'c'=2,'y'=4] {'x','y'}, dimensions={0} | all-to-all | bytes 1048576 | tf_op jit(solution)/shard_map/all_to_all | solution.py:286
  75.4 4.2 %collective-permute-start.4 = (bf16[32,64,128]{2,1,0:T(8,128)(2,1)S(1)}, bf16[32,64,128]{2,1,0:T(8,128)(2,1)S(1)}, u32[]{:S(2)}, u32[]{:S(2)}) collective-permute-start(bf16[32,64,128]{2,1,0:T(8,128)(2,1)S(1)} %bitcast.9), channel_id=1, source_target_pairs={{0,4},{4,0},{1,5},{5,1},{2,6},{6,2},{3,7},{7,3},{8,12},{12,8},{9,1... | collective-permute-start | bytes 1572872 | tf_op jit(solution)/shard_map/ppermute | solution.py:29
  79.6 0.5 acts_p.2
  80.1 1.1 collective-permute-done.4.p.other
  81.2 0.5 acts_p.3
  81.6 0.5 collective-permute-start.5
  82.1 1.7 %collective-permute-start.6 = (bf16[64,128]{1,0:T(8,128)(2,1)S(1)}, bf16[64,128]{1,0:T(8,128)(2,1)S(1)}, u32[]{:S(2)}, u32[]{:S(2)}) collective-permute-start(bf16[64,128]{1,0:T(8,128)(2,1)S(1)} %add_convert_fusion.1.a0), channel_id=1, source_target_pairs={{0,2},{1,3},{2,0},{3,1},{4,6},{5,7},{6,4},{7,5},{8,10},{9,11},{10,... | collective-permute-start | bytes 49160 | tf_op jit(solution)/shard_map/ppermute | solution.py:29
  83.8 1.3 %collective-permute-start.7 = (bf16[64,128]{1,0:T(8,128)(2,1)S(1)}, bf16[64,128]{1,0:T(8,128)(2,1)S(1)}, u32[]{:S(2)}, u32[]{:S(2)}) collective-permute-start(bf16[64,128]{1,0:T(8,128)(2,1)S(1)} %add_convert_fusion.1.a0), channel_id=1, source_target_pairs={{0,3},{1,0},{2,1},{3,2},{4,7},{5,4},{6,5},{7,6},{8,11},{9,8},{10,9... | collective-permute-start | bytes 49160 | tf_op jit(solution)/shard_map/ppermute | solution.py:29
  85.1 0.5 err_p.2.qa
  85.6 0.5 err_p.3.qb
  86.1 0.1 collective-permute-done.5.a1
  86.2 0.3 collective-permute-done.6.a2
  86.6 0.8 collective-permute-done.7.a3
  87.3 0.2 right.1
  87.5 1.7 %collective-permute-start.8 = (f32[64,256]{1,0:T(8,128)S(1)}, f32[64,256]{1,0:T(8,128)S(1)}, u32[]{:S(2)}, u32[]{:S(2)}) collective-permute-start(f32[64,256]{1,0:T(8,128)S(1)} %right.1), channel_id=1, source_target_pairs={{0,4},{4,0},{1,5},{5,1},{2,6},{6,2},{3,7},{7,3},{8,12},{12,8},{9,1... | collective-permute-start | bytes 196616 | tf_op jit(solution)/shard_map/ppermute | solution.py:29
  89.3 0.9 collective-permute-done.8
  90.2 0.6 collective-permute-start.9
  90.8 2.4 %collective-permute-start.10 = (f32[64,256]{1,0:T(8,128)S(1)}, f32[64,256]{1,0:T(8,128)S(1)}, u32[]{:S(2)}, u32[]{:S(2)}) collective-permute-start(f32[64,256]{1,0:T(8,128)S(1)} %add.13.a), channel_id=1, source_target_pairs={{0,16},{8,24},{16,0},{24,8},{1,17},{9,25},{17,1},{25,9},{2,18},{10... | collective-permute-start | bytes 196616 | tf_op jit(solution)/shard_map/ppermute | solution.py:29
  93.2 1.2 collective-permute-start.11
  94.3 0.6 collective-permute-done.9.b
  95.0 1.1 collective-permute-done.10.c
  96.1 1.2 %collective-permute-done.11.d = f32[64,256]{1,0:T(8,128)S(1)} collective-permute-done((f32[64,256]{1,0:T(8,128)S(1)}, f32[64,256]{1,0:T(8,128)S(1)}, u32[]{:S(2)}, u32[]{:S(2)}) %collective-permute-start.11) | collective-permute-done | bytes 65568 | tf_op jit(solution)/shard_map/ppermute | solution.py:29
  97.4 0.7 pairs.1
  98.1 3.4 %all-to-all-start.3 = ((bf16[8,64,256]{2,1,0:T(8,128)(2,1)}), bf16[8,64,256]{2,1,0:T(8,128)(2,1)S(1)}, u32[]{:S(2)}, u32[]{:S(2)}) async-start(bf16[8,64,256]{2,1,0:T(8,128)(2,1)} %pairs.1), calls=%async_computation.4 | async-start | bytes 524288 | tf_op jit(solution)/shard_map/all_to_all | solution.py:286
  101.5 6.0 %inverse.1 = f32[64,64]{1,0:T(8,128)S(1)} custom-call(bf16[32,64,128]{2,1,0:T(8,128)(2,1)S(1)} %bitcast.12, bf16[32,64,128]{2,1,0:T(8,128)(2,1)S(1)} %collective-permute-done.4.p.other), custom_call_target="tpu_custom_call" | custom-call | flops 67108864 | bytes 2097152 | tf_op jit(solution)/shard_map/inverse/pallas_call | solution.py:224
  107.6 4.1 %all-to-all-done.3 = bf16[8,64,256]{2,1,0:T(8,128)(2,1)S(1)} async-done(((bf16[8,64,256]{2,1,0:T(8,128)(2,1)}), bf16[8,64,256]{2,1,0:T(8,128)(2,1)S(1)}, u32[]{:S(2)}, u32[]{:S(2)}) %all-to-all-start.3) | async-done | bytes 262176 | tf_op jit(solution)/shard_map/all_to_all | solution.py:286
  111.7 0.2 fusion
  111.9 0.0 copy-start.2
  111.9 0.3 subtract_convert_fusion
  112.2 2.9 %update.1 = bf16[8192,256]{1,0:T(8,128)(2,1)} custom-call(s32[1]{0:T(128)} %bitcast.h.c, bf16[32,64,128]{2,1,0:T(8,128)(2,1)S(1)} %bitcast.13, bf16[32,64,128]{2,1,0:T(8,128)(2,1)S(1)} %collective-permute-done.4.p.other, bf16[128,256]{1,0:T(8,128)(2,1)S(1)} %pad_maximum_fusion.mix), custom_call_target="tpu_custom_call" | custom-call | flops 536870912 | bytes 5242880 | tf_op jit(solution)/shard_map/update/pallas_call | solution.py:246
  115.1 0.0 reduce-scatter.2.cloned.1.call-done
  115.1 0.0 copy-done.2
  (4 shorter events, 0.1 us)
Async XLA Ops:
  7.2 108.0 %reduce-scatter.2.cloned.1.call-start = ((), (), s32[]{:S(2)}) async-start(), calls=%async_computation.5 | async-start | bytes 10485760 | tf_op jit(solution)/shard_map/reduce_scatter | solution.py:300
  13.6 0.8 copy-start.3
  13.6 1.0 copy-start.1
  14.8 9.8 %collective-permute-start = (bf16[64,128]{1,0:T(8,128)(2,1)S(1)}, bf16[64,128]{1,0:T(8,128)(2,1)S(1)}, u32[]{:S(2)}, u32[]{:S(2)}) collective-permute-start(bf16[64,128]{1,0:T(8,128)(2,1)S(1)} %get-tuple-element.17), channel_id=1, source_target_pairs={{0,1},{1,2},{2,3},{3,0},{4,5},{5,6},{6,7},{7,4},{8,9},{9,10},{10,1... | collective-permute-start | bytes 49160 | tf_op jit(solution)/shard_map/ppermute | solution.py:29
  17.0 7.6 %collective-permute-start.1 = (bf16[64,128]{1,0:T(8,128)(2,1)S(1)}, bf16[64,128]{1,0:T(8,128)(2,1)S(1)}, u32[]{:S(2)}, u32[]{:S(2)}) collective-permute-start(bf16[64,128]{1,0:T(8,128)(2,1)S(1)} %get-tuple-element.18), channel_id=1, source_target_pairs={{0,2},{1,3},{2,0},{3,1},{4,6},{5,7},{6,4},{7,5},{8,10},{9,11},{10,... | collective-permute-start | bytes 49160 | tf_op jit(solution)/shard_map/ppermute | solution.py:29
  19.6 5.0 %collective-permute-start.2 = (bf16[64,128]{1,0:T(8,128)(2,1)S(1)}, bf16[64,128]{1,0:T(8,128)(2,1)S(1)}, u32[]{:S(2)}, u32[]{:S(2)}) collective-permute-start(bf16[64,128]{1,0:T(8,128)(2,1)S(1)} %get-tuple-element.19), channel_id=1, source_target_pairs={{0,3},{1,0},{2,1},{3,2},{4,7},{5,4},{6,5},{7,6},{8,11},{9,8},{10,9... | collective-permute-start | bytes 49160 | tf_op jit(solution)/shard_map/ppermute | solution.py:29
  20.7 4.1 %copy-start = (bf16[128,8192]{1,0:T(8,128)(2,1)S(1)}, bf16[128,8192]{1,0:T(8,128)(2,1)}, u32[]{:S(2)}) copy-start(bf16[128,8192]{1,0:T(8,128)(2,1)} %acts.7) | copy-start | bytes 6291460
  25.0 3.1 %collective-permute-start.3 = (bf16[32,64,128]{2,1,0:T(8,128)(2,1)S(1)}, bf16[32,64,128]{2,1,0:T(8,128)(2,1)S(1)}, u32[]{:S(2)}, u32[]{:S(2)}) collective-permute-start(bf16[32,64,128]{2,1,0:T(8,128)(2,1)S(1)} %left.3), channel_id=1, source_target_pairs={{0,4},{4,0},{1,5},{5,1},{2,6},{6,2},{3,7},{7,3},{8,12},{12,8},{9,1... | collective-permute-start | bytes 1572872 | tf_op jit(solution)/shard_map/ppermute | solution.py:29
  75.4 5.7 %collective-permute-start.4 = (bf16[32,64,128]{2,1,0:T(8,128)(2,1)S(1)}, bf16[32,64,128]{2,1,0:T(8,128)(2,1)S(1)}, u32[]{:S(2)}, u32[]{:S(2)}) collective-permute-start(bf16[32,64,128]{2,1,0:T(8,128)(2,1)S(1)} %bitcast.9), channel_id=1, source_target_pairs={{0,4},{4,0},{1,5},{5,1},{2,6},{6,2},{3,7},{7,3},{8,12},{12,8},{9,1... | collective-permute-start | bytes 1572872 | tf_op jit(solution)/shard_map/ppermute | solution.py:29
  81.6 4.6 %collective-permute-start.5 = (bf16[64,128]{1,0:T(8,128)(2,1)S(1)}, bf16[64,128]{1,0:T(8,128)(2,1)S(1)}, u32[]{:S(2)}, u32[]{:S(2)}) collective-permute-start(bf16[64,128]{1,0:T(8,128)(2,1)S(1)} %add_convert_fusion.1.a0), channel_id=1, source_target_pairs={{0,1},{1,2},{2,3},{3,0},{4,5},{5,6},{6,7},{7,4},{8,9},{9,10},{10,1... | collective-permute-start | bytes 49160 | tf_op jit(solution)/shard_map/ppermute | solution.py:29
  82.1 4.5 %collective-permute-start.6 = (bf16[64,128]{1,0:T(8,128)(2,1)S(1)}, bf16[64,128]{1,0:T(8,128)(2,1)S(1)}, u32[]{:S(2)}, u32[]{:S(2)}) collective-permute-start(bf16[64,128]{1,0:T(8,128)(2,1)S(1)} %add_convert_fusion.1.a0), channel_id=1, source_target_pairs={{0,2},{1,3},{2,0},{3,1},{4,6},{5,7},{6,4},{7,5},{8,10},{9,11},{10,... | collective-permute-start | bytes 49160 | tf_op jit(solution)/shard_map/ppermute | solution.py:29
  83.8 3.5 %collective-permute-start.7 = (bf16[64,128]{1,0:T(8,128)(2,1)S(1)}, bf16[64,128]{1,0:T(8,128)(2,1)S(1)}, u32[]{:S(2)}, u32[]{:S(2)}) collective-permute-start(bf16[64,128]{1,0:T(8,128)(2,1)S(1)} %add_convert_fusion.1.a0), channel_id=1, source_target_pairs={{0,3},{1,0},{2,1},{3,2},{4,7},{5,4},{6,5},{7,6},{8,11},{9,8},{10,9... | collective-permute-start | bytes 49160 | tf_op jit(solution)/shard_map/ppermute | solution.py:29
  87.5 2.6 %collective-permute-start.8 = (f32[64,256]{1,0:T(8,128)S(1)}, f32[64,256]{1,0:T(8,128)S(1)}, u32[]{:S(2)}, u32[]{:S(2)}) collective-permute-start(f32[64,256]{1,0:T(8,128)S(1)} %right.1), channel_id=1, source_target_pairs={{0,4},{4,0},{1,5},{5,1},{2,6},{6,2},{3,7},{7,3},{8,12},{12,8},{9,1... | collective-permute-start | bytes 196616 | tf_op jit(solution)/shard_map/ppermute | solution.py:29
  90.2 4.8 %collective-permute-start.9 = (f32[64,256]{1,0:T(8,128)S(1)}, f32[64,256]{1,0:T(8,128)S(1)}, u32[]{:S(2)}, u32[]{:S(2)}) collective-permute-start(f32[64,256]{1,0:T(8,128)S(1)} %add.13.a), channel_id=1, source_target_pairs={{0,8},{8,16},{16,24},{24,0},{1,9},{9,17},{17,25},{25,1},{2,10},{10... | collective-permute-start | bytes 196616 | tf_op jit(solution)/shard_map/ppermute | solution.py:29
  90.8 5.4 %collective-permute-start.10 = (f32[64,256]{1,0:T(8,128)S(1)}, f32[64,256]{1,0:T(8,128)S(1)}, u32[]{:S(2)}, u32[]{:S(2)}) collective-permute-start(f32[64,256]{1,0:T(8,128)S(1)} %add.13.a), channel_id=1, source_target_pairs={{0,16},{8,24},{16,0},{24,8},{1,17},{9,25},{17,1},{25,9},{2,18},{10... | collective-permute-start | bytes 196616 | tf_op jit(solution)/shard_map/ppermute | solution.py:29
  93.2 4.2 %collective-permute-start.11 = (f32[64,256]{1,0:T(8,128)S(1)}, f32[64,256]{1,0:T(8,128)S(1)}, u32[]{:S(2)}, u32[]{:S(2)}) collective-permute-start(f32[64,256]{1,0:T(8,128)S(1)} %add.13.a), channel_id=1, source_target_pairs={{0,24},{8,0},{16,8},{24,16},{1,25},{9,1},{17,9},{25,17},{2,26},{10... | collective-permute-start | bytes 196616 | tf_op jit(solution)/shard_map/ppermute | solution.py:29
  98.1 13.6 %all-to-all-start.3 = ((bf16[8,64,256]{2,1,0:T(8,128)(2,1)}), bf16[8,64,256]{2,1,0:T(8,128)(2,1)S(1)}, u32[]{:S(2)}, u32[]{:S(2)}) async-start(bf16[8,64,256]{2,1,0:T(8,128)(2,1)} %pairs.1), calls=%async_computation.4 | async-start | bytes 524288 | tf_op jit(solution)/shard_map/all_to_all | solution.py:286
  111.9 3.2 %copy-start.2 = (f32[64,256]{1,0:T(8,128)}, f32[64,256]{1,0:T(8,128)S(1)}, u32[]{:S(2)}) copy-start(f32[64,256]{1,0:T(8,128)S(1)} %fusion) | copy-start | bytes 196612
Sparse Core Ops, SparseCore 0:
  13.7 98.8 reduce-scatter.1

commit v4 on v3

--- a/solution.py
+++ b/solution.py
@@ -54,24 +54,7 @@
     return lax.optimization_barrier((first, then))
 
 
-def small_body(y, q, kg, q_t, own, s1, s2, s3):
-    qt = q[...].T.astype(BF)
-    q_t[...] = qt
-    for k, out in enumerate((own, s1, s2, s3)):
-        start = pl.multiple_of(lax.rem(y[0] + k, N_Y) * ROWS, ROWS)
-        out[...] = dot(qt, kg[pl.ds(start, ROWS), :], 1, 1).astype(out.dtype)
-
-
-def small(y, q, kg):
-    block = (RANK, ROWS)
-    return kernel(
-        small_body, "small", [IN_SMEM, IN_VMEM, IN_VMEM], [IN_VMEM] * 5,
-        [shape((RANK, COLS), BF), shape(block, F32)] + [shape(block, BF)] * 3,
-        2 * RANK * COLS * ROWS * N_Y, 4 * 10**5,
-    )(y, q, kg)
-
-
-def partial_body(kg, w, out, kg_in, w_in, held, sem_kg, sem_w, sem_out):
+def partial_body(y, q, kg, w, out, q_t, own, s1, s2, s3, kg_in, w_in, q_in, held, sem_in, sem_w, sem_out):
     n = D // PARTS
 
     def load(i):
@@ -82,33 +65,43 @@
         cols = pl.ds(i * n, n)
         return pltpu.make_async_copy(held.at[:, cols], out.at[:, cols], sem_out.at[i])
 
-    first = pltpu.make_async_copy(kg, kg_in, sem_kg)
-    first.start()
+    kg_copy = pltpu.make_async_copy(kg, kg_in, sem_in.at[0])
+    q_copy = pltpu.make_async_copy(q, q_in, sem_in.at[1])
+    kg_copy.start()
     for i in range(PARTS):
         load(i).start()
-    first.wait()
+    q_copy.start()
+    kg_copy.wait()
     for i in range(PARTS):
         load(i).wait()
-        for j in range(n // SPAN):
-            cols = slice(i * n + j * SPAN, i * n + (j + 1) * SPAN)
-            held[:, cols] = dot(kg_in[...], w_in[cols, :], 1, 1).astype(BF)
+        cols = slice(i * n, (i + 1) * n)
+        held[:, cols] = dot(kg_in[...], w_in[cols, :], 1, 1).astype(BF)
         store(i).start()
+    q_copy.wait()
+    qt = q_in[...].astype(BF)
+    q_t[...] = qt
+    for k, block in enumerate((own, s1, s2, s3)):
+        start = pl.multiple_of(lax.rem(y[0] + k, N_Y) * ROWS, ROWS)
+        block[...] = dot(qt, kg_in[pl.ds(start, ROWS), :], 1, 1).astype(block.dtype)
     for i in range(PARTS):
         store(i).wait()
 
 
-def partial_grad(kg, w):
+def partial_grad(y, q, kg, w):
     n = kg.shape[0]
     dma = pltpu.SemaphoreType.DMA
-    return kernel(
-        partial_body, "partial", [IN_HBM, IN_HBM], IN_HBM, pltpu.HBM((n, D), BF),
+    block = (RANK, ROWS)
+    return kernel(
+        partial_body, "partial", [IN_SMEM] + [IN_HBM] * 3, [IN_HBM] + [IN_VMEM] * 5,
+        [pltpu.HBM((n, D), BF), pltpu.VMEM((RANK, COLS), BF), pltpu.VMEM(block, F32)]
+        + [pltpu.VMEM(block, BF)] * 3,
         2 * n * COLS * D, 2 * D * (COLS + n),
         [
-            pltpu.VMEM((n, COLS), BF), pltpu.VMEM((D, COLS), BF), pltpu.VMEM((n, D), BF),
-            dma(()), dma((PARTS,)), dma((PARTS,)),
+            pltpu.VMEM((n, COLS), BF), pltpu.VMEM((D, COLS), BF), pltpu.VMEM((RANK, COLS), F32),
+            pltpu.VMEM((n, D), BF), dma((2,)), dma((PARTS,)), dma((PARTS,)),
         ],
         24,
-    )(*(pltpu.with_memory_space_constraint(v, pltpu.HBM) for v in (kg, w)))
+    )(y, *(pltpu.with_memory_space_constraint(v, pltpu.HBM) for v in (q, kg, w)))
 
 
 def error_body(q, err, pe, eb, held, sem):
@@ -228,25 +221,26 @@
 
 
 def update_body(c, own, other, mix, out, held, sem):
-    def copy(half):
-        span = pl.ds(pl.multiple_of(half * (D // 2), D // 2), D // 2)
-        return pltpu.make_async_copy(held.at[span], out.at[span], sem.at[half])
+    def copy(half, i):
+        span = pl.ds(at(half, i), SPAN)
+        return pltpu.make_async_copy(held.at[span], out.at[span], sem.at[half * STEPS + i])
 
     for half, p in ((c[0], own), (1 - c[0], other)):
         for i in range(STEPS):
             v = rows(p, i)
             v = jnp.concatenate([v, v], axis=0)
             held[pl.ds(at(half, i), SPAN), :] = dot(v, mix[...], 0, 0).astype(BF)
-        copy(half).start()
-    copy(c[0]).wait()
-    copy(1 - c[0]).wait()
+            copy(half, i).start()
+    for half in (c[0], 1 - c[0]):
+        for i in range(STEPS):
+            copy(half, i).wait()
 
 
 def update_from(c, own, other, mix):
     return kernel(
-        update_body, "update", [IN_SMEM] + [IN_VMEM] * 3, IN_HBM, shape((D, COLS), BF),
+        update_body, "update", [IN_SMEM] + [IN_VMEM] * 3, IN_HBM, pltpu.HBM((D, COLS), BF),
         4 * D * RANK * COLS, 2 * D * (RANK + COLS),
-        [pltpu.VMEM((D, COLS), BF), pltpu.SemaphoreType.DMA((2,))], 12,
+        [pltpu.VMEM((D, COLS), BF), pltpu.SemaphoreType.DMA((2 * STEPS,))], 12,
     )(c, own, other, mix)
 
 
@@ -269,7 +263,8 @@
 
 
 def pairs_body(a, b, c, d, out):
-    total = ((a[...] + c[...]) + (b[...] + d[...])).astype(BF)
+    a, b, c, d = (v[...].astype(F32) for v in (a, b, c, d))
+    total = ((a + c) + (b + d)).astype(BF)
     for i in range(out.shape[0]):
         out[i] = total
 
@@ -278,7 +273,7 @@
     v = [v] + [shift(v, axis, 4, k) for k in (1, 2, 3)]
     return kernel(
         pairs_body, "pairs", [IN_VMEM] * 4, IN_VMEM, shape((copies,) + v[0].shape, BF),
-        4 * v[0].size, 2 * v[0].size * (8 + copies),
+        4 * v[0].size, 2 * v[0].size * (4 + copies),
     )(*v)
 
 
@@ -296,10 +291,8 @@
 def local(acts, key_grad, w_key, error_fb, q_prev):
     y = lax.axis_index("y").astype(jnp.int32)[None]
     c = lax.axis_index("c").astype(jnp.int32)[None]
-    part = partial_grad(key_grad, w_key)
+    part, q_t, k0, k1, k2, k3 = partial_grad(y, q_prev.T, key_grad, w_key)
     act_grad = lax.psum_scatter(part, "y", scatter_dimension=0, tiled=True)
-    q_t, k0, k1, k2, k3 = small(y, q_prev, key_grad)
-    k1, q_t = tie(k1, q_t)
     kgq = [k0] + [shift(v, "y", N_Y, k) for k, v in ((1, k1), (2, k2), (3, k3))]
     pe, err = error_side(q_t, error_fb)
 
@@ -315,7 +308,7 @@
     qb = err_side(1 - c, other, err)
     q = right(y, qa, qb, ap, key_grad)
 
-    q = q + shift(q, "c", 2, 1)
+    q = (q + shift(q, "c", 2, 1)).astype(BF)
     q = ring_sum(q, "x", N_Z)
     q, other = tie(q, other)
     q = exchange(q, "z")

time: 123 us -> 121 us (0.984)
  waiting for transfers between devices: 11.6 us -> 10.3 us
    pallas_call x3 -> x2, Pallas kernels: 9.45 us -> 8.48 us  [the longest x1 5.94 us: partial_grad(): kernel(partial_body, 'partial', [IN_SMEM] + [IN_HBM] * 3, [IN_HBM] + [IN_...]
  transfers between devices with their start and end apart: 14 -> 14, of which waited for: 10 -> 10; matrix products, arithmetic and copies ran while one was open for 1% -> 1% of each run, Pallas kernels for 14% -> 13%
where the time goes in v4:
time: 121 us; the launch traced here: 119 us
  blocking collectives  46.9 us (39%)
  starting transfers between devices  24.9 us (21%)
  Pallas kernels  22 us (18%)
  between operations  14.2 us (12%)
  waiting for transfers between devices  10.3 us (9%)
    all_to_all x3, blocking collectives, exchange(): return lax.all_to_all(v, axes, 0, 0, tiled=True)  46.9 us
    ppermute x12, starting transfers between devices, shift(): return lax.ppermute(v, axis, [(i, (i + k) % n) for i in range(n)])  21.4 us
    ppermute x12, waiting for transfers between devices, shift(): return lax.ppermute(v, axis, [(i, (i + k) % n) for i in range(n)])  6.34 us
    pallas_call x1, Pallas kernels, inverse(): kernel(inverse_body, 'inverse', [IN_VMEM, IN_VMEM], IN_VMEM, shape((RANK,...  6.05 us
    pallas_call x1, Pallas kernels, partial_grad(): kernel(partial_body, 'partial', [IN_SMEM] + [IN_HBM] * 3, [IN_HBM] + [IN_...  5.94 us
    pallas_call x1, Pallas kernels, error_side(): kernel(error_body, 'error', [IN_VMEM, IN_HBM], [IN_VMEM, IN_VMEM], [pltpu...  3.91 us
    all_to_all x1, waiting for transfers between devices, exchange(): return lax.all_to_all(v, axes, 0, 0, tiled=True)  3.78 us
    all_to_all x1, starting transfers between devices, exchange(): return lax.all_to_all(v, axes, 0, 0, tiled=True)  3.41 us
  transfers between devices with their start and end apart: 14, of which 10 were waited for; matrix products, arithmetic and copies ran while one was open for 1% of the time, Pallas kernels for 13%

profile of v4, /device:TPU:1, one launch (start us, length us, event | category | flops | bytes accessed | tf_op | source)
XLA Modules:
  0.0 119.1 jit_solution(11303266629778197833)
XLA Ops:
  7.2 0.0 reduce-scatter.2.cloned.1.call-start
  7.2 5.9 %partial.1 = (bf16[512,8192]{1,0:T(8,128)(2,1)}, bf16[64,256]{1,0:T(8,128)(2,1)S(1)}, f32[64,128]{1,0:T(8,128)S(1)}, bf16[64,128]{1,0:T(8,128)(2,1)S(1)}, bf16[6...) custom-call(s32[1]{0:T(128)} %bitcast.y, f32[64,256]{1,0:T(8,128)} %bitcast.17, bf16[512,256]{1,0:T(8,128)(2,1)} %kg.3, ...), custom_call_target="tpu_custom_call" | custom-call | flops 2147483648 | bytes 12582912 | tf_op jit(solution)/shard_map/partial/pallas_call | solution.py:94
  13.2 0.0 reduce-scatter.2.cloned.1.call-update
  13.2 2.2 %collective-permute-start = (bf16[64,128]{1,0:T(8,128)(2,1)S(1)}, bf16[64,128]{1,0:T(8,128)(2,1)S(1)}, u32[]{:S(2)}, u32[]{:S(2)}) collective-permute-start(bf16[64,128]{1,0:T(8,128)(2,1)S(1)} %get-tuple-element.15), channel_id=1, source_target_pairs={{0,1},{1,2},{2,3},{3,0},{4,5},{5,6},{6,7},{7,4},{8,9},{9,10},{10,1... | collective-permute-start | bytes 49160 | tf_op jit(solution)/shard_map/ppermute | solution.py:29
  15.4 2.6 %collective-permute-start.1 = (bf16[64,128]{1,0:T(8,128)(2,1)S(1)}, bf16[64,128]{1,0:T(8,128)(2,1)S(1)}, u32[]{:S(2)}, u32[]{:S(2)}) collective-permute-start(bf16[64,128]{1,0:T(8,128)(2,1)S(1)} %get-tuple-element.16), channel_id=1, source_target_pairs={{0,2},{1,3},{2,0},{3,1},{4,6},{5,7},{6,4},{7,5},{8,10},{9,11},{10,... | collective-permute-start | bytes 49160 | tf_op jit(solution)/shard_map/ppermute | solution.py:29
  18.0 1.1 collective-permute-start.2
  19.1 0.0 copy-start
  19.1 3.9 %error.1 = (f32[64,64,128]{2,1,0:T(8,128)S(1)}, bf16[8192,256]{1,0:T(8,128)(2,1)S(1)}) custom-call(bf16[64,256]{1,0:T(8,128)(2,1)S(1)} %get-tuple-element.18.q, f32[8192,256]{1,0:T(8,128)} %err.1), custom_call_target="tpu_custom_call" | custom-call | flops 268435456 | bytes 14680064 | tf_op jit(solution)/shard_map/error/pallas_call | solution.py:125
  23.0 0.0 collective-permute-done.k1
  23.0 0.0 collective-permute-done.1.k2
  23.0 0.0 collective-permute-done.2.k3
  23.0 0.1 copy-done
  23.1 0.3 left.3
  23.5 1.6 %collective-permute-start.3 = (bf16[32,64,128]{2,1,0:T(8,128)(2,1)S(1)}, bf16[32,64,128]{2,1,0:T(8,128)(2,1)S(1)}, u32[]{:S(2)}, u32[]{:S(2)}) collective-permute-start(bf16[32,64,128]{2,1,0:T(8,128)(2,1)S(1)} %left.3), channel_id=1, source_target_pairs={{0,4},{4,0},{1,5},{5,1},{2,6},{6,2},{3,7},{7,3},{8,12},{12,8},{9,1... | collective-permute-start | bytes 1572872 | tf_op jit(solution)/shard_map/ppermute | solution.py:29
  25.1 0.3 left.2
  25.4 1.2 %collective-permute-done.3 = bf16[32,64,128]{2,1,0:T(8,128)(2,1)S(1)} collective-permute-done((bf16[32,64,128]{2,1,0:T(8,128)(2,1)S(1)}, bf16[32,64,128]{2,1,0:T(8,128)(2,1)S(1)}, u32[]{:S(2)}, u32[]{:S(2)}) %collective-permute-start.3) | collective-permute-done | bytes 524320 | tf_op jit(solution)/shard_map/ppermute | solution.py:29
  26.6 0.1 add_convert_fusion
  26.7 14.6 %all_to_all.20 = bf16[32,64,128]{2,1,0:T(8,128)(2,1)S(1)} all-to-all(bf16[32,64,128]{2,1,0:T(8,128)(2,1)S(1)} %add_convert_fusion), channel_id=1, replica_groups=mesh['z'=8,'x'=4,'c'=2,'y'=4] {'x','y'}, dimensions={0} | all-to-all | bytes 1048576 | tf_op jit(solution)/shard_map/all_to_all | solution.py:281
  41.4 0.1 merge.2
  41.4 17.4 %all_to_all.21.v = bf16[8,2,64,128]{3,2,1,0:T(8,128)(2,1)S(1)} all-to-all(bf16[8,2,64,128]{3,2,1,0:T(8,128)(2,1)S(1)} %merge.2), channel_id=1, replica_groups=mesh['z'=8,'x'=4,'c'=2,'y'=4] {'z'}, dimensions={0} | all-to-all | bytes 524288 | tf_op jit(solution)/shard_map/all_to_all | solution.py:281
  58.9 0.1 merge.3
  58.9 14.9 %all_to_all.22 = bf16[16,2,64,128]{3,2,1,0:T(8,128)(2,1)S(1)} all-to-all(bf16[16,2,64,128]{3,2,1,0:T(8,128)(2,1)S(1)} %merge.3), channel_id=1, replica_groups=mesh['z'=8,'x'=4,'c'=2,'y'=4] {'x','y'}, dimensions={0} | all-to-all | bytes 1048576 | tf_op jit(solution)/shard_map/all_to_all | solution.py:281
  73.8 4.2 %collective-permute-start.4 = (bf16[32,64,128]{2,1,0:T(8,128)(2,1)S(1)}, bf16[32,64,128]{2,1,0:T(8,128)(2,1)S(1)}, u32[]{:S(2)}, u32[]{:S(2)}) collective-permute-start(bf16[32,64,128]{2,1,0:T(8,128)(2,1)S(1)} %bitcast.10), channel_id=1, source_target_pairs={{0,4},{4,0},{1,5},{5,1},{2,6},{6,2},{3,7},{7,3},{8,12},{12,8},{9,1... | collective-permute-start | bytes 1572872 | tf_op jit(solution)/shard_map/ppermute | solution.py:29
  78.0 0.5 acts_p.2
  78.5 1.1 collective-permute-done.4.p.other
  79.6 0.5 acts_p.3
  80.1 0.5 collective-permute-start.5
  80.5 1.9 %collective-permute-start.6 = (bf16[64,128]{1,0:T(8,128)(2,1)S(1)}, bf16[64,128]{1,0:T(8,128)(2,1)S(1)}, u32[]{:S(2)}, u32[]{:S(2)}) collective-permute-start(bf16[64,128]{1,0:T(8,128)(2,1)S(1)} %add_convert_fusion.2.a0), channel_id=1, source_target_pairs={{0,2},{1,3},{2,0},{3,1},{4,6},{5,7},{6,4},{7,5},{8,10},{9,11},{10,... | collective-permute-start | bytes 49160 | tf_op jit(solution)/shard_map/ppermute | solution.py:29
  82.4 1.4 %collective-permute-start.7 = (bf16[64,128]{1,0:T(8,128)(2,1)S(1)}, bf16[64,128]{1,0:T(8,128)(2,1)S(1)}, u32[]{:S(2)}, u32[]{:S(2)}) collective-permute-start(bf16[64,128]{1,0:T(8,128)(2,1)S(1)} %add_convert_fusion.2.a0), channel_id=1, source_target_pairs={{0,3},{1,0},{2,1},{3,2},{4,7},{5,4},{6,5},{7,6},{8,11},{9,8},{10,9... | collective-permute-start | bytes 49160 | tf_op jit(solution)/shard_map/ppermute | solution.py:29
  83.7 0.0 copy-start.1
  83.8 0.5 err_p.2.qa
  84.2 0.5 err_p.3.qb
  84.7 0.0 collective-permute-done.5.a1
  84.7 0.3 collective-permute-done.6.a2
  85.0 0.7 collective-permute-done.7.a3
  85.8 0.0 copy-done.1
  85.8 0.2 right.1
  85.9 1.7 %collective-permute-start.8 = (f32[64,256]{1,0:T(8,128)S(1)}, f32[64,256]{1,0:T(8,128)S(1)}, u32[]{:S(2)}, u32[]{:S(2)}) collective-permute-start(f32[64,256]{1,0:T(8,128)S(1)} %right.1), channel_id=1, source_target_pairs={{0,4},{4,0},{1,5},{5,1},{2,6},{6,2},{3,7},{7,3},{8,12},{12,8},{9,1... | collective-permute-start | bytes 196616 | tf_op jit(solution)/shard_map/ppermute | solution.py:29
  87.6 0.9 collective-permute-done.8
  88.5 0.8 collective-permute-start.9
  89.3 2.4 %collective-permute-start.10 = (bf16[64,256]{1,0:T(8,128)(2,1)S(1)}, bf16[64,256]{1,0:T(8,128)(2,1)S(1)}, u32[]{:S(2)}, u32[]{:S(2)}) collective-permute-start(bf16[64,256]{1,0:T(8,128)(2,1)S(1)} %add_convert_fusion.1.a), channel_id=1, source_target_pairs={{0,16},{8,24},{16,0},{24,8},{1,17},{9,25},{17,1},{25,9},{2,18},{10... | collective-permute-start | bytes 98312 | tf_op jit(solution)/shard_map/ppermute | solution.py:29
  91.7 1.2 collective-permute-start.11
  92.9 0.1 collective-permute-done.9.b
  93.0 0.7 collective-permute-done.10.c
  93.7 1.3 %collective-permute-done.11.d = bf16[64,256]{1,0:T(8,128)(2,1)S(1)} collective-permute-done((bf16[64,256]{1,0:T(8,128)(2,1)S(1)}, bf16[64,256]{1,0:T(8,128)(2,1)S(1)}, u32[]{:S(2)}, u32[]{:S(2)}) %collective-permute-start.11) | collective-permute-done | bytes 32800 | tf_op jit(solution)/shard_map/ppermute | solution.py:29
  95.0 0.7 pairs.1
  95.7 3.4 %all-to-all-start.3 = ((bf16[8,64,256]{2,1,0:T(8,128)(2,1)}), bf16[8,64,256]{2,1,0:T(8,128)(2,1)S(1)}, u32[]{:S(2)}, u32[]{:S(2)}) async-start(bf16[8,64,256]{2,1,0:T(8,128)(2,1)} %pairs.1), calls=%async_computation.4 | async-start | bytes 524288 | tf_op jit(solution)/shard_map/all_to_all | solution.py:281
  99.2 6.1 %inverse.1 = f32[64,64]{1,0:T(8,128)S(1)} custom-call(bf16[32,64,128]{2,1,0:T(8,128)(2,1)S(1)} %bitcast.13, bf16[32,64,128]{2,1,0:T(8,128)(2,1)S(1)} %collective-permute-done.4.p.other), custom_call_target="tpu_custom_call" | custom-call | flops 67108864 | bytes 2097152 | tf_op jit(solution)/shard_map/inverse/pallas_call | solution.py:217
  105.2 3.8 %all-to-all-done.3 = bf16[8,64,256]{2,1,0:T(8,128)(2,1)S(1)} async-done(((bf16[8,64,256]{2,1,0:T(8,128)(2,1)}), bf16[8,64,256]{2,1,0:T(8,128)(2,1)S(1)}, u32[]{:S(2)}, u32[]{:S(2)}) %all-to-all-start.3) | async-done | bytes 262176 | tf_op jit(solution)/shard_map/all_to_all | solution.py:281
  109.0 0.2 fusion
  109.2 0.0 copy-start.2
  109.3 0.3 subtract_convert_fusion
  109.5 2.5 %update.1 = bf16[8192,256]{1,0:T(8,128)(2,1)} custom-call(s32[1]{0:T(128)} %bitcast.2.h.c, bf16[32,64,128]{2,1,0:T(8,128)(2,1)S(1)} %bitcast.14, bf16[32,64,128]{2,1,0:T(8,128)(2,1)S(1)} %collective-permute-done.4.p.other, bf16[128,256]{1,0:T(8,128)(2,1)S(1)} %pad_maximum_fusion.mix), custom_call_target="tpu_custom_call" | custom-call | flops 536870912 | bytes 5242880 | tf_op jit(solution)/shard_map/update/pallas_call | solution.py:240
  112.1 0.2 reduce-scatter.2.cloned.1.call-done
  112.2 0.0 copy-done.2
  (4 shorter events, 0.1 us)
Async XLA Ops:
  7.2 105.1 %reduce-scatter.2.cloned.1.call-start = ((), (), s32[]{:S(2)}) async-start(), calls=%async_computation.5 | async-start | bytes 10485760 | tf_op jit(solution)/shard_map/reduce_scatter | solution.py:295
  13.2 9.8 %collective-permute-start = (bf16[64,128]{1,0:T(8,128)(2,1)S(1)}, bf16[64,128]{1,0:T(8,128)(2,1)S(1)}, u32[]{:S(2)}, u32[]{:S(2)}) collective-permute-start(bf16[64,128]{1,0:T(8,128)(2,1)S(1)} %get-tuple-element.15), channel_id=1, source_target_pairs={{0,1},{1,2},{2,3},{3,0},{4,5},{5,6},{6,7},{7,4},{8,9},{9,10},{10,1... | collective-permute-start | bytes 49160 | tf_op jit(solution)/shard_map/ppermute | solution.py:29
  15.4 7.6 %collective-permute-start.1 = (bf16[64,128]{1,0:T(8,128)(2,1)S(1)}, bf16[64,128]{1,0:T(8,128)(2,1)S(1)}, u32[]{:S(2)}, u32[]{:S(2)}) collective-permute-start(bf16[64,128]{1,0:T(8,128)(2,1)S(1)} %get-tuple-element.16), channel_id=1, source_target_pairs={{0,2},{1,3},{2,0},{3,1},{4,6},{5,7},{6,4},{7,5},{8,10},{9,11},{10,... | collective-permute-start | bytes 49160 | tf_op jit(solution)/shard_map/ppermute | solution.py:29
  18.0 5.0 %collective-permute-start.2 = (bf16[64,128]{1,0:T(8,128)(2,1)S(1)}, bf16[64,128]{1,0:T(8,128)(2,1)S(1)}, u32[]{:S(2)}, u32[]{:S(2)}) collective-permute-start(bf16[64,128]{1,0:T(8,128)(2,1)S(1)} %get-tuple-element.17), channel_id=1, source_target_pairs={{0,3},{1,0},{2,1},{3,2},{4,7},{5,4},{6,5},{7,6},{8,11},{9,8},{10,9... | collective-permute-start | bytes 49160 | tf_op jit(solution)/shard_map/ppermute | solution.py:29
  19.1 4.1 %copy-start = (bf16[128,8192]{1,0:T(8,128)(2,1)S(1)}, bf16[128,8192]{1,0:T(8,128)(2,1)}, u32[]{:S(2)}) copy-start(bf16[128,8192]{1,0:T(8,128)(2,1)} %acts.7) | copy-start | bytes 6291460
  23.5 3.1 %collective-permute-start.3 = (bf16[32,64,128]{2,1,0:T(8,128)(2,1)S(1)}, bf16[32,64,128]{2,1,0:T(8,128)(2,1)S(1)}, u32[]{:S(2)}, u32[]{:S(2)}) collective-permute-start(bf16[32,64,128]{2,1,0:T(8,128)(2,1)S(1)} %left.3), channel_id=1, source_target_pairs={{0,4},{4,0},{1,5},{5,1},{2,6},{6,2},{3,7},{7,3},{8,12},{12,8},{9,1... | collective-permute-start | bytes 1572872 | tf_op jit(solution)/shard_map/ppermute | solution.py:29
  73.8 5.7 %collective-permute-start.4 = (bf16[32,64,128]{2,1,0:T(8,128)(2,1)S(1)}, bf16[32,64,128]{2,1,0:T(8,128)(2,1)S(1)}, u32[]{:S(2)}, u32[]{:S(2)}) collective-permute-start(bf16[32,64,128]{2,1,0:T(8,128)(2,1)S(1)} %bitcast.10), channel_id=1, source_target_pairs={{0,4},{4,0},{1,5},{5,1},{2,6},{6,2},{3,7},{7,3},{8,12},{12,8},{9,1... | collective-permute-start | bytes 1572872 | tf_op jit(solution)/shard_map/ppermute | solution.py:29
  80.1 4.7 %collective-permute-start.5 = (bf16[64,128]{1,0:T(8,128)(2,1)S(1)}, bf16[64,128]{1,0:T(8,128)(2,1)S(1)}, u32[]{:S(2)}, u32[]{:S(2)}) collective-permute-start(bf16[64,128]{1,0:T(8,128)(2,1)S(1)} %add_convert_fusion.2.a0), channel_id=1, source_target_pairs={{0,1},{1,2},{2,3},{3,0},{4,5},{5,6},{6,7},{7,4},{8,9},{9,10},{10,1... | collective-permute-start | bytes 49160 | tf_op jit(solution)/shard_map/ppermute | solution.py:29
  80.5 4.5 %collective-permute-start.6 = (bf16[64,128]{1,0:T(8,128)(2,1)S(1)}, bf16[64,128]{1,0:T(8,128)(2,1)S(1)}, u32[]{:S(2)}, u32[]{:S(2)}) collective-permute-start(bf16[64,128]{1,0:T(8,128)(2,1)S(1)} %add_convert_fusion.2.a0), channel_id=1, source_target_pairs={{0,2},{1,3},{2,0},{3,1},{4,6},{5,7},{6,4},{7,5},{8,10},{9,11},{10,... | collective-permute-start | bytes 49160 | tf_op jit(solution)/shard_map/ppermute | solution.py:29
  82.4 3.4 %collective-permute-start.7 = (bf16[64,128]{1,0:T(8,128)(2,1)S(1)}, bf16[64,128]{1,0:T(8,128)(2,1)S(1)}, u32[]{:S(2)}, u32[]{:S(2)}) collective-permute-start(bf16[64,128]{1,0:T(8,128)(2,1)S(1)} %add_convert_fusion.2.a0), channel_id=1, source_target_pairs={{0,3},{1,0},{2,1},{3,2},{4,7},{5,4},{6,5},{7,6},{8,11},{9,8},{10,9... | collective-permute-start | bytes 49160 | tf_op jit(solution)/shard_map/ppermute | solution.py:29
  83.7 2.0 %copy-start.1 = (bf16[512,256]{1,0:T(8,128)(2,1)S(1)}, bf16[512,256]{1,0:T(8,128)(2,1)}, u32[]{:S(2)}) copy-start(bf16[512,256]{1,0:T(8,128)(2,1)} %kg.3) | copy-start | bytes 786436
  85.9 2.6 %collective-permute-start.8 = (f32[64,256]{1,0:T(8,128)S(1)}, f32[64,256]{1,0:T(8,128)S(1)}, u32[]{:S(2)}, u32[]{:S(2)}) collective-permute-start(f32[64,256]{1,0:T(8,128)S(1)} %right.1), channel_id=1, source_target_pairs={{0,4},{4,0},{1,5},{5,1},{2,6},{6,2},{3,7},{7,3},{8,12},{12,8},{9,1... | collective-permute-start | bytes 196616 | tf_op jit(solution)/shard_map/ppermute | solution.py:29
  88.5 4.5 %collective-permute-start.9 = (bf16[64,256]{1,0:T(8,128)(2,1)S(1)}, bf16[64,256]{1,0:T(8,128)(2,1)S(1)}, u32[]{:S(2)}, u32[]{:S(2)}) collective-permute-start(bf16[64,256]{1,0:T(8,128)(2,1)S(1)} %add_convert_fusion.1.a), channel_id=1, source_target_pairs={{0,8},{8,16},{16,24},{24,0},{1,9},{9,17},{17,25},{25,1},{2,10},{10... | collective-permute-start | bytes 98312 | tf_op jit(solution)/shard_map/ppermute | solution.py:29
  89.3 4.4 %collective-permute-start.10 = (bf16[64,256]{1,0:T(8,128)(2,1)S(1)}, bf16[64,256]{1,0:T(8,128)(2,1)S(1)}, u32[]{:S(2)}, u32[]{:S(2)}) collective-permute-start(bf16[64,256]{1,0:T(8,128)(2,1)S(1)} %add_convert_fusion.1.a), channel_id=1, source_target_pairs={{0,16},{8,24},{16,0},{24,8},{1,17},{9,25},{17,1},{25,9},{2,18},{10... | collective-permute-start | bytes 98312 | tf_op jit(solution)/shard_map/ppermute | solution.py:29
  91.7 3.3 %collective-permute-start.11 = (bf16[64,256]{1,0:T(8,128)(2,1)S(1)}, bf16[64,256]{1,0:T(8,128)(2,1)S(1)}, u32[]{:S(2)}, u32[]{:S(2)}) collective-permute-start(bf16[64,256]{1,0:T(8,128)(2,1)S(1)} %add_convert_fusion.1.a), channel_id=1, source_target_pairs={{0,24},{8,0},{16,8},{24,16},{1,25},{9,1},{17,9},{25,17},{2,26},{10... | collective-permute-start | bytes 98312 | tf_op jit(solution)/shard_map/ppermute | solution.py:29
  95.7 13.3 %all-to-all-start.3 = ((bf16[8,64,256]{2,1,0:T(8,128)(2,1)}), bf16[8,64,256]{2,1,0:T(8,128)(2,1)S(1)}, u32[]{:S(2)}, u32[]{:S(2)}) async-start(bf16[8,64,256]{2,1,0:T(8,128)(2,1)} %pairs.1), calls=%async_computation.4 | async-start | bytes 524288 | tf_op jit(solution)/shard_map/all_to_all | solution.py:281
  109.2 3.0 %copy-start.2 = (f32[64,256]{1,0:T(8,128)}, f32[64,256]{1,0:T(8,128)S(1)}, u32[]{:S(2)}) copy-start(f32[64,256]{1,0:T(8,128)S(1)} %fusion) | copy-start | bytes 196612
Sparse Core Ops, SparseCore 0:
  13.3 98.8 reduce-scatter.1

commit v5 on v4

--- a/solution.py
+++ b/solution.py
@@ -8,6 +8,7 @@
 F32 = jnp.float32
 BF = jnp.bfloat16
 N_Z, N_X, N_C, N_Y = 8, 4, 2, 4
+PAIR = 2
 D, RANK, COLS, ROWS = 8192, 64, 256, 128
 LANES = 128
 CHUNKS = D // LANES
@@ -282,10 +283,10 @@
 
 
 def sum_left(p):
-    n = HALF // 16
-    p = merge(exchange(p, ("x", "y")).reshape(16, n, RANK, LANES), N_Z)
-    p = merge(exchange(p, "z"), 16)
-    return exchange(p, ("x", "y")).reshape(HALF, RANK, LANES)
+    axes = ("x", "zp", "y")
+    p = merge(exchange(p, axes), N_Z // PAIR)
+    p = merge(exchange(p, "zq"), HALF)
+    return exchange(p, axes)
 
 
 def local(acts, key_grad, w_key, error_fb, q_prev):
@@ -311,7 +312,7 @@
     q = (q + shift(q, "c", 2, 1)).astype(BF)
     q = ring_sum(q, "x", N_Z)
     q, other = tie(q, other)
-    q = exchange(q, "z")
+    q = exchange(q, ("zq", "zp"))
     inv = inverse(own, other)
     q = q.astype(F32).sum(0)
     q_new = jnp.dot(inv, q, precision=lax.Precision.HIGHEST)
@@ -323,8 +324,8 @@
 
 
 def solution(mesh):
-    fine = Mesh(mesh.devices.reshape(N_Z, N_X, N_C, N_Y), ("z", "x", "c", "y"))
-    dp = ("z", "x", "c")
+    dp = ("zq", "zp", "x", "c")
+    fine = Mesh(mesh.devices.reshape(N_Z // PAIR, PAIR, N_X, N_C, N_Y), dp + ("y",))
     rows_of = P(dp + ("y",), None)
     return jax.shard_map(
         local,

time: 121 us -> 119 us (0.983); the launches traced: 119 us -> 119 us
  waiting for transfers between devices: 10.3 us -> 13.6 us
  blocking collectives: 46.9 us -> 45 us
  starting transfers between devices: 24.9 us -> 23.5 us
    reduce_scatter x1, waiting for transfers between devices: 0.16 us -> 2.68 us  [local(): act_grad = lax.psum_scatter(part, 'y', scatter_dimension=0, tiled=True)]
    all_to_all x3, blocking collectives: 46.9 us -> 45 us  [exchange(): return lax.all_to_all(v, axes, 0, 0, tiled=True)]
    ppermute x12, starting transfers between devices: 21.4 us -> 20 us  [shift(): return lax.ppermute(v, axis, [(i, (i + k) % n) for i in range(n)])]
where the time goes in v5:
time: 119 us
  blocking collectives  45 us (38%)
  starting transfers between devices  23.5 us (20%)
  Pallas kernels  22 us (18%)
  between operations  14.2 us (12%)
  waiting for transfers between devices  13.6 us (11%)
    all_to_all x3, blocking collectives, exchange(): return lax.all_to_all(v, axes, 0, 0, tiled=True)  45 us
    ppermute x12, starting transfers between devices, shift(): return lax.ppermute(v, axis, [(i, (i + k) % n) for i in range(n)])  20 us
    ppermute x12, waiting for transfers between devices, shift(): return lax.ppermute(v, axis, [(i, (i + k) % n) for i in range(n)])  6.85 us
    pallas_call x1, Pallas kernels, inverse(): kernel(inverse_body, 'inverse', [IN_VMEM, IN_VMEM], IN_VMEM, shape((RANK,...  6.05 us
    pallas_call x1, Pallas kernels, partial_grad(): kernel(partial_body, 'partial', [IN_SMEM] + [IN_HBM] * 3, [IN_HBM] + [IN_...  5.94 us
    all_to_all x1, waiting for transfers between devices, exchange(): return lax.all_to_all(v, axes, 0, 0, tiled=True)  4.05 us
    pallas_call x1, Pallas kernels, error_side(): kernel(error_body, 'error', [IN_VMEM, IN_HBM], [IN_VMEM, IN_VMEM], [pltpu...  3.91 us
    all_to_all x1, starting transfers between devices, exchange(): return lax.all_to_all(v, axes, 0, 0, tiled=True)  3.41 us
  transfers between devices with their start and end apart: 14, of which 10 were waited for; matrix products, arithmetic and copies ran while one was open for 1% of the time, Pallas kernels for 13%

profile of v5, /device:TPU:1, one launch (start us, length us, event | category | flops | bytes accessed | tf_op | source)
XLA Modules:
  0.0 119.1 jit_solution(2838712050415947928)
XLA Ops:
  7.2 0.0 reduce-scatter.2.cloned.1.call-start
  7.2 5.9 %partial.1 = (bf16[512,8192]{1,0:T(8,128)(2,1)}, bf16[64,256]{1,0:T(8,128)(2,1)S(1)}, f32[64,128]{1,0:T(8,128)S(1)}, bf16[64,128]{1,0:T(8,128)(2,1)S(1)}, bf16[6...) custom-call(s32[1]{0:T(128)} %bitcast.y, f32[64,256]{1,0:T(8,128)} %bitcast.9, bf16[512,256]{1,0:T(8,128)(2,1)} %kg.3, ...), custom_call_target="tpu_custom_call" | custom-call | flops 2147483648 | bytes 12582912 | tf_op jit(solution)/shard_map/partial/pallas_call | solution.py:95
  13.2 0.0 reduce-scatter.2.cloned.1.call-update
  13.2 2.2 %collective-permute-start = (bf16[64,128]{1,0:T(8,128)(2,1)S(1)}, bf16[64,128]{1,0:T(8,128)(2,1)S(1)}, u32[]{:S(2)}, u32[]{:S(2)}) collective-permute-start(bf16[64,128]{1,0:T(8,128)(2,1)S(1)} %get-tuple-element.15), channel_id=1, source_target_pairs={{0,1},{1,2},{2,3},{3,0},{4,5},{5,6},{6,7},{7,4},{8,9},{9,10},{10,1... | collective-permute-start | bytes 49160 | tf_op jit(solution)/shard_map/ppermute | solution.py:30
  15.4 2.6 %collective-permute-start.1 = (bf16[64,128]{1,0:T(8,128)(2,1)S(1)}, bf16[64,128]{1,0:T(8,128)(2,1)S(1)}, u32[]{:S(2)}, u32[]{:S(2)}) collective-permute-start(bf16[64,128]{1,0:T(8,128)(2,1)S(1)} %get-tuple-element.16), channel_id=1, source_target_pairs={{0,2},{1,3},{2,0},{3,1},{4,6},{5,7},{6,4},{7,5},{8,10},{9,11},{10,... | collective-permute-start | bytes 49160 | tf_op jit(solution)/shard_map/ppermute | solution.py:30
  18.0 1.1 collective-permute-start.2
  19.1 0.0 copy-start
  19.1 3.9 %error.1 = (f32[64,64,128]{2,1,0:T(8,128)S(1)}, bf16[8192,256]{1,0:T(8,128)(2,1)S(1)}) custom-call(bf16[64,256]{1,0:T(8,128)(2,1)S(1)} %get-tuple-element.18.q, f32[8192,256]{1,0:T(8,128)} %err.1), custom_call_target="tpu_custom_call" | custom-call | flops 268435456 | bytes 14680064 | tf_op jit(solution)/shard_map/error/pallas_call | solution.py:126
  23.0 0.0 collective-permute-done.k1
  23.0 0.0 collective-permute-done.1.k2
  23.0 0.0 collective-permute-done.2.k3
  23.0 0.1 copy-done
  23.1 0.3 left.3
  23.5 1.6 %collective-permute-start.3 = (bf16[32,64,128]{2,1,0:T(8,128)(2,1)S(1)}, bf16[32,64,128]{2,1,0:T(8,128)(2,1)S(1)}, u32[]{:S(2)}, u32[]{:S(2)}) collective-permute-start(bf16[32,64,128]{2,1,0:T(8,128)(2,1)S(1)} %left.3), channel_id=1, source_target_pairs={{0,4},{4,0},{1,5},{5,1},{2,6},{6,2},{3,7},{7,3},{8,12},{12,8},{9,1... | collective-permute-start | bytes 1572872 | tf_op jit(solution)/shard_map/ppermute | solution.py:30
  25.1 0.3 left.2
  25.4 1.2 %collective-permute-done.3 = bf16[32,64,128]{2,1,0:T(8,128)(2,1)S(1)} collective-permute-done((bf16[32,64,128]{2,1,0:T(8,128)(2,1)S(1)}, bf16[32,64,128]{2,1,0:T(8,128)(2,1)S(1)}, u32[]{:S(2)}, u32[]{:S(2)}) %collective-permute-start.3) | collective-permute-done | bytes 524320 | tf_op jit(solution)/shard_map/ppermute | solution.py:30
  26.6 0.1 add_convert_fusion
  26.7 16.0 %all_to_all.20.v = bf16[32,64,128]{2,1,0:T(8,128)(2,1)S(1)} all-to-all(bf16[32,64,128]{2,1,0:T(8,128)(2,1)S(1)} %add_convert_fusion), channel_id=1, replica_groups=mesh['zq'=4,'zp'=2,'x'=4,'c'=2,'y'=4] {'x','zp','y'}, dimensions={0} | all-to-all | bytes 1048576 | tf_op jit(solution)/shard_map/all_to_all | solution.py:282
  42.8 0.1 merge.2
  42.9 14.1 %all_to_all.21.v = bf16[4,64,128]{2,1,0:T(8,128)(2,1)S(1)} all-to-all(bf16[4,64,128]{2,1,0:T(8,128)(2,1)S(1)} %merge.2), channel_id=1, replica_groups=mesh['zq'=4,'zp'=2,'x'=4,'c'=2,'y'=4] {'zq'}, dimensions={0} | all-to-all | bytes 131072 | tf_op jit(solution)/shard_map/all_to_all | solution.py:282
  57.0 0.1 merge.3
  57.1 14.8 %all_to_all.22.p.own = bf16[32,64,128]{2,1,0:T(8,128)(2,1)S(1)} all-to-all(bf16[32,64,128]{2,1,0:T(8,128)(2,1)S(1)} %merge.3), channel_id=1, replica_groups=mesh['zq'=4,'zp'=2,'x'=4,'c'=2,'y'=4] {'x','zp','y'}, dimensions={0} | all-to-all | bytes 1048576 | tf_op jit(solution)/shard_map/all_to_all | solution.py:282
  71.9 3.5 %collective-permute-start.4 = (bf16[32,64,128]{2,1,0:T(8,128)(2,1)S(1)}, bf16[32,64,128]{2,1,0:T(8,128)(2,1)S(1)}, u32[]{:S(2)}, u32[]{:S(2)}) collective-permute-start(bf16[32,64,128]{2,1,0:T(8,128)(2,1)S(1)} %all_to_all.22.p.own), channel_id=1, source_target_pairs={{0,4},{4,0},{1,5},{5,1},{2,6},{6,2},{3,7},{7,3},{8,12},{12,8},{9,1... | collective-permute-start | bytes 1572872 | tf_op jit(solution)/shard_map/ppermute | solution.py:30
  75.4 0.5 acts_p.2
  75.9 1.1 collective-permute-done.4.p.other
  76.9 0.5 acts_p.3
  77.4 0.7 collective-permute-start.5
  78.2 1.2 collective-permute-start.6
  79.4 1.8 %collective-permute-start.7 = (bf16[64,128]{1,0:T(8,128)(2,1)S(1)}, bf16[64,128]{1,0:T(8,128)(2,1)S(1)}, u32[]{:S(2)}, u32[]{:S(2)}) collective-permute-start(bf16[64,128]{1,0:T(8,128)(2,1)S(1)} %add_convert_fusion.2.a0), channel_id=1, source_target_pairs={{0,3},{1,0},{2,1},{3,2},{4,7},{5,4},{6,5},{7,6},{8,11},{9,8},{10,9... | collective-permute-start | bytes 49160 | tf_op jit(solution)/shard_map/ppermute | solution.py:30
  81.2 0.0 copy-start.1
  81.2 0.5 err_p.2.qa
  81.6 0.5 err_p.3.qb
  82.1 0.0 collective-permute-done.5.a1
  82.1 0.5 collective-permute-done.6.a2
  82.7 0.5 collective-permute-done.7.a3
  83.2 0.0 copy-done.1
  83.2 0.2 right.1
  83.3 1.5 %collective-permute-start.8 = (f32[64,256]{1,0:T(8,128)S(1)}, f32[64,256]{1,0:T(8,128)S(1)}, u32[]{:S(2)}, u32[]{:S(2)}) collective-permute-start(f32[64,256]{1,0:T(8,128)S(1)} %right.1), channel_id=1, source_target_pairs={{0,4},{4,0},{1,5},{5,1},{2,6},{6,2},{3,7},{7,3},{8,12},{12,8},{9,1... | collective-permute-start | bytes 196616 | tf_op jit(solution)/shard_map/ppermute | solution.py:30
  84.8 0.9 collective-permute-done.8
  85.7 0.3 collective-permute-start.9
  86.0 2.8 %collective-permute-start.10 = (bf16[64,256]{1,0:T(8,128)(2,1)S(1)}, bf16[64,256]{1,0:T(8,128)(2,1)S(1)}, u32[]{:S(2)}, u32[]{:S(2)}) collective-permute-start(bf16[64,256]{1,0:T(8,128)(2,1)S(1)} %add_convert_fusion.1.a), channel_id=1, source_target_pairs={{0,16},{8,24},{16,0},{24,8},{1,17},{9,25},{17,1},{25,9},{2,18},{10... | collective-permute-start | bytes 98312 | tf_op jit(solution)/shard_map/ppermute | solution.py:30
  88.9 0.7 collective-permute-start.11
  89.6 0.6 collective-permute-done.9.b
  90.2 0.4 collective-permute-done.10.c
  90.5 1.7 %collective-permute-done.11.d = bf16[64,256]{1,0:T(8,128)(2,1)S(1)} collective-permute-done((bf16[64,256]{1,0:T(8,128)(2,1)S(1)}, bf16[64,256]{1,0:T(8,128)(2,1)S(1)}, u32[]{:S(2)}, u32[]{:S(2)}) %collective-permute-start.11) | collective-permute-done | bytes 32800 | tf_op jit(solution)/shard_map/ppermute | solution.py:30
  92.2 0.7 pairs.1
  92.9 3.4 %all-to-all-start.3 = ((bf16[8,64,256]{2,1,0:T(8,128)(2,1)}), bf16[8,64,256]{2,1,0:T(8,128)(2,1)S(1)}, u32[]{:S(2)}, u32[]{:S(2)}) async-start(bf16[8,64,256]{2,1,0:T(8,128)(2,1)} %pairs.1), calls=%async_computation.4 | async-start | bytes 524288 | tf_op jit(solution)/shard_map/all_to_all | solution.py:282
  96.4 6.0 %inverse.1 = f32[64,64]{1,0:T(8,128)S(1)} custom-call(bf16[32,64,128]{2,1,0:T(8,128)(2,1)S(1)} %all_to_all.22.p.own, bf16[32,64,128]{2,1,0:T(8,128)(2,1)S(1)} %collective-permute-done.4.p.other), custom_call_target="tpu_custom_call" | custom-call | flops 67108864 | bytes 2097152 | tf_op jit(solution)/shard_map/inverse/pallas_call | solution.py:218
  102.4 4.1 %all-to-all-done.3 = bf16[8,64,256]{2,1,0:T(8,128)(2,1)S(1)} async-done(((bf16[8,64,256]{2,1,0:T(8,128)(2,1)}), bf16[8,64,256]{2,1,0:T(8,128)(2,1)S(1)}, u32[]{:S(2)}, u32[]{:S(2)}) %all-to-all-start.3) | async-done | bytes 262176 | tf_op jit(solution)/shard_map/all_to_all | solution.py:282
  106.5 0.2 fusion
  106.7 0.0 copy-start.2
  106.7 0.3 subtract_convert_fusion
  107.0 2.5 %update.1 = bf16[8192,256]{1,0:T(8,128)(2,1)} custom-call(s32[1]{0:T(128)} %bitcast.2.h.c, bf16[32,64,128]{2,1,0:T(8,128)(2,1)S(1)} %all_to_all.22.p.own, bf16[32,64,128]{2,1,0:T(8,128)(2,1)S(1)} %collective-permute-done.4.p.other, bf16[128,256]{1,0:T(8,128)(2,1)S(1)} %pad_maximum_fusion.mix), custom_call_target="tpu_custom_call" | custom-call | flops 536870912 | bytes 5242880 | tf_op jit(solution)/shard_map/update/pallas_call | solution.py:241
  109.5 2.7 %reduce-scatter.2.cloned.1.call-done = bf16[128,8192]{1,0:T(8,128)(2,1)} async-done(((bf16[512,8192]{1,0:T(8,128)(2,1)}), bf16[128,8192]{1,0:T(8,128)(2,1)}) %reduce-scatter.2.cloned.1.call-update) | async-done | bytes 2097168 | tf_op jit(solution)/shard_map/reduce_scatter | solution.py:296
  112.2 0.0 copy-done.2
  (4 shorter events, 0.1 us)
Async XLA Ops:
  7.2 105.1 %reduce-scatter.2.cloned.1.call-start = ((), (), s32[]{:S(2)}) async-start(), calls=%async_computation.5 | async-start | bytes 10485760 | tf_op jit(solution)/shard_map/reduce_scatter | solution.py:296
  13.2 9.8 %collective-permute-start = (bf16[64,128]{1,0:T(8,128)(2,1)S(1)}, bf16[64,128]{1,0:T(8,128)(2,1)S(1)}, u32[]{:S(2)}, u32[]{:S(2)}) collective-permute-start(bf16[64,128]{1,0:T(8,128)(2,1)S(1)} %get-tuple-element.15), channel_id=1, source_target_pairs={{0,1},{1,2},{2,3},{3,0},{4,5},{5,6},{6,7},{7,4},{8,9},{9,10},{10,1... | collective-permute-start | bytes 49160 | tf_op jit(solution)/shard_map/ppermute | solution.py:30
  15.4 7.6 %collective-permute-start.1 = (bf16[64,128]{1,0:T(8,128)(2,1)S(1)}, bf16[64,128]{1,0:T(8,128)(2,1)S(1)}, u32[]{:S(2)}, u32[]{:S(2)}) collective-permute-start(bf16[64,128]{1,0:T(8,128)(2,1)S(1)} %get-tuple-element.16), channel_id=1, source_target_pairs={{0,2},{1,3},{2,0},{3,1},{4,6},{5,7},{6,4},{7,5},{8,10},{9,11},{10,... | collective-permute-start | bytes 49160 | tf_op jit(solution)/shard_map/ppermute | solution.py:30
  18.0 5.0 %collective-permute-start.2 = (bf16[64,128]{1,0:T(8,128)(2,1)S(1)}, bf16[64,128]{1,0:T(8,128)(2,1)S(1)}, u32[]{:S(2)}, u32[]{:S(2)}) collective-permute-start(bf16[64,128]{1,0:T(8,128)(2,1)S(1)} %get-tuple-element.17), channel_id=1, source_target_pairs={{0,3},{1,0},{2,1},{3,2},{4,7},{5,4},{6,5},{7,6},{8,11},{9,8},{10,9... | collective-permute-start | bytes 49160 | tf_op jit(solution)/shard_map/ppermute | solution.py:30
  19.1 4.1 %copy-start = (bf16[128,8192]{1,0:T(8,128)(2,1)S(1)}, bf16[128,8192]{1,0:T(8,128)(2,1)}, u32[]{:S(2)}) copy-start(bf16[128,8192]{1,0:T(8,128)(2,1)} %acts.7) | copy-start | bytes 6291460
  23.5 3.1 %collective-permute-start.3 = (bf16[32,64,128]{2,1,0:T(8,128)(2,1)S(1)}, bf16[32,64,128]{2,1,0:T(8,128)(2,1)S(1)}, u32[]{:S(2)}, u32[]{:S(2)}) collective-permute-start(bf16[32,64,128]{2,1,0:T(8,128)(2,1)S(1)} %left.3), channel_id=1, source_target_pairs={{0,4},{4,0},{1,5},{5,1},{2,6},{6,2},{3,7},{7,3},{8,12},{12,8},{9,1... | collective-permute-start | bytes 1572872 | tf_op jit(solution)/shard_map/ppermute | solution.py:30
  71.9 5.1 %collective-permute-start.4 = (bf16[32,64,128]{2,1,0:T(8,128)(2,1)S(1)}, bf16[32,64,128]{2,1,0:T(8,128)(2,1)S(1)}, u32[]{:S(2)}, u32[]{:S(2)}) collective-permute-start(bf16[32,64,128]{2,1,0:T(8,128)(2,1)S(1)} %all_to_all.22.p.own), channel_id=1, source_target_pairs={{0,4},{4,0},{1,5},{5,1},{2,6},{6,2},{3,7},{7,3},{8,12},{12,8},{9,1... | collective-permute-start | bytes 1572872 | tf_op jit(solution)/shard_map/ppermute | solution.py:30
  77.4 4.7 %collective-permute-start.5 = (bf16[64,128]{1,0:T(8,128)(2,1)S(1)}, bf16[64,128]{1,0:T(8,128)(2,1)S(1)}, u32[]{:S(2)}, u32[]{:S(2)}) collective-permute-start(bf16[64,128]{1,0:T(8,128)(2,1)S(1)} %add_convert_fusion.2.a0), channel_id=1, source_target_pairs={{0,1},{1,2},{2,3},{3,0},{4,5},{5,6},{6,7},{7,4},{8,9},{9,10},{10,1... | collective-permute-start | bytes 49160 | tf_op jit(solution)/shard_map/ppermute | solution.py:30
  78.2 4.5 %collective-permute-start.6 = (bf16[64,128]{1,0:T(8,128)(2,1)S(1)}, bf16[64,128]{1,0:T(8,128)(2,1)S(1)}, u32[]{:S(2)}, u32[]{:S(2)}) collective-permute-start(bf16[64,128]{1,0:T(8,128)(2,1)S(1)} %add_convert_fusion.2.a0), channel_id=1, source_target_pairs={{0,2},{1,3},{2,0},{3,1},{4,6},{5,7},{6,4},{7,5},{8,10},{9,11},{10,... | collective-permute-start | bytes 49160 | tf_op jit(solution)/shard_map/ppermute | solution.py:30
  79.4 3.8 %collective-permute-start.7 = (bf16[64,128]{1,0:T(8,128)(2,1)S(1)}, bf16[64,128]{1,0:T(8,128)(2,1)S(1)}, u32[]{:S(2)}, u32[]{:S(2)}) collective-permute-start(bf16[64,128]{1,0:T(8,128)(2,1)S(1)} %add_convert_fusion.2.a0), channel_id=1, source_target_pairs={{0,3},{1,0},{2,1},{3,2},{4,7},{5,4},{6,5},{7,6},{8,11},{9,8},{10,9... | collective-permute-start | bytes 49160 | tf_op jit(solution)/shard_map/ppermute | solution.py:30
  81.2 2.0 %copy-start.1 = (bf16[512,256]{1,0:T(8,128)(2,1)S(1)}, bf16[512,256]{1,0:T(8,128)(2,1)}, u32[]{:S(2)}) copy-start(bf16[512,256]{1,0:T(8,128)(2,1)} %kg.3) | copy-start | bytes 786436
  83.3 2.4 %collective-permute-start.8 = (f32[64,256]{1,0:T(8,128)S(1)}, f32[64,256]{1,0:T(8,128)S(1)}, u32[]{:S(2)}, u32[]{:S(2)}) collective-permute-start(f32[64,256]{1,0:T(8,128)S(1)} %right.1), channel_id=1, source_target_pairs={{0,4},{4,0},{1,5},{5,1},{2,6},{6,2},{3,7},{7,3},{8,12},{12,8},{9,1... | collective-permute-start | bytes 196616 | tf_op jit(solution)/shard_map/ppermute | solution.py:30
  85.7 4.5 %collective-permute-start.9 = (bf16[64,256]{1,0:T(8,128)(2,1)S(1)}, bf16[64,256]{1,0:T(8,128)(2,1)S(1)}, u32[]{:S(2)}, u32[]{:S(2)}) collective-permute-start(bf16[64,256]{1,0:T(8,128)(2,1)S(1)} %add_convert_fusion.1.a), channel_id=1, source_target_pairs={{0,8},{8,16},{16,24},{24,0},{1,9},{9,17},{17,25},{25,1},{2,10},{10... | collective-permute-start | bytes 98312 | tf_op jit(solution)/shard_map/ppermute | solution.py:30
  86.0 4.5 %collective-permute-start.10 = (bf16[64,256]{1,0:T(8,128)(2,1)S(1)}, bf16[64,256]{1,0:T(8,128)(2,1)S(1)}, u32[]{:S(2)}, u32[]{:S(2)}) collective-permute-start(bf16[64,256]{1,0:T(8,128)(2,1)S(1)} %add_convert_fusion.1.a), channel_id=1, source_target_pairs={{0,16},{8,24},{16,0},{24,8},{1,17},{9,25},{17,1},{25,9},{2,18},{10... | collective-permute-start | bytes 98312 | tf_op jit(solution)/shard_map/ppermute | solution.py:30
  88.9 3.3 %collective-permute-start.11 = (bf16[64,256]{1,0:T(8,128)(2,1)S(1)}, bf16[64,256]{1,0:T(8,128)(2,1)S(1)}, u32[]{:S(2)}, u32[]{:S(2)}) collective-permute-start(bf16[64,256]{1,0:T(8,128)(2,1)S(1)} %add_convert_fusion.1.a), channel_id=1, source_target_pairs={{0,24},{8,0},{16,8},{24,16},{1,25},{9,1},{17,9},{25,17},{2,26},{10... | collective-permute-start | bytes 98312 | tf_op jit(solution)/shard_map/ppermute | solution.py:30
  92.9 13.5 %all-to-all-start.3 = ((bf16[8,64,256]{2,1,0:T(8,128)(2,1)}), bf16[8,64,256]{2,1,0:T(8,128)(2,1)S(1)}, u32[]{:S(2)}, u32[]{:S(2)}) async-start(bf16[8,64,256]{2,1,0:T(8,128)(2,1)} %pairs.1), calls=%async_computation.4 | async-start | bytes 524288 | tf_op jit(solution)/shard_map/all_to_all | solution.py:282
  106.7 5.5 %copy-start.2 = (f32[64,256]{1,0:T(8,128)}, f32[64,256]{1,0:T(8,128)S(1)}, u32[]{:S(2)}) copy-start(f32[64,256]{1,0:T(8,128)S(1)} %fusion) | copy-start | bytes 196612
Sparse Core Ops, SparseCore 0:
  13.3 98.8 reduce-scatter.1

commit v6 on v5

--- a/solution.py
+++ b/solution.py
@@ -43,6 +43,10 @@
     )
 
 
+def fold(v):
+    return v[:RANK] + v[RANK:]
+
+
 def shape(s, dtype):
     return jax.ShapeDtypeStruct(s, dtype)
 
@@ -79,11 +83,13 @@
         held[:, cols] = dot(kg_in[...], w_in[cols, :], 1, 1).astype(BF)
         store(i).start()
     q_copy.wait()
-    qt = q_in[...].astype(BF)
+    high = q_in[...].astype(BF)
+    low = (q_in[...] - high.astype(F32)).astype(BF)
+    qt = jnp.concatenate([high, low], axis=0)
     q_t[...] = qt
     for k, block in enumerate((own, s1, s2, s3)):
         start = pl.multiple_of(lax.rem(y[0] + k, N_Y) * ROWS, ROWS)
-        block[...] = dot(qt, kg_in[pl.ds(start, ROWS), :], 1, 1).astype(block.dtype)
+        block[...] = fold(dot(qt, kg_in[pl.ds(start, ROWS), :], 1, 1)).astype(block.dtype)
     for i in range(PARTS):
         store(i).wait()
 
@@ -94,7 +100,7 @@
     block = (RANK, ROWS)
     return kernel(
         partial_body, "partial", [IN_SMEM] + [IN_HBM] * 3, [IN_HBM] + [IN_VMEM] * 5,
-        [pltpu.HBM((n, D), BF), pltpu.VMEM((RANK, COLS), BF), pltpu.VMEM(block, F32)]
+        [pltpu.HBM((n, D), BF), pltpu.VMEM((2 * RANK, COLS), BF), pltpu.VMEM(block, F32)]
         + [pltpu.VMEM(block, BF)] * 3,
         2 * n * COLS * D, 2 * D * (COLS + n),
         [
@@ -117,7 +123,7 @@
         span = slice(i * SPAN, (i + 1) * SPAN)
         e = held[span, :].astype(BF)
         eb[span, :] = e
-        p = dot(q[...], e, 1, 1)
+        p = fold(dot(q[...], e, 1, 1))
         for j in range(STEP):
             pe[i * STEP + j] = p[:, j * LANES:(j + 1) * LANES]
 

time: 119 us -> 119 us (level)
  transfers between devices with their start and end apart: 14 -> 14, of which waited for: 10 -> 10; matrix products, arithmetic and copies ran while one was open for 1% -> 1% of each run, Pallas kernels for 13% -> 14%
where the time goes in v6:
time: 119 us
  blocking collectives  45 us (38%)
  starting transfers between devices  23.5 us (20%)
  Pallas kernels  22.1 us (19%)
  between operations  14.2 us (12%)
  waiting for transfers between devices  13.6 us (11%)
    all_to_all x3, blocking collectives, exchange(): return lax.all_to_all(v, axes, 0, 0, tiled=True)  45 us
    ppermute x12, starting transfers between devices, shift(): return lax.ppermute(v, axis, [(i, (i + k) % n) for i in range(n)])  20 us
    ppermute x12, waiting for transfers between devices, shift(): return lax.ppermute(v, axis, [(i, (i + k) % n) for i in range(n)])  6.85 us
    pallas_call x1, Pallas kernels, inverse(): kernel(inverse_body, 'inverse', [IN_VMEM, IN_VMEM], IN_VMEM, shape((RANK,...  6.05 us
    pallas_call x1, Pallas kernels, partial_grad(): kernel(partial_body, 'partial', [IN_SMEM] + [IN_HBM] * 3, [IN_HBM] + [IN_...  5.94 us
    all_to_all x1, waiting for transfers between devices, exchange(): return lax.all_to_all(v, axes, 0, 0, tiled=True)  4.05 us
    pallas_call x1, Pallas kernels, error_side(): kernel(error_body, 'error', [IN_VMEM, IN_HBM], [IN_VMEM, IN_VMEM], [pltpu...  4.01 us
    all_to_all x1, starting transfers between devices, exchange(): return lax.all_to_all(v, axes, 0, 0, tiled=True)  3.41 us
  transfers between devices with their start and end apart: 14, of which 10 were waited for; matrix products, arithmetic and copies ran while one was open for 1% of the time, Pallas kernels for 14%

profile of v6, /device:TPU:1, one launch (start us, length us, event | category | flops | bytes accessed | tf_op | source)
XLA Modules:
  0.0 119.1 jit_solution(11123842968765098089)
XLA Ops:
  7.2 0.0 reduce-scatter.2.cloned.1.call-start
  7.2 5.9 %partial.1 = (bf16[512,8192]{1,0:T(8,128)(2,1)}, bf16[128,256]{1,0:T(8,128)(2,1)S(1)}, f32[64,128]{1,0:T(8,128)S(1)}, bf16[64,128]{1,0:T(8,128)(2,1)S(1)}, bf16[...) custom-call(s32[1]{0:T(128)} %bitcast.y, f32[64,256]{1,0:T(8,128)} %bitcast.9, bf16[512,256]{1,0:T(8,128)(2,1)} %kg.3, ...), custom_call_target="tpu_custom_call" | custom-call | flops 2147483648 | bytes 12582912 | tf_op jit(solution)/shard_map/partial/pallas_call | solution.py:101
  13.2 0.0 reduce-scatter.2.cloned.1.call-update
  13.2 2.2 %collective-permute-start = (bf16[64,128]{1,0:T(8,128)(2,1)S(1)}, bf16[64,128]{1,0:T(8,128)(2,1)S(1)}, u32[]{:S(2)}, u32[]{:S(2)}) collective-permute-start(bf16[64,128]{1,0:T(8,128)(2,1)S(1)} %get-tuple-element.15), channel_id=1, source_target_pairs={{0,1},{1,2},{2,3},{3,0},{4,5},{5,6},{6,7},{7,4},{8,9},{9,10},{10,1... | collective-permute-start | bytes 49160 | tf_op jit(solution)/shard_map/ppermute | solution.py:30
  15.4 2.6 %collective-permute-start.1 = (bf16[64,128]{1,0:T(8,128)(2,1)S(1)}, bf16[64,128]{1,0:T(8,128)(2,1)S(1)}, u32[]{:S(2)}, u32[]{:S(2)}) collective-permute-start(bf16[64,128]{1,0:T(8,128)(2,1)S(1)} %get-tuple-element.16), channel_id=1, source_target_pairs={{0,2},{1,3},{2,0},{3,1},{4,6},{5,7},{6,4},{7,5},{8,10},{9,11},{10,... | collective-permute-start | bytes 49160 | tf_op jit(solution)/shard_map/ppermute | solution.py:30
  18.0 1.1 collective-permute-start.2
  19.1 0.0 copy-start
  19.1 4.0 %error.1 = (f32[64,64,128]{2,1,0:T(8,128)S(1)}, bf16[8192,256]{1,0:T(8,128)(2,1)S(1)}) custom-call(bf16[128,256]{1,0:T(8,128)(2,1)S(1)} %get-tuple-element.18.q, f32[8192,256]{1,0:T(8,128)} %err.1), custom_call_target="tpu_custom_call" | custom-call | flops 268435456 | bytes 14680064 | tf_op jit(solution)/shard_map/error/pallas_call | solution.py:132
  23.1 0.0 collective-permute-done.k1
  23.1 0.0 collective-permute-done.1.k2
  23.1 0.0 collective-permute-done.2.k3
  23.1 0.0 copy-done
  23.1 0.3 left.3
  23.5 1.6 %collective-permute-start.3 = (bf16[32,64,128]{2,1,0:T(8,128)(2,1)S(1)}, bf16[32,64,128]{2,1,0:T(8,128)(2,1)S(1)}, u32[]{:S(2)}, u32[]{:S(2)}) collective-permute-start(bf16[32,64,128]{2,1,0:T(8,128)(2,1)S(1)} %left.3), channel_id=1, source_target_pairs={{0,4},{4,0},{1,5},{5,1},{2,6},{6,2},{3,7},{7,3},{8,12},{12,8},{9,1... | collective-permute-start | bytes 1572872 | tf_op jit(solution)/shard_map/ppermute | solution.py:30
  25.1 0.3 left.2
  25.4 1.2 %collective-permute-done.3 = bf16[32,64,128]{2,1,0:T(8,128)(2,1)S(1)} collective-permute-done((bf16[32,64,128]{2,1,0:T(8,128)(2,1)S(1)}, bf16[32,64,128]{2,1,0:T(8,128)(2,1)S(1)}, u32[]{:S(2)}, u32[]{:S(2)}) %collective-permute-start.3) | collective-permute-done | bytes 524320 | tf_op jit(solution)/shard_map/ppermute | solution.py:30
  26.6 0.1 add_convert_fusion
  26.7 16.0 %all_to_all.20.v = bf16[32,64,128]{2,1,0:T(8,128)(2,1)S(1)} all-to-all(bf16[32,64,128]{2,1,0:T(8,128)(2,1)S(1)} %add_convert_fusion), channel_id=1, replica_groups=mesh['zq'=4,'zp'=2,'x'=4,'c'=2,'y'=4] {'x','zp','y'}, dimensions={0} | all-to-all | bytes 1048576 | tf_op jit(solution)/shard_map/all_to_all | solution.py:288
  42.8 0.1 merge.2
  42.9 14.1 %all_to_all.21.v = bf16[4,64,128]{2,1,0:T(8,128)(2,1)S(1)} all-to-all(bf16[4,64,128]{2,1,0:T(8,128)(2,1)S(1)} %merge.2), channel_id=1, replica_groups=mesh['zq'=4,'zp'=2,'x'=4,'c'=2,'y'=4] {'zq'}, dimensions={0} | all-to-all | bytes 131072 | tf_op jit(solution)/shard_map/all_to_all | solution.py:288
  57.0 0.1 merge.3
  57.1 14.8 %all_to_all.22.p.own = bf16[32,64,128]{2,1,0:T(8,128)(2,1)S(1)} all-to-all(bf16[32,64,128]{2,1,0:T(8,128)(2,1)S(1)} %merge.3), channel_id=1, replica_groups=mesh['zq'=4,'zp'=2,'x'=4,'c'=2,'y'=4] {'x','zp','y'}, dimensions={0} | all-to-all | bytes 1048576 | tf_op jit(solution)/shard_map/all_to_all | solution.py:288
  71.9 3.5 %collective-permute-start.4 = (bf16[32,64,128]{2,1,0:T(8,128)(2,1)S(1)}, bf16[32,64,128]{2,1,0:T(8,128)(2,1)S(1)}, u32[]{:S(2)}, u32[]{:S(2)}) collective-permute-start(bf16[32,64,128]{2,1,0:T(8,128)(2,1)S(1)} %all_to_all.22.p.own), channel_id=1, source_target_pairs={{0,4},{4,0},{1,5},{5,1},{2,6},{6,2},{3,7},{7,3},{8,12},{12,8},{9,1... | collective-permute-start | bytes 1572872 | tf_op jit(solution)/shard_map/ppermute | solution.py:30
  75.4 0.5 acts_p.2
  75.9 1.1 collective-permute-done.4.p.other
  76.9 0.5 acts_p.3
  77.4 0.7 collective-permute-start.5
  78.2 1.2 collective-permute-start.6
  79.4 1.8 %collective-permute-start.7 = (bf16[64,128]{1,0:T(8,128)(2,1)S(1)}, bf16[64,128]{1,0:T(8,128)(2,1)S(1)}, u32[]{:S(2)}, u32[]{:S(2)}) collective-permute-start(bf16[64,128]{1,0:T(8,128)(2,1)S(1)} %add_convert_fusion.2.a0), channel_id=1, source_target_pairs={{0,3},{1,0},{2,1},{3,2},{4,7},{5,4},{6,5},{7,6},{8,11},{9,8},{10,9... | collective-permute-start | bytes 49160 | tf_op jit(solution)/shard_map/ppermute | solution.py:30
  81.2 0.0 copy-start.1
  81.2 0.5 err_p.2.qa
  81.6 0.5 err_p.3.qb
  82.1 0.0 collective-permute-done.5.a1
  82.1 0.5 collective-permute-done.6.a2
  82.7 0.5 collective-permute-done.7.a3
  83.2 0.0 copy-done.1
  83.2 0.2 right.1
  83.3 1.5 %collective-permute-start.8 = (f32[64,256]{1,0:T(8,128)S(1)}, f32[64,256]{1,0:T(8,128)S(1)}, u32[]{:S(2)}, u32[]{:S(2)}) collective-permute-start(f32[64,256]{1,0:T(8,128)S(1)} %right.1), channel_id=1, source_target_pairs={{0,4},{4,0},{1,5},{5,1},{2,6},{6,2},{3,7},{7,3},{8,12},{12,8},{9,1... | collective-permute-start | bytes 196616 | tf_op jit(solution)/shard_map/ppermute | solution.py:30
  84.8 0.9 collective-permute-done.8
  85.7 0.3 collective-permute-start.9
  86.0 2.8 %collective-permute-start.10 = (bf16[64,256]{1,0:T(8,128)(2,1)S(1)}, bf16[64,256]{1,0:T(8,128)(2,1)S(1)}, u32[]{:S(2)}, u32[]{:S(2)}) collective-permute-start(bf16[64,256]{1,0:T(8,128)(2,1)S(1)} %add_convert_fusion.1.a), channel_id=1, source_target_pairs={{0,16},{8,24},{16,0},{24,8},{1,17},{9,25},{17,1},{25,9},{2,18},{10... | collective-permute-start | bytes 98312 | tf_op jit(solution)/shard_map/ppermute | solution.py:30
  88.9 0.7 collective-permute-start.11
  89.6 0.6 collective-permute-done.9.b
  90.2 0.4 collective-permute-done.10.c
  90.5 1.7 %collective-permute-done.11.d = bf16[64,256]{1,0:T(8,128)(2,1)S(1)} collective-permute-done((bf16[64,256]{1,0:T(8,128)(2,1)S(1)}, bf16[64,256]{1,0:T(8,128)(2,1)S(1)}, u32[]{:S(2)}, u32[]{:S(2)}) %collective-permute-start.11) | collective-permute-done | bytes 32800 | tf_op jit(solution)/shard_map/ppermute | solution.py:30
  92.2 0.7 pairs.1
  92.9 3.4 %all-to-all-start.3 = ((bf16[8,64,256]{2,1,0:T(8,128)(2,1)}), bf16[8,64,256]{2,1,0:T(8,128)(2,1)S(1)}, u32[]{:S(2)}, u32[]{:S(2)}) async-start(bf16[8,64,256]{2,1,0:T(8,128)(2,1)} %pairs.1), calls=%async_computation.4 | async-start | bytes 524288 | tf_op jit(solution)/shard_map/all_to_all | solution.py:288
  96.4 6.0 %inverse.1 = f32[64,64]{1,0:T(8,128)S(1)} custom-call(bf16[32,64,128]{2,1,0:T(8,128)(2,1)S(1)} %all_to_all.22.p.own, bf16[32,64,128]{2,1,0:T(8,128)(2,1)S(1)} %collective-permute-done.4.p.other), custom_call_target="tpu_custom_call" | custom-call | flops 67108864 | bytes 2097152 | tf_op jit(solution)/shard_map/inverse/pallas_call | solution.py:224
  102.4 4.1 %all-to-all-done.3 = bf16[8,64,256]{2,1,0:T(8,128)(2,1)S(1)} async-done(((bf16[8,64,256]{2,1,0:T(8,128)(2,1)}), bf16[8,64,256]{2,1,0:T(8,128)(2,1)S(1)}, u32[]{:S(2)}, u32[]{:S(2)}) %all-to-all-start.3) | async-done | bytes 262176 | tf_op jit(solution)/shard_map/all_to_all | solution.py:288
  106.5 0.2 fusion
  106.7 0.0 copy-start.2
  106.7 0.3 subtract_convert_fusion
  107.0 2.5 %update.1 = bf16[8192,256]{1,0:T(8,128)(2,1)} custom-call(s32[1]{0:T(128)} %bitcast.2.h.c, bf16[32,64,128]{2,1,0:T(8,128)(2,1)S(1)} %all_to_all.22.p.own, bf16[32,64,128]{2,1,0:T(8,128)(2,1)S(1)} %collective-permute-done.4.p.other, bf16[128,256]{1,0:T(8,128)(2,1)S(1)} %pad_maximum_fusion.mix), custom_call_target="tpu_custom_call" | custom-call | flops 536870912 | bytes 5242880 | tf_op jit(solution)/shard_map/update/pallas_call | solution.py:247
  109.5 2.7 %reduce-scatter.2.cloned.1.call-done = bf16[128,8192]{1,0:T(8,128)(2,1)} async-done(((bf16[512,8192]{1,0:T(8,128)(2,1)}), bf16[128,8192]{1,0:T(8,128)(2,1)}) %reduce-scatter.2.cloned.1.call-update) | async-done | bytes 2097168 | tf_op jit(solution)/shard_map/reduce_scatter | solution.py:302
  112.2 0.0 copy-done.2
  (4 shorter events, 0.1 us)
Async XLA Ops:
  7.2 105.1 %reduce-scatter.2.cloned.1.call-start = ((), (), s32[]{:S(2)}) async-start(), calls=%async_computation.5 | async-start | bytes 10485760 | tf_op jit(solution)/shard_map/reduce_scatter | solution.py:302
  13.2 9.9 %collective-permute-start = (bf16[64,128]{1,0:T(8,128)(2,1)S(1)}, bf16[64,128]{1,0:T(8,128)(2,1)S(1)}, u32[]{:S(2)}, u32[]{:S(2)}) collective-permute-start(bf16[64,128]{1,0:T(8,128)(2,1)S(1)} %get-tuple-element.15), channel_id=1, source_target_pairs={{0,1},{1,2},{2,3},{3,0},{4,5},{5,6},{6,7},{7,4},{8,9},{9,10},{10,1... | collective-permute-start | bytes 49160 | tf_op jit(solution)/shard_map/ppermute | solution.py:30
  15.4 7.7 %collective-permute-start.1 = (bf16[64,128]{1,0:T(8,128)(2,1)S(1)}, bf16[64,128]{1,0:T(8,128)(2,1)S(1)}, u32[]{:S(2)}, u32[]{:S(2)}) collective-permute-start(bf16[64,128]{1,0:T(8,128)(2,1)S(1)} %get-tuple-element.16), channel_id=1, source_target_pairs={{0,2},{1,3},{2,0},{3,1},{4,6},{5,7},{6,4},{7,5},{8,10},{9,11},{10,... | collective-permute-start | bytes 49160 | tf_op jit(solution)/shard_map/ppermute | solution.py:30
  18.0 5.1 %collective-permute-start.2 = (bf16[64,128]{1,0:T(8,128)(2,1)S(1)}, bf16[64,128]{1,0:T(8,128)(2,1)S(1)}, u32[]{:S(2)}, u32[]{:S(2)}) collective-permute-start(bf16[64,128]{1,0:T(8,128)(2,1)S(1)} %get-tuple-element.17), channel_id=1, source_target_pairs={{0,3},{1,0},{2,1},{3,2},{4,7},{5,4},{6,5},{7,6},{8,11},{9,8},{10,9... | collective-permute-start | bytes 49160 | tf_op jit(solution)/shard_map/ppermute | solution.py:30
  19.1 4.1 %copy-start = (bf16[128,8192]{1,0:T(8,128)(2,1)S(1)}, bf16[128,8192]{1,0:T(8,128)(2,1)}, u32[]{:S(2)}) copy-start(bf16[128,8192]{1,0:T(8,128)(2,1)} %acts.7) | copy-start | bytes 6291460
  23.5 3.1 %collective-permute-start.3 = (bf16[32,64,128]{2,1,0:T(8,128)(2,1)S(1)}, bf16[32,64,128]{2,1,0:T(8,128)(2,1)S(1)}, u32[]{:S(2)}, u32[]{:S(2)}) collective-permute-start(bf16[32,64,128]{2,1,0:T(8,128)(2,1)S(1)} %left.3), channel_id=1, source_target_pairs={{0,4},{4,0},{1,5},{5,1},{2,6},{6,2},{3,7},{7,3},{8,12},{12,8},{9,1... | collective-permute-start | bytes 1572872 | tf_op jit(solution)/shard_map/ppermute | solution.py:30
  71.9 5.1 %collective-permute-start.4 = (bf16[32,64,128]{2,1,0:T(8,128)(2,1)S(1)}, bf16[32,64,128]{2,1,0:T(8,128)(2,1)S(1)}, u32[]{:S(2)}, u32[]{:S(2)}) collective-permute-start(bf16[32,64,128]{2,1,0:T(8,128)(2,1)S(1)} %all_to_all.22.p.own), channel_id=1, source_target_pairs={{0,4},{4,0},{1,5},{5,1},{2,6},{6,2},{3,7},{7,3},{8,12},{12,8},{9,1... | collective-permute-start | bytes 1572872 | tf_op jit(solution)/shard_map/ppermute | solution.py:30
  77.4 4.7 %collective-permute-start.5 = (bf16[64,128]{1,0:T(8,128)(2,1)S(1)}, bf16[64,128]{1,0:T(8,128)(2,1)S(1)}, u32[]{:S(2)}, u32[]{:S(2)}) collective-permute-start(bf16[64,128]{1,0:T(8,128)(2,1)S(1)} %add_convert_fusion.2.a0), channel_id=1, source_target_pairs={{0,1},{1,2},{2,3},{3,0},{4,5},{5,6},{6,7},{7,4},{8,9},{9,10},{10,1... | collective-permute-start | bytes 49160 | tf_op jit(solution)/shard_map/ppermute | solution.py:30
  78.2 4.5 %collective-permute-start.6 = (bf16[64,128]{1,0:T(8,128)(2,1)S(1)}, bf16[64,128]{1,0:T(8,128)(2,1)S(1)}, u32[]{:S(2)}, u32[]{:S(2)}) collective-permute-start(bf16[64,128]{1,0:T(8,128)(2,1)S(1)} %add_convert_fusion.2.a0), channel_id=1, source_target_pairs={{0,2},{1,3},{2,0},{3,1},{4,6},{5,7},{6,4},{7,5},{8,10},{9,11},{10,... | collective-permute-start | bytes 49160 | tf_op jit(solution)/shard_map/ppermute | solution.py:30
  79.4 3.8 %collective-permute-start.7 = (bf16[64,128]{1,0:T(8,128)(2,1)S(1)}, bf16[64,128]{1,0:T(8,128)(2,1)S(1)}, u32[]{:S(2)}, u32[]{:S(2)}) collective-permute-start(bf16[64,128]{1,0:T(8,128)(2,1)S(1)} %add_convert_fusion.2.a0), channel_id=1, source_target_pairs={{0,3},{1,0},{2,1},{3,2},{4,7},{5,4},{6,5},{7,6},{8,11},{9,8},{10,9... | collective-permute-start | bytes 49160 | tf_op jit(solution)/shard_map/ppermute | solution.py:30
  81.2 2.0 %copy-start.1 = (bf16[512,256]{1,0:T(8,128)(2,1)S(1)}, bf16[512,256]{1,0:T(8,128)(2,1)}, u32[]{:S(2)}) copy-start(bf16[512,256]{1,0:T(8,128)(2,1)} %kg.3) | copy-start | bytes 786436
  83.3 2.4 %collective-permute-start.8 = (f32[64,256]{1,0:T(8,128)S(1)}, f32[64,256]{1,0:T(8,128)S(1)}, u32[]{:S(2)}, u32[]{:S(2)}) collective-permute-start(f32[64,256]{1,0:T(8,128)S(1)} %right.1), channel_id=1, source_target_pairs={{0,4},{4,0},{1,5},{5,1},{2,6},{6,2},{3,7},{7,3},{8,12},{12,8},{9,1... | collective-permute-start | bytes 196616 | tf_op jit(solution)/shard_map/ppermute | solution.py:30
  85.7 4.5 %collective-permute-start.9 = (bf16[64,256]{1,0:T(8,128)(2,1)S(1)}, bf16[64,256]{1,0:T(8,128)(2,1)S(1)}, u32[]{:S(2)}, u32[]{:S(2)}) collective-permute-start(bf16[64,256]{1,0:T(8,128)(2,1)S(1)} %add_convert_fusion.1.a), channel_id=1, source_target_pairs={{0,8},{8,16},{16,24},{24,0},{1,9},{9,17},{17,25},{25,1},{2,10},{10... | collective-permute-start | bytes 98312 | tf_op jit(solution)/shard_map/ppermute | solution.py:30
  86.0 4.5 %collective-permute-start.10 = (bf16[64,256]{1,0:T(8,128)(2,1)S(1)}, bf16[64,256]{1,0:T(8,128)(2,1)S(1)}, u32[]{:S(2)}, u32[]{:S(2)}) collective-permute-start(bf16[64,256]{1,0:T(8,128)(2,1)S(1)} %add_convert_fusion.1.a), channel_id=1, source_target_pairs={{0,16},{8,24},{16,0},{24,8},{1,17},{9,25},{17,1},{25,9},{2,18},{10... | collective-permute-start | bytes 98312 | tf_op jit(solution)/shard_map/ppermute | solution.py:30
  88.9 3.3 %collective-permute-start.11 = (bf16[64,256]{1,0:T(8,128)(2,1)S(1)}, bf16[64,256]{1,0:T(8,128)(2,1)S(1)}, u32[]{:S(2)}, u32[]{:S(2)}) collective-permute-start(bf16[64,256]{1,0:T(8,128)(2,1)S(1)} %add_convert_fusion.1.a), channel_id=1, source_target_pairs={{0,24},{8,0},{16,8},{24,16},{1,25},{9,1},{17,9},{25,17},{2,26},{10... | collective-permute-start | bytes 98312 | tf_op jit(solution)/shard_map/ppermute | solution.py:30
  92.9 13.5 %all-to-all-start.3 = ((bf16[8,64,256]{2,1,0:T(8,128)(2,1)}), bf16[8,64,256]{2,1,0:T(8,128)(2,1)S(1)}, u32[]{:S(2)}, u32[]{:S(2)}) async-start(bf16[8,64,256]{2,1,0:T(8,128)(2,1)} %pairs.1), calls=%async_computation.4 | async-start | bytes 524288 | tf_op jit(solution)/shard_map/all_to_all | solution.py:288
  106.7 5.5 %copy-start.2 = (f32[64,256]{1,0:T(8,128)}, f32[64,256]{1,0:T(8,128)S(1)}, u32[]{:S(2)}) copy-start(f32[64,256]{1,0:T(8,128)S(1)} %fusion) | copy-start | bytes 196612
Sparse Core Ops, SparseCore 0:
  13.3 98.8 reduce-scatter.1
